TPU v7x, 128 devices: a whole 4x4x4 slice. The times are simulated.
128 devices in a mesh: wide: 16 (over z_lo, y, core), narrow: 8 (over z_hi, x).
Axes of the slice: x: 4, y: 4, z: 4 (z_hi: 2, z_lo: 2; z = z_hi * 2 + z_lo), core: 2. Of those that a mesh axis runs over, the one named last changes fastest.
Arguments:
- trajectory: bfloat16 [5, 72, 512, 2048], P(None, None, 'narrow', 'wide'), may hold values from -6 to 6
- innovation: float32 [5, 72, 128, 512], P(None, None, 'narrow', 'wide'), may hold values from -6 to 6
- background: float32 [5, 72, 128, 512], P(None, None, 'narrow', 'wide'), may hold values from -6 to 6
- obs_weight: float32 [72, 128, 512], P(None, 'narrow', 'wide'), may hold values from 0.3 to 3
Outputs:
- analysis: bfloat16 [5, 72, 512, 2048], P(None, None, 'narrow', 'wide')
All inputs are finite; a program needn't handle non-finite values.
Results may differ from a plain program's by a relative error of at most 0.001.
Values sent between devices are 32-bit elements; how exact they have to be, the bound alone decides.
No kernel may reach another device: no remote copies, remote signals or barrier semaphores. Data moves between devices by JAX's collectives and lax.ppermute only.
A program may use at most 128 MiB of HBM per device.

v0:
```python
import jax
import jax.numpy as jnp
from jax import lax
from jax.sharding import PartitionSpec as P

FIELDS = 5
LEVELS = 72
COARSEN = 4
STEPS = 2


diffusion = 0.2
advection_scale = 0.3
descent_step = 1.0


def shifted(block, axis, distance):
    devices = range(lax.axis_size(axis))
    route = [((i - distance) % len(devices), i) for i in devices]
    return lax.ppermute(block, axis, route)


def from_behind(value, axis, steps):
    count = lax.axis_size(axis)
    first, last = (max(0, -steps), min(count, count - steps))
    return lax.ppermute(value, axis, [(source, source + steps) for source in range(first, last)])


def filter_rows(row_index, total_rows, cycle_size):
    wavenumber = jnp.arange(cycle_size, dtype=jnp.int32)
    folded = jnp.minimum(wavenumber, cycle_size - wavenumber).astype(jnp.float32)
    latitude = jnp.pi * ((row_index.astype(jnp.float32) + 0.5) / total_rows - 0.5)
    cutoff = 0.5 * cycle_size * jnp.cos(latitude)
    scaled_wave = folded[None, :] / cutoff[:, None]
    response = 1.0 / (1.0 + scaled_wave**4)
    phase_index = wavenumber[:, None] * wavenumber[None, :] % cycle_size
    angles = 2.0 * jnp.pi / cycle_size * phase_index.astype(jnp.float32)
    basis = jnp.concatenate([jnp.cos(angles), jnp.sin(angles)], axis=0)
    doubled = jnp.concatenate([response, response], axis=1)
    weighted = doubled[:, :, None] * basis[None]
    return jnp.einsum("rka,kb->rab", weighted, basis, precision=lax.Precision.HIGHEST) / cycle_size


def tangent_step(model_state, extend_rows, drift_coef, kernel):
    padded = extend_rows(model_state)
    north_row = padded[:, :, :-2]
    south_row = padded[:, :, 2:]
    east_cell = jnp.roll(model_state, -1, axis=3)
    west_cell = jnp.roll(model_state, 1, axis=3)
    updated = (
        model_state
        + diffusion * (north_row + south_row + east_cell + west_cell - 4.0 * model_state)
        + drift_coef * (east_cell - west_cell)
    )
    return jnp.einsum("flrb,rbc->flrc", updated, kernel, precision=lax.Precision.HIGHEST)


def adjoint_step(costate, extend_rows, drift_coef, kernel):
    filtered = jnp.einsum("flrb,rbc->flrc", costate, kernel, precision=lax.Precision.HIGHEST)
    padded = extend_rows(filtered)
    north_row = padded[:, :, :-2]
    south_row = padded[:, :, 2:]
    east_cell = jnp.roll(filtered, -1, axis=3)
    west_cell = jnp.roll(filtered, 1, axis=3)
    carried = drift_coef * filtered
    return (
        filtered
        + diffusion * (north_row + south_row + east_cell + west_cell - 4.0 * filtered)
        + jnp.roll(carried, 1, axis=3)
        - jnp.roll(carried, -1, axis=3)
    )


def shards(trajectory, innovation, background, obs_weight):
    wide_count = lax.axis_size("wide")
    narrow_count = lax.axis_size("narrow")
    wide_index = lax.axis_index("wide")
    narrow_index = lax.axis_index("narrow")
    coarse_rows = innovation.shape[2]
    coarse_cols = innovation.shape[3]
    fine_cols = trajectory.shape[3]
    total_rows = coarse_rows * narrow_count
    cycle_size = coarse_cols * wide_count
    zonal_wind = (
        trajectory[0]
        .astype(jnp.float32)
        .reshape(LEVELS, coarse_rows, COARSEN, fine_cols)
        .sum(axis=2)
    )
    zonal_wind = zonal_wind.reshape(LEVELS, coarse_rows, coarse_cols, COARSEN).sum(axis=3) / (
        COARSEN * COARSEN
    )
    side_fields = jnp.stack([obs_weight, advection_scale * jnp.tanh(zonal_wind)])
    band_rows = coarse_rows // wide_count
    level_count = LEVELS

    def spread(layer_field):
        return layer_field.reshape(layer_field.shape[0], LEVELS, wide_count, band_rows, coarse_cols)

    depart_part, backing_part, side_part = (
        lax.all_to_all(spread(innovation), "wide", split_axis=2, concat_axis=4, tiled=True),
        lax.all_to_all(spread(background), "wide", split_axis=2, concat_axis=4, tiled=True),
        lax.all_to_all(spread(side_fields), "wide", split_axis=2, concat_axis=4, tiled=True),
    )
    first_row = narrow_index * coarse_rows + wide_index * band_rows

    def extend_rows(model_state):
        from_before = shifted(model_state, "wide", 1)
        from_corner = from_behind(from_before, "narrow", 1)
        above_row = jnp.where(wide_index == 0, from_corner, from_before)
        from_after = shifted(model_state, "wide", -1)
        from_beyond = from_behind(from_after, "narrow", -1)
        below_row = jnp.where(wide_index == wide_count - 1, from_beyond, from_after)
        return jnp.concatenate([above_row, model_state, below_row], axis=2)

    departure = depart_part.reshape(FIELDS, level_count, band_rows, cycle_size)
    backing = backing_part.reshape(FIELDS, level_count, band_rows, cycle_size)
    side_band = side_part.reshape(2, level_count, band_rows, cycle_size)
    weight_band = side_band[0][None]
    drift_coef = side_band[1][None]
    kernel = filter_rows(first_row + jnp.arange(band_rows, dtype=jnp.int32), total_rows, cycle_size)
    increment = backing
    model_state = increment
    for step_index in range(STEPS):
        model_state = tangent_step(model_state, extend_rows, drift_coef, kernel)
    costate = weight_band * (model_state - departure)
    for step_index in range(STEPS):
        costate = adjoint_step(costate, extend_rows, drift_coef, kernel)
    increment = increment - descent_step * (increment - backing + costate)
    moved_back = lax.all_to_all(
        increment.reshape(FIELDS, LEVELS, 1, band_rows, cycle_size),
        "wide",
        split_axis=4,
        concat_axis=2,
        tiled=True,
    )
    coarse_part = moved_back.reshape(FIELDS, LEVELS, coarse_rows, coarse_cols)
    fine_part = jnp.repeat(jnp.repeat(coarse_part, COARSEN, axis=3), COARSEN, axis=2)
    return (trajectory.astype(jnp.float32) + fine_part).astype(jnp.bfloat16)


def solution(mesh):
    in_specs = (
        P(None, None, "narrow", "wide"),
        P(None, None, "narrow", "wide"),
        P(None, None, "narrow", "wide"),
        P(None, "narrow", "wide"),
    )
    out_specs = P(None, None, "narrow", "wide")
    return jax.shard_map(shards, mesh=mesh, in_specs=in_specs, out_specs=out_specs, check_vma=False)
```

profile of v0, /device:TPU:64, one launch (start us, length us, event | category | flops | bytes accessed | tf_op | source)
XLA Modules:
  0.0 270.0 jit_solution(17127801614041965263)
XLA Ops:
  0.0 2.5 copy.80
  2.5 5.8 %all-to-all-start = ((f32[5,72,16,1,32]{1,4,0,3,2:T(8,128)}), f32[5,72,16,1,32]{1,4,0,3,2:T(8,128)S(1)}, u32[]{:S(2)}, u32[]{:S(2)}) async-start(f32[5,72,16,1,32]{1,4,0,3,2:T(8,128)} %bitcast.72), calls=%async_computation | async-start | bytes 2621440 | tf_op jit(solution)/shard_map/all_to_all | solution.py:102
  8.3 1.5 convert_reduce_fusion
  9.8 0.6 copy.56
  10.5 0.2 copy_bitcast_fusion.2
  10.7 16.9 %all-to-all-done = f32[5,72,16,1,32]{1,4,0,3,2:T(8,128)S(1)} async-done(((f32[5,72,16,1,32]{1,4,0,3,2:T(8,128)}), f32[5,72,16,1,32]{1,4,0,3,2:T(8,128)S(1)}, u32[]{:S(2)}, u32[]{:S(2)}) %all-to-all-start) | async-done | bytes 737312 | tf_op jit(solution)/shard_map/all_to_all | solution.py:102
  27.5 1.2 copy.52
  28.7 1.7 copy.71
  30.4 0.6 collective-permute-start.2
  31.1 0.9 copy.57
  32.0 5.2 %all-to-all-start.1 = ((f32[2,72,16,1,32]{1,4,0,3,2:T(8,128)}), f32[2,72,16,1,32]{1,4,0,3,2:T(8,128)S(1)}, u32[]{:S(2)}, u32[]{:S(2)}) async-start(f32[2,72,16,1,32]{1,4,0,3,2:T(8,128)} %copy.57), calls=%async_computation.1 | async-start | bytes 1048576 | tf_op jit(solution)/shard_map/all_to_all | solution.py:103
  37.4 5.3 %fusion.83 = (f32[512,512]{1,0:T(8,128)S(1)}, f32[512,512]{1,0:T(8,128)}) fusion(), kind=kLoop, calls=%fused_computation.93 | loop fusion | flops 3670016 | bytes 2097152 | tf_op jit(solution)/shard_map/sin | solution.py:38
  42.7 5.4 %fusion.10 = f32[512,512,1]{1,0,2:T(8,128)S(1)} fusion(f32[512,512]{1,0:T(8,128)S(1)} %get-tuple-element.37, f32[512,512]{1,0:T(8,128)} %get-tuple-element.38, f32[1024]{0:T(1024)S(1)} %bitcast.78), kind=kOutput, calls=%fused_computation.11 | convolution fusion | flops 3223060480 | bytes 3149824 | tf_op jit(solution)/shard_map/rka,kb->rab/dot_general | solution.py:41
  48.1 4.1 %collective-permute-start.3 = (f32[5,72,1,512]{3,1,0,2:T(8,128)}, f32[5,72,1,512]{3,1,0,2:T(8,128)}, u32[]{:S(2)}, u32[]{:S(2)}) collective-permute-start(f32[5,72,1,512]{3,1,0,2:T(8,128)} %collective-permute-done.2), channel_id=1, source_target_pairs={{1,0},{2,1},{3,2},{4,3},{5,4},{6,5},{7,6},{9,8},{10,9},{11,10},{12... | collective-permute-start | bytes 2211848 | tf_op jit(solution)/shard_map/ppermute | solution.py:26
  52.1 1.9 collective-permute-start.1
  54.1 0.1 copy.67
  54.2 0.1 fusion.124
  54.4 0.3 fusion.123
  54.6 14.5 %collective-permute-done.3 = f32[5,72,1,512]{3,1,0,2:T(8,128)} collective-permute-done((f32[5,72,1,512]{3,1,0,2:T(8,128)}, f32[5,72,1,512]{3,1,0,2:T(8,128)}, u32[]{:S(2)}, u32[]{:S(2)}) %collective-permute-start.3) | collective-permute-done | bytes 737312 | tf_op jit(solution)/shard_map/ppermute | solution.py:26
  69.1 7.4 %collective-permute-done.1 = f32[5,72,1,512]{3,1,0,2:T(8,128)} collective-permute-done((f32[5,72,1,512]{3,1,0,2:T(8,128)}, f32[5,72,1,512]{3,1,0,2:T(8,128)}, u32[]{:S(2)}, u32[]{:S(2)}) %collective-permute-start.1) | collective-permute-done | bytes 737312 | tf_op jit(solution)/shard_map/ppermute | solution.py:26
  76.5 3.2 %convolution_bitcast_fusion.3 = f32[5,72,1,512]{3,1,0,2:T(8,128)S(1)} fusion(f32[512,512,1]{1,0,2:T(8,128)S(1)} %fusion.10, f32[5,72,1,512]{3,1,0,2:T(8,128)S(1)} %copy.71, f32[5,72,1,511]{3,1,0,2:T(8,128)S(1)} %get-tuple-element.26, f32[5,72,1,1]{3,1,0,2:T(8,128)S(1)} %get-tuple-element.28, f32[5,72,1,1]{3,1,0,2:T(8,128)S(1)} %get-tuple-element.27, ...), kind=kOutput, calls=%fused_computation.17 | convolution fusion | flops 1135042560 | bytes 7094274 | tf_op jit(solution)/shard_map/flrb,rbc->flrc/dot_general | solution.py:55
  79.7 3.0 %collective-permute-start.6 = (f32[5,72,1,512]{3,1,0,2:T(8,128)S(1)}, f32[5,72,1,512]{3,1,0,2:T(8,128)}, u32[]{:S(2)}, u32[]{:S(2)}) collective-permute-start(f32[5,72,1,512]{3,1,0,2:T(8,128)S(1)} %convolution_bitcast_fusion.3), channel_id=1, source_target_pairs={{8,0},{16,8},{24,16},{32,24},{40,32},{48,40},{56,48},{64,56},{72,6... | collective-permute-start | bytes 2211848 | tf_op jit(solution)/shard_map/ppermute | solution.py:20
  82.8 1.2 copy.79
  83.9 5.3 %all-to-all-start.2 = ((f32[5,72,16,1,32]{1,4,0,3,2:T(8,128)}), f32[5,72,16,1,32]{1,4,0,3,2:T(8,128)}, u32[]{:S(2)}, u32[]{:S(2)}) async-start(f32[5,72,16,1,32]{1,4,0,3,2:T(8,128)} %bitcast.71), calls=%async_computation.2 | async-start | bytes 2621440 | tf_op jit(solution)/shard_map/all_to_all | solution.py:101
  89.2 5.7 %collective-permute-done.6 = f32[5,72,1,512]{3,1,0,2:T(8,128)} collective-permute-done((f32[5,72,1,512]{3,1,0,2:T(8,128)S(1)}, f32[5,72,1,512]{3,1,0,2:T(8,128)}, u32[]{:S(2)}, u32[]{:S(2)}) %collective-permute-start.6) | collective-permute-done | bytes 737312 | tf_op jit(solution)/shard_map/ppermute | solution.py:20
  94.9 1.9 collective-permute-start.7
  96.8 2.7 collective-permute-done.4
  99.5 1.9 collective-permute-start.5
  101.4 0.1 copy.58
  101.5 7.6 %all-to-all-done.2 = f32[5,72,16,1,32]{1,4,0,3,2:T(8,128)} async-done(((f32[5,72,16,1,32]{1,4,0,3,2:T(8,128)}), f32[5,72,16,1,32]{1,4,0,3,2:T(8,128)}, u32[]{:S(2)}, u32[]{:S(2)}) %all-to-all-start.2) | async-done | bytes 737312 | tf_op jit(solution)/shard_map/all_to_all | solution.py:101
  109.1 2.5 copy.69
  111.6 1.7 copy.70
  113.5 0.3 fusion.121
  113.7 2.7 collective-permute-done.7
  116.4 1.0 collective-permute-done.5
  117.4 3.1 %fusion.17 = f32[5,72,512]{2,1,0:T(8,128)S(1)} fusion(f32[5,72,1,512]{3,1,0,2:T(8,128)S(1)} %copy.70, f32[512,512,1]{1,0,2:T(8,128)S(1)} %fusion.10, f32[5,72,1,512]{3,1,0,2:T(8,128)S(1)} %convolution_bitcast_fusion.3, f32[5,72,1,511]{3,1,0,2:T(8,128)S(1)} %get-tuple-element.22, f32[5,72,1,1]{3,1,0,2:T(8,128)S(1)} %get-tuple-element.24, ...), kind=kOutput, calls=%fused_computation.20 | convolution fusion | flops 1135411200 | bytes 7979010 | tf_op jit(solution)/shard_map/flrb,rbc->flrc/dot_general | solution.py:55
  120.5 1.4 broadcast_multiply_fusion.1
  122.0 4.0 %collective-permute-start.10 = (f32[5,72,1,512]{3,1,0,2:T(8,128)S(1)}, f32[5,72,1,512]{3,1,0,2:T(8,128)S(1)}, u32[]{:S(2)}, u32[]{:S(2)}) collective-permute-start(f32[5,72,1,512]{3,1,0,2:T(8,128)S(1)} %get-tuple-element.32), channel_id=1, source_target_pairs={{8,0},{16,8},{24,16},{32,24},{40,32},{48,40},{56,48},{64,56},{72,6... | collective-permute-start | bytes 2211848 | tf_op jit(solution)/shard_map/ppermute | solution.py:20
  126.1 8.9 %collective-permute-done.10 = f32[5,72,1,512]{3,1,0,2:T(8,128)S(1)} collective-permute-done((f32[5,72,1,512]{3,1,0,2:T(8,128)S(1)}, f32[5,72,1,512]{3,1,0,2:T(8,128)S(1)}, u32[]{:S(2)}, u32[]{:S(2)}) %collective-permute-start.10) | collective-permute-done | bytes 737312 | tf_op jit(solution)/shard_map/ppermute | solution.py:20
  134.9 3.6 %collective-permute-start.11 = (f32[5,72,1,512]{3,1,0,2:T(8,128)S(1)}, f32[5,72,1,512]{3,1,0,2:T(8,128)S(1)}, u32[]{:S(2)}, u32[]{:S(2)}) collective-permute-start(f32[5,72,1,512]{3,1,0,2:T(8,128)S(1)} %collective-permute-done.10), channel_id=1, source_target_pairs={{1,0},{2,1},{3,2},{4,3},{5,4},{6,5},{7,6},{9,8},{10,9},{11,10},{12... | collective-permute-start | bytes 2211848 | tf_op jit(solution)/shard_map/ppermute | solution.py:26
  138.6 0.4 collective-permute-done.8
  139.0 1.9 collective-permute-start.9
  141.0 0.3 fusion.117
  141.3 0.3 fusion.120
  141.6 15.7 %collective-permute-done.11 = f32[5,72,1,512]{3,1,0,2:T(8,128)S(1)} collective-permute-done((f32[5,72,1,512]{3,1,0,2:T(8,128)S(1)}, f32[5,72,1,512]{3,1,0,2:T(8,128)S(1)}, u32[]{:S(2)}, u32[]{:S(2)}) %collective-permute-start.11) | collective-permute-done | bytes 737312 | tf_op jit(solution)/shard_map/ppermute | solution.py:26
  157.3 11.1 %collective-permute-done.9 = f32[5,72,1,512]{3,1,0,2:T(8,128)S(1)} collective-permute-done((f32[5,72,1,512]{3,1,0,2:T(8,128)S(1)}, f32[5,72,1,512]{3,1,0,2:T(8,128)S(1)}, u32[]{:S(2)}, u32[]{:S(2)}) %collective-permute-start.9) | collective-permute-done | bytes 737312 | tf_op jit(solution)/shard_map/ppermute | solution.py:26
  168.4 1.9 broadcast_multiply_fusion
  170.3 3.5 %collective-permute-start.14 = (f32[5,72,1,512]{3,1,0,2:T(8,128)S(1)}, f32[5,72,1,512]{3,1,0,2:T(8,128)S(1)}, u32[]{:S(2)}, u32[]{:S(2)}) collective-permute-start(f32[5,72,1,512]{3,1,0,2:T(8,128)S(1)} %get-tuple-element.34), channel_id=1, source_target_pairs={{8,0},{16,8},{24,16},{32,24},{40,32},{48,40},{56,48},{64,56},{72,6... | collective-permute-start | bytes 2211848 | tf_op jit(solution)/shard_map/ppermute | solution.py:20
  174.0 8.9 %collective-permute-done.14 = f32[5,72,1,512]{3,1,0,2:T(8,128)S(1)} collective-permute-done((f32[5,72,1,512]{3,1,0,2:T(8,128)S(1)}, f32[5,72,1,512]{3,1,0,2:T(8,128)S(1)}, u32[]{:S(2)}, u32[]{:S(2)}) %collective-permute-start.14) | collective-permute-done | bytes 737312 | tf_op jit(solution)/shard_map/ppermute | solution.py:20
  182.8 1.9 collective-permute-start.15
  184.8 2.1 collective-permute-done.12
  186.9 1.9 collective-permute-start.13
  188.9 0.3 fusion.113
  189.2 0.3 fusion.116
  189.5 6.7 %collective-permute-done.15 = f32[5,72,1,512]{3,1,0,2:T(8,128)S(1)} collective-permute-done((f32[5,72,1,512]{3,1,0,2:T(8,128)S(1)}, f32[5,72,1,512]{3,1,0,2:T(8,128)S(1)}, u32[]{:S(2)}, u32[]{:S(2)}) %collective-permute-start.15) | collective-permute-done | bytes 737312 | tf_op jit(solution)/shard_map/ppermute | solution.py:26
  196.2 17.7 %collective-permute-done.13 = f32[5,72,1,512]{3,1,0,2:T(8,128)S(1)} collective-permute-done((f32[5,72,1,512]{3,1,0,2:T(8,128)S(1)}, f32[5,72,1,512]{3,1,0,2:T(8,128)S(1)}, u32[]{:S(2)}, u32[]{:S(2)}) %collective-permute-start.13) | collective-permute-done | bytes 737312 | tf_op jit(solution)/shard_map/ppermute | solution.py:26
  213.8 1.1 fusion.52
  214.9 0.9 copy.72
  215.8 25.7 %all_to_all.16 = f32[5,72,1,1,512]{1,3,2,0,4:T(1,128)S(1)} all-to-all(f32[5,72,1,1,512]{1,3,2,0,4:T(1,128)S(1)} %copy.72), channel_id=1, replica_groups=mesh['wide'=16,'narrow'=8] {'wide'}, dimensions={4} | all-to-all | bytes 1474560 | tf_op jit(solution)/shard_map/all_to_all | solution.py:130
  241.7 0.7 copy.74
  242.4 2.8 %broadcast_in_dim.4 = f32[5,72,16,32,4]{1,2,4,3,0:T(8,128)} broadcast(f32[5,72,16,32]{1,2,3,0:T(8,128)S(1)} %copy.74), dimensions={0,1,2,3} | broadcast | bytes 3686400 | tf_op jit(solution)/shard_map/broadcast_in_dim | solution.py:138
  245.2 5.5 %copy.75 = f32[5,72,16,128]{3,2,1,0:T(8,128)} copy(f32[5,72,16,128]{1,2,3,0:T(8,128)} %bitcast.69) | data formatting | bytes 5898240 | tf_op jit(solution)/shard_map/reshape | solution.py:138
  250.7 8.1 %broadcast_in_dim.5 = f32[5,72,16,4,128]{4,3,2,1,0:T(4,128)} broadcast(f32[5,72,16,128]{3,2,1,0:T(8,128)} %copy.75), dimensions={0,1,2,4} | broadcast | bytes 14745600 | tf_op jit(solution)/shard_map/broadcast_in_dim | solution.py:138
  258.8 11.2 %add_convert_fusion = bf16[5,72,64,128]{3,2,1,0:T(8,128)(2,1)} fusion(f32[5,72,64,128]{3,2,1,0:T(8,128)} %bitcast.68, bf16[5,72,64,128]{3,2,1,0:T(8,128)(2,1)} %param.4), kind=kLoop, calls=%fused_computation | loop fusion | flops 8847360 | bytes 23592960 | tf_op jit(solution)/shard_map/convert_element_type | solution.py:139
  (24 shorter events, 0.9 us)
Async XLA Ops:
  2.5 5.8 %slice-start = ((bf16[5,72,64,128]{3,2,1,0:T(8,128)(2,1)}), bf16[1,72,64,128]{3,2,1,0:T(8,128)(2,1)S(1)}, s32[]{:S(2)}) async-start(bf16[5,72,64,128]{3,2,1,0:T(8,128)(2,1)} %param.4), calls=%async_computation.4 | async-start | bytes 2359296 | tf_op jit(solution)/shard_map/slice | solution.py:85
  2.5 25.1 %all-to-all-start = ((f32[5,72,16,1,32]{1,4,0,3,2:T(8,128)}), f32[5,72,16,1,32]{1,4,0,3,2:T(8,128)S(1)}, u32[]{:S(2)}, u32[]{:S(2)}) async-start(f32[5,72,16,1,32]{1,4,0,3,2:T(8,128)} %bitcast.72), calls=%async_computation | async-start | bytes 2621440 | tf_op jit(solution)/shard_map/all_to_all | solution.py:102
  8.3 2.2 copy-start.1
  30.4 17.6 %collective-permute-start.2 = (f32[5,72,1,512]{3,1,0,2:T(8,128)S(1)}, f32[5,72,1,512]{3,1,0,2:T(8,128)}, u32[]{:S(2)}, u32[]{:S(2)}) collective-permute-start(f32[5,72,1,512]{3,1,0,2:T(8,128)S(1)} %copy.71), channel_id=1, source_target_pairs={{8,0},{16,8},{24,16},{32,24},{40,32},{48,40},{56,48},{64,56},{72,6... | collective-permute-start | bytes 2211848 | tf_op jit(solution)/shard_map/ppermute | solution.py:20
  31.0 21.1 %collective-permute-start = (f32[5,72,1,512]{3,1,0,2:T(8,128)S(1)}, f32[5,72,1,512]{3,1,0,2:T(8,128)}, u32[]{:S(2)}, u32[]{:S(2)}) collective-permute-start(f32[5,72,1,512]{3,1,0,2:T(8,128)S(1)} %copy.71), channel_id=1, source_target_pairs={{120,0},{0,8},{8,16},{16,24},{24,32},{32,40},{40,48},{48,56},{56,6... | collective-permute-start | bytes 2211848 | tf_op jit(solution)/shard_map/ppermute | solution.py:20
  32.0 22.1 %all-to-all-start.1 = ((f32[2,72,16,1,32]{1,4,0,3,2:T(8,128)}), f32[2,72,16,1,32]{1,4,0,3,2:T(8,128)S(1)}, u32[]{:S(2)}, u32[]{:S(2)}) async-start(f32[2,72,16,1,32]{1,4,0,3,2:T(8,128)} %copy.57), calls=%async_computation.1 | async-start | bytes 1048576 | tf_op jit(solution)/shard_map/all_to_all | solution.py:103
  48.1 21.0 %collective-permute-start.3 = (f32[5,72,1,512]{3,1,0,2:T(8,128)}, f32[5,72,1,512]{3,1,0,2:T(8,128)}, u32[]{:S(2)}, u32[]{:S(2)}) collective-permute-start(f32[5,72,1,512]{3,1,0,2:T(8,128)} %collective-permute-done.2), channel_id=1, source_target_pairs={{1,0},{2,1},{3,2},{4,3},{5,4},{6,5},{7,6},{9,8},{10,9},{11,10},{12... | collective-permute-start | bytes 2211848 | tf_op jit(solution)/shard_map/ppermute | solution.py:26
  52.1 24.4 %collective-permute-start.1 = (f32[5,72,1,512]{3,1,0,2:T(8,128)}, f32[5,72,1,512]{3,1,0,2:T(8,128)}, u32[]{:S(2)}, u32[]{:S(2)}) collective-permute-start(f32[5,72,1,512]{3,1,0,2:T(8,128)} %collective-permute-done), channel_id=1, source_target_pairs={{0,1},{1,2},{2,3},{3,4},{4,5},{5,6},{6,7},{8,9},{9,10},{10,11},{11... | collective-permute-start | bytes 2211848 | tf_op jit(solution)/shard_map/ppermute | solution.py:26
  76.5 6.3 %copy-start = (f32[5,72,16,32]{1,3,2,0:T(8,128)S(1)}, f32[5,72,16,32]{1,3,2,0:T(8,128)}, u32[]{:S(2)}) copy-start(f32[5,72,16,32]{1,3,2,0:T(8,128)} %param.5) | copy-start | bytes 2211844
  79.7 15.2 %collective-permute-start.6 = (f32[5,72,1,512]{3,1,0,2:T(8,128)S(1)}, f32[5,72,1,512]{3,1,0,2:T(8,128)}, u32[]{:S(2)}, u32[]{:S(2)}) collective-permute-start(f32[5,72,1,512]{3,1,0,2:T(8,128)S(1)} %convolution_bitcast_fusion.3), channel_id=1, source_target_pairs={{8,0},{16,8},{24,16},{32,24},{40,32},{48,40},{56,48},{64,56},{72,6... | collective-permute-start | bytes 2211848 | tf_op jit(solution)/shard_map/ppermute | solution.py:20
  82.8 16.7 %collective-permute-start.4 = (f32[5,72,1,512]{3,1,0,2:T(8,128)S(1)}, f32[5,72,1,512]{3,1,0,2:T(8,128)}, u32[]{:S(2)}, u32[]{:S(2)}) collective-permute-start(f32[5,72,1,512]{3,1,0,2:T(8,128)S(1)} %convolution_bitcast_fusion.3), channel_id=1, source_target_pairs={{120,0},{0,8},{8,16},{16,24},{24,32},{32,40},{40,48},{48,56},{56,6... | collective-permute-start | bytes 2211848 | tf_op jit(solution)/shard_map/ppermute | solution.py:20
  83.9 25.2 %all-to-all-start.2 = ((f32[5,72,16,1,32]{1,4,0,3,2:T(8,128)}), f32[5,72,16,1,32]{1,4,0,3,2:T(8,128)}, u32[]{:S(2)}, u32[]{:S(2)}) async-start(f32[5,72,16,1,32]{1,4,0,3,2:T(8,128)} %bitcast.71), calls=%async_computation.2 | async-start | bytes 2621440 | tf_op jit(solution)/shard_map/all_to_all | solution.py:101
  94.9 21.5 %collective-permute-start.7 = (f32[5,72,1,512]{3,1,0,2:T(8,128)}, f32[5,72,1,512]{3,1,0,2:T(8,128)}, u32[]{:S(2)}, u32[]{:S(2)}) collective-permute-start(f32[5,72,1,512]{3,1,0,2:T(8,128)} %collective-permute-done.6), channel_id=1, source_target_pairs={{1,0},{2,1},{3,2},{4,3},{5,4},{6,5},{7,6},{9,8},{10,9},{11,10},{12... | collective-permute-start | bytes 2211848 | tf_op jit(solution)/shard_map/ppermute | solution.py:26
  99.5 17.9 %collective-permute-start.5 = (f32[5,72,1,512]{3,1,0,2:T(8,128)}, f32[5,72,1,512]{3,1,0,2:T(8,128)}, u32[]{:S(2)}, u32[]{:S(2)}) collective-permute-start(f32[5,72,1,512]{3,1,0,2:T(8,128)} %collective-permute-done.4), channel_id=1, source_target_pairs={{0,1},{1,2},{2,3},{3,4},{4,5},{5,6},{6,7},{8,9},{9,10},{10,11},{11... | collective-permute-start | bytes 2211848 | tf_op jit(solution)/shard_map/ppermute | solution.py:26
  122.0 13.0 %collective-permute-start.10 = (f32[5,72,1,512]{3,1,0,2:T(8,128)S(1)}, f32[5,72,1,512]{3,1,0,2:T(8,128)S(1)}, u32[]{:S(2)}, u32[]{:S(2)}) collective-permute-start(f32[5,72,1,512]{3,1,0,2:T(8,128)S(1)} %get-tuple-element.32), channel_id=1, source_target_pairs={{8,0},{16,8},{24,16},{32,24},{40,32},{48,40},{56,48},{64,56},{72,6... | collective-permute-start | bytes 2211848 | tf_op jit(solution)/shard_map/ppermute | solution.py:20
  126.0 13.0 %collective-permute-start.8 = (f32[5,72,1,512]{3,1,0,2:T(8,128)S(1)}, f32[5,72,1,512]{3,1,0,2:T(8,128)S(1)}, u32[]{:S(2)}, u32[]{:S(2)}) collective-permute-start(f32[5,72,1,512]{3,1,0,2:T(8,128)S(1)} %get-tuple-element.32), channel_id=1, source_target_pairs={{120,0},{0,8},{8,16},{16,24},{24,32},{32,40},{40,48},{48,56},{56,6... | collective-permute-start | bytes 2211848 | tf_op jit(solution)/shard_map/ppermute | solution.py:20
  134.9 22.4 %collective-permute-start.11 = (f32[5,72,1,512]{3,1,0,2:T(8,128)S(1)}, f32[5,72,1,512]{3,1,0,2:T(8,128)S(1)}, u32[]{:S(2)}, u32[]{:S(2)}) collective-permute-start(f32[5,72,1,512]{3,1,0,2:T(8,128)S(1)} %collective-permute-done.10), channel_id=1, source_target_pairs={{1,0},{2,1},{3,2},{4,3},{5,4},{6,5},{7,6},{9,8},{10,9},{11,10},{12... | collective-permute-start | bytes 2211848 | tf_op jit(solution)/shard_map/ppermute | solution.py:26
  139.0 29.5 %collective-permute-start.9 = (f32[5,72,1,512]{3,1,0,2:T(8,128)S(1)}, f32[5,72,1,512]{3,1,0,2:T(8,128)S(1)}, u32[]{:S(2)}, u32[]{:S(2)}) collective-permute-start(f32[5,72,1,512]{3,1,0,2:T(8,128)S(1)} %collective-permute-done.8), channel_id=1, source_target_pairs={{0,1},{1,2},{2,3},{3,4},{4,5},{5,6},{6,7},{8,9},{9,10},{10,11},{11... | collective-permute-start | bytes 2211848 | tf_op jit(solution)/shard_map/ppermute | solution.py:26
  170.3 12.5 %collective-permute-start.14 = (f32[5,72,1,512]{3,1,0,2:T(8,128)S(1)}, f32[5,72,1,512]{3,1,0,2:T(8,128)S(1)}, u32[]{:S(2)}, u32[]{:S(2)}) collective-permute-start(f32[5,72,1,512]{3,1,0,2:T(8,128)S(1)} %get-tuple-element.34), channel_id=1, source_target_pairs={{8,0},{16,8},{24,16},{32,24},{40,32},{48,40},{56,48},{64,56},{72,6... | collective-permute-start | bytes 2211848 | tf_op jit(solution)/shard_map/ppermute | solution.py:20
  173.9 13.0 %collective-permute-start.12 = (f32[5,72,1,512]{3,1,0,2:T(8,128)S(1)}, f32[5,72,1,512]{3,1,0,2:T(8,128)S(1)}, u32[]{:S(2)}, u32[]{:S(2)}) collective-permute-start(f32[5,72,1,512]{3,1,0,2:T(8,128)S(1)} %get-tuple-element.34), channel_id=1, source_target_pairs={{120,0},{0,8},{8,16},{16,24},{24,32},{32,40},{40,48},{48,56},{56,6... | collective-permute-start | bytes 2211848 | tf_op jit(solution)/shard_map/ppermute | solution.py:20
  182.8 13.3 %collective-permute-start.15 = (f32[5,72,1,512]{3,1,0,2:T(8,128)S(1)}, f32[5,72,1,512]{3,1,0,2:T(8,128)S(1)}, u32[]{:S(2)}, u32[]{:S(2)}) collective-permute-start(f32[5,72,1,512]{3,1,0,2:T(8,128)S(1)} %collective-permute-done.14), channel_id=1, source_target_pairs={{1,0},{2,1},{3,2},{4,3},{5,4},{6,5},{7,6},{9,8},{10,9},{11,10},{12... | collective-permute-start | bytes 2211848 | tf_op jit(solution)/shard_map/ppermute | solution.py:26
  186.9 27.0 %collective-permute-start.13 = (f32[5,72,1,512]{3,1,0,2:T(8,128)S(1)}, f32[5,72,1,512]{3,1,0,2:T(8,128)S(1)}, u32[]{:S(2)}, u32[]{:S(2)}) collective-permute-start(f32[5,72,1,512]{3,1,0,2:T(8,128)S(1)} %collective-permute-done.12), channel_id=1, source_target_pairs={{0,1},{1,2},{2,3},{3,4},{4,5},{5,6},{6,7},{8,9},{9,10},{10,11},{11... | collective-permute-start | bytes 2211848 | tf_op jit(solution)/shard_map/ppermute | solution.py:26
where the time goes:
time: 271 us; the launch traced here: 270 us
  waiting for transfers between devices  130 us (48%)
  starting transfers between devices  46.6 us (17%)
  local copies, waits for them, and re-layouts  32.9 us (12%)
  blocking collectives  25.7 us (9%)
  other arithmetic  19.4 us (7%)
  matrix products  15.1 us (6%)
    ppermute x8, waiting for transfers between devices, from_behind(): lax.ppermute(value, axis, [(source, source + steps) for source in range(f...  76.8 us
    ppermute x8, waiting for transfers between devices, shifted(): return lax.ppermute(block, axis, route)  28.6 us
    all_to_all x1, blocking collectives, shards(): lax.all_to_all(increment.reshape(FIELDS, LEVELS, 1, band_rows, cycle_size...  25.7 us
    ppermute x8, starting transfers between devices, from_behind(): lax.ppermute(value, axis, [(source, source + steps) for source in range(f...  19.2 us
    all_to_all x1, waiting for transfers between devices, shards(): lax.all_to_all(spread(background), 'wide', split_axis=2, concat_axis=4, t...  16.9 us
    convert_element_type x1, other arithmetic, shards(): return (trajectory.astype(jnp.float32) + fine_part).astype(jnp.bfloat16)  11.2 us
    ppermute x8, starting transfers between devices, shifted(): return lax.ppermute(block, axis, route)  11.2 us
    broadcast_in_dim x1, local copies, waits for them, and re-layouts, shards(): jnp.repeat(jnp.repeat(coarse_part, COARSEN, axis=3), COARSEN, axis=2)  8.07 us
  transfers between devices with their start and end apart: 19, of which 16 were waited for; matrix products, arithmetic and copies ran while one was open for 8% of the time, Pallas kernels for 0%

commit v1 on v0

v1 whole, which is shorter than its diff:
```python
import jax
import jax.numpy as jnp
import ml_dtypes
import numpy as np
from jax import lax
from jax.experimental import pallas as pl
from jax.experimental.pallas import tpu as pltpu
from jax.sharding import PartitionSpec as P

FIELDS = 5
LEVELS = 72
COARSEN = 4
ROWS = 16
COLS = 32
CYCLE = 512
HALF = 256
TOTAL_ROWS = 128
SHARE = 5
GROUP = 32
PLANES = FIELDS * SHARE
WIDE = 16
HALO = 4
BAND = ROWS + 2 * HALO

diffusion = 0.2
advection_scale = 0.3
MIB = 2**20


def harmonics():
    column = np.arange(HALF)

    def wave(function, wavenumbers):
        angle = 2 * np.pi * ((column[:, None] * wavenumbers[None, :]) % CYCLE) / CYCLE
        scale = np.where((wavenumbers == 0) | (wavenumbers == HALF), 1.0, 2.0)
        return function(angle) * np.sqrt(scale / CYCLE)

    even_cos, even_sin = np.arange(0, HALF + 1, 2), np.arange(2, HALF, 2)
    odd = np.arange(1, HALF, 2)
    even = np.concatenate([wave(np.cos, even_cos), wave(np.sin, even_sin)], axis=1)
    odds = np.concatenate([wave(np.cos, odd), wave(np.sin, odd)], axis=1)
    order = np.concatenate([even_cos, even_sin, odd, odd])
    return even, odds, order


def stacked(matrix):
    high = matrix.astype(ml_dtypes.bfloat16)
    low = (matrix - high.astype(np.float64)).astype(ml_dtypes.bfloat16)
    return np.concatenate([high, high, low], axis=0)


EVEN, ODD, WAVES = harmonics()
BASIS = np.stack([stacked(EVEN), stacked(ODD), stacked(EVEN.T), stacked(ODD.T)])


def pooling():
    fine = np.arange(4 * COLS)
    matrix = np.zeros((4, 4 * COLS, 4 * COLS), np.float32)
    for part in range(4):
        matrix[part, fine, part * COLS + fine // 4] = 1.0 / 16
    return matrix.reshape(4 * 4 * COLS, 4 * COLS)


def spreading():
    fine = np.arange(4 * COLS)
    matrix = np.zeros((4 * COLS, 4, 4 * COLS), np.float32)
    for part in range(4):
        matrix[part * COLS + fine // 4, part, fine] = 1.0
    matrix = matrix.reshape(4 * COLS, 16 * COLS)
    return np.concatenate([matrix, matrix]).astype(ml_dtypes.bfloat16)


def params(mib):
    return pltpu.CompilerParams(vmem_limit_bytes=mib * MIB)


def estimate(micros):
    return pl.CostEstimate(flops=int(micros * 1e9), bytes_accessed=int(micros * 1e6), transcendentals=0)


def scatter_levels(turned_ref, send_ref, fields, groups):
    size = groups * GROUP
    for field in range(fields):
        for group in range(groups):
            for level in range(SHARE):
                value = turned_ref[field * groups + group, pl.ds(level, WIDE, stride=SHARE), :]
                send_ref[pl.ds(group * GROUP + field * SHARE + level, WIDE, stride=size), :] = value


def pack_state(back_ref, traj_ref, pool_ref, send_ref, turned_ref, fine_ref):
    spare = jnp.zeros((8, 128), jnp.float32)
    fine_ref[...] = traj_ref[0].astype(jnp.float32).reshape(LEVELS * 64, 128)
    for group in range(4):
        for field in range(FIELDS):
            block = back_ref[field, 4 * group : 4 * group + 4].reshape(4 * COLS, LEVELS)
            turned_ref[field * 4 + group, 0:LEVELS, :] = block.T
            turned_ref[field * 4 + group, LEVELS:, :] = spare
        parts = []
        for part in range(4):
            first = 16 * group + 4 * part
            total = fine_ref[pl.ds(first, LEVELS, stride=64), :]
            for extra in range(1, 4):
                total = total + fine_ref[pl.ds(first + extra, LEVELS, stride=64), :]
            parts.append(total)
        mean = jnp.dot(
            jnp.concatenate(parts, axis=1),
            pool_ref[...],
            precision=lax.Precision.HIGHEST,
            preferred_element_type=jnp.float32,
        )
        turned_ref[FIELDS * 4 + group, 0:LEVELS, :] = advection_scale * jnp.tanh(mean)
        turned_ref[FIELDS * 4 + group, LEVELS:, :] = spare
    scatter_levels(turned_ref, send_ref, FIELDS + 1, 4)


def pack_departures(innov_ref, weight_ref, before_ref, after_ref, send_ref, turned_ref):
    spare = jnp.zeros((8, 128), jnp.float32)
    for field in range(FIELDS + 1):
        source = innov_ref.at[field] if field < FIELDS else weight_ref
        for group in range(5):
            if group < 4:
                block = source[4 * group : 4 * group + 4].reshape(4 * COLS, LEVELS)
            else:
                block = jnp.concatenate([before_ref[field], after_ref[field]], axis=0).reshape(4 * COLS, LEVELS)
            turned_ref[field * 5 + group, 0:LEVELS, :] = block.T
            turned_ref[field * 5 + group, LEVELS:, :] = spare
    scatter_levels(turned_ref, send_ref, FIELDS + 1, 5)


def lane_block():
    return lax.broadcasted_iota(jnp.int32, (GROUP, 128), 1) // COLS


def turn(value, blocks):
    shift = (COLS * blocks) % 128
    return value if shift == 0 else pltpu.roll(value, shift, 1)


def unpack_rows(load, store):
    block = lane_block()
    for quarter in range(4):
        pieces = [load(4 * quarter + source) for source in range(4)]
        for row in range(4):
            value = turn(pieces[0], -row)
            for source in range(1, 4):
                value = jnp.where(block == source, turn(pieces[source], source - row), value)
            store(row, slice(128 * quarter, 128 * quarter + 128), value)


def split_store(ref, at, value):
    high = value.astype(jnp.bfloat16)
    low = (value - high.astype(jnp.float32)).astype(jnp.bfloat16)
    ref[at, 0:HALF] = high
    ref[at, HALF:CYCLE] = low


def fold_store(even_ref, odd_ref, index, value):
    at = pl.ds(pl.multiple_of(index * GROUP, GROUP), GROUP)
    split_store(even_ref, at, value[:, :HALF] + value[:, HALF:])
    split_store(odd_ref, at, value[:, :HALF] - value[:, HALF:])


def product(ref, count, basis_ref, which):
    rows = slice(0, count)
    total = jnp.dot(ref[rows, :], basis_ref[which, 0:CYCLE], preferred_element_type=jnp.float32)
    return total + jnp.dot(
        ref[rows, 0:HALF], basis_ref[which, CYCLE:], preferred_element_type=jnp.float32
    )


def filtered(even_ref, odd_ref, basis_ref, resp_ref, first, rows, out_ref):
    count = rows * GROUP
    band = slice(first, first + rows)
    for ref, which, lanes in ((even_ref, 0, slice(0, HALF)), (odd_ref, 1, slice(HALF, CYCLE))):
        coefs = product(ref, count, basis_ref, which).reshape(rows, GROUP, HALF)
        coefs = (coefs * resp_ref[band, :, lanes]).reshape(count, HALF)
        split_store(ref, slice(0, count), coefs)
    even = product(even_ref, count, basis_ref, 2)
    odd = product(odd_ref, count, basis_ref, 3)
    out_ref[band, :, 0:HALF] = (even + odd).reshape(rows, GROUP, HALF)
    out_ref[band, :, HALF:CYCLE] = (even - odd).reshape(rows, GROUP, HALF)


def expand(source_ref, rows, out_ref):
    for field in range(FIELDS):
        out_ref[0:rows, SHARE * field : SHARE * field + SHARE, :] = source_ref[0:rows, PLANES : PLANES + SHARE, :]


def tangent(recv_ref, before_ref, after_ref, resp_ref, basis_ref, state_ref, drift_ref, row_ref, even_ref, odd_ref):
    for group in range(6):
        def load(source):
            if group == 0:
                return before_ref[source]
            if group == 5:
                return after_ref[source]
            return recv_ref[source, GROUP * (group - 1) : GROUP * group, :]

        def store(row, lanes, value):
            row_ref[4 * group + row, :, lanes] = value

        unpack_rows(load, store)
    drift_ref[:, GROUP - 8 :, :] = jnp.zeros((BAND, 8, CYCLE), jnp.float32)
    expand(row_ref, BAND, drift_ref)

    for step in range(2):
        first, last = 1 + step, BAND - 1 - step
        source_ref = row_ref if step == 0 else state_ref

        def body(index, carry):
            here = source_ref[index]
            east = pltpu.roll(here, CYCLE - 1, 1)
            west = pltpu.roll(here, 1, 1)
            near = source_ref[index - 1] + source_ref[index + 1] + east + west
            moved = here + diffusion * (near - 4.0 * here) + drift_ref[index] * (east - west)
            fold_store(even_ref, odd_ref, index - first, moved)
            return carry

        lax.fori_loop(first, last, body, 0)
        filtered(even_ref, odd_ref, basis_ref, resp_ref, first, last - first, state_ref)


def adjoint(recv_ref, state_ref, drift_ref, resp_ref, basis_ref, send_ref, row_ref, field_ref, weight_ref, even_ref, odd_ref):
    for group in range(5):
        def load(source):
            return recv_ref[source, GROUP * group : GROUP * group + GROUP, :]

        def store(row, lanes, value):
            if group < 4:
                at = 4 * group + row + HALO
            else:
                at = 2 + row if row < 2 else 18 + row
            row_ref[at, :, lanes] = value

        unpack_rows(load, store)
    weight_ref[:, GROUP - 8 :, :] = jnp.zeros((BAND, 8, CYCLE), jnp.float32)
    for field in range(FIELDS):
        weight_ref[2:22, SHARE * field : SHARE * field + SHARE, :] = row_ref[2:22, PLANES : PLANES + SHARE, :]

    def depart(index, carry):
        fold_store(even_ref, odd_ref, index - 2, weight_ref[index] * (state_ref[index] - row_ref[index]))
        return carry

    lax.fori_loop(2, 22, depart, 0)
    for step in range(2):
        first, last = 2 + step, BAND - 2 - step
        filtered(even_ref, odd_ref, basis_ref, resp_ref, first, last - first, field_ref)

        def body(index, carry):
            here = field_ref[index]
            carried = drift_ref[index] * here
            near = field_ref[index - 1] + field_ref[index + 1]
            near = near + pltpu.roll(here, CYCLE - 1, 1) + pltpu.roll(here, 1, 1)
            moved = here + diffusion * (near - 4.0 * here)
            moved = moved + pltpu.roll(carried, 1, 1) - pltpu.roll(carried, CYCLE - 1, 1)
            if step == 0:
                fold_store(even_ref, odd_ref, index - 3, moved)
            else:
                row_ref[index] = moved
            return carry

        lax.fori_loop(first + 1, last - 1, body, 0)
    block = lane_block()
    for group in range(4):
        for quarter in range(4):
            lanes = slice(128 * quarter, 128 * quarter + 128)
            pieces = [row_ref[HALO + 4 * group + row, :, lanes] for row in range(4)]
            for source in range(4):
                value = turn(pieces[0], -source)
                for row in range(1, 4):
                    value = jnp.where(block == row, turn(pieces[row], row - source), value)
                send_ref[4 * quarter + source, PLANES * group : PLANES * group + PLANES, :] = value[:PLANES]


def prolong(back_ref, cost_ref, traj_ref, spread_ref, out_ref, wide_ref):
    for group in range(4):
        change = (
            back_ref[0, GROUP * group : GROUP * group + PLANES, :]
            - cost_ref[0, PLANES * group : PLANES * group + PLANES, :]
        )
        high = change.astype(jnp.bfloat16)
        low = (change - high.astype(jnp.float32)).astype(jnp.bfloat16)
        spread = jnp.dot(
            jnp.concatenate([high, low], axis=1), spread_ref[...], preferred_element_type=jnp.float32
        )
        for part in range(4):
            wide_ref[4 * group + part, 0:PLANES, :] = spread[:, 128 * part : 128 * part + 128]
    upper = lax.broadcasted_iota(jnp.int32, (8, 128), 0) < 4
    for field in range(FIELDS):
        for level in range(SHARE):
            plane = field * SHARE + level
            rows = []
            for pair in range(8):
                above = jnp.broadcast_to(wide_ref[2 * pair, plane : plane + 1, :], (8, 128))
                below = jnp.broadcast_to(wide_ref[2 * pair + 1, plane : plane + 1, :], (8, 128))
                rows.append(jnp.where(upper, above, below))
            fine = jnp.concatenate(rows, axis=0)
            out_ref[field, level] = (traj_ref[field, level].astype(jnp.float32) + fine).astype(jnp.bfloat16)


def response_rows(narrow_index):
    row = narrow_index * ROWS - HALO + jnp.arange(BAND, dtype=jnp.int32)
    latitude = jnp.pi * ((row.astype(jnp.float32) + 0.5) / TOTAL_ROWS - 0.5)
    cutoff = 0.5 * CYCLE * jnp.cos(latitude)
    inside = (row >= 0) & (row < TOTAL_ROWS)
    cutoff = jnp.where(inside, cutoff, 1.0)
    scaled = jnp.asarray(WAVES, jnp.float32)[None, :] / cutoff[:, None]
    response = jnp.where(inside[:, None], 1.0 / (1.0 + scaled**4), 0.0)
    return response.reshape(BAND, 1, CYCLE)


def shards(trajectory, innovation, background, obs_weight):
    f32 = jnp.float32
    narrow_count = lax.axis_size("narrow")
    narrow_index = lax.axis_index("narrow")
    onward = [(i, i + 1) for i in range(narrow_count - 1)]
    backward = [(i + 1, i) for i in range(narrow_count - 1)]
    innov = innovation.transpose(0, 2, 3, 1)
    back = background.transpose(0, 2, 3, 1)
    weight = obs_weight.transpose(1, 2, 0)
    basis = jnp.asarray(BASIS)
    response = response_rows(narrow_index)

    def edge(rows):
        return jnp.concatenate([innov[:, rows], weight[None, rows]], axis=0)

    before = lax.ppermute(edge(slice(14, 16)), "narrow", onward)
    after = lax.ppermute(edge(slice(0, 2)), "narrow", backward)

    full = pl.BlockSpec(memory_space=pltpu.VMEM)
    send_state = pl.pallas_call(
        pack_state,
        grid=(1,),
        in_specs=[
            pl.BlockSpec((FIELDS, ROWS, COLS, LEVELS), lambda i: (0, 0, 0, 0)),
            pl.BlockSpec((1, LEVELS, 64, 128), lambda i: (0, 0, 0, 0)),
            pl.BlockSpec((512, 128), lambda i: (0, 0)),
        ],
        out_specs=pl.BlockSpec((WIDE * 4 * GROUP, 128), lambda i: (0, 0)),
        out_shape=jax.ShapeDtypeStruct((WIDE * 4 * GROUP, 128), f32),
        scratch_shapes=[pltpu.VMEM((24, 80, 128), f32), pltpu.VMEM((LEVELS * 64, 128), f32)],
        compiler_params=params(40),
        cost_estimate=estimate(3),
    )(back, trajectory, jnp.asarray(pooling()))
    send_state = send_state.reshape(WIDE, 4 * GROUP, 128)
    held_state = lax.all_to_all(send_state, "wide", split_axis=0, concat_axis=0, tiled=True)

    send_depart = pl.pallas_call(
        pack_departures,
        in_specs=[full] * 4,
        out_specs=full,
        out_shape=jax.ShapeDtypeStruct((WIDE * 5 * GROUP, 128), f32),
        scratch_shapes=[pltpu.VMEM((30, 80, 128), f32)],
        compiler_params=params(40),
        cost_estimate=estimate(3),
    )(innov, weight, before, after)
    send_depart = send_depart.reshape(WIDE, 5 * GROUP, 128)

    north = lax.ppermute(held_state[:, 3 * GROUP :], "narrow", onward)
    south = lax.ppermute(held_state[:, :GROUP], "narrow", backward)
    held_depart = lax.all_to_all(send_depart, "wide", split_axis=0, concat_axis=0, tiled=True)

    rows_shape = (BAND, GROUP, CYCLE)
    folded = pltpu.VMEM(((BAND - 2) * GROUP, CYCLE), jnp.bfloat16)
    state, drift = pl.pallas_call(
        tangent,
        in_specs=[full] * 5,
        out_specs=[full] * 2,
        out_shape=[jax.ShapeDtypeStruct(rows_shape, f32)] * 2,
        scratch_shapes=[pltpu.VMEM(rows_shape, f32), folded, folded],
        compiler_params=params(48),
        cost_estimate=estimate(5),
    )(held_state, north, south, response, basis)
    send_cost = pl.pallas_call(
        adjoint,
        in_specs=[full] * 5,
        out_specs=full,
        out_shape=jax.ShapeDtypeStruct((WIDE, 4 * PLANES, 128), f32),
        scratch_shapes=[pltpu.VMEM(rows_shape, f32)] * 3 + [folded, folded],
        compiler_params=params(48),
        cost_estimate=estimate(5),
    )(held_depart, state, drift, response, basis)
    costate = lax.all_to_all(send_cost, "wide", split_axis=0, concat_axis=0, tiled=True)

    fine_block = pl.BlockSpec((FIELDS, SHARE, 64, 128), lambda i: (0, i, 0, 0))
    return pl.pallas_call(
        prolong,
        grid=(pl.cdiv(LEVELS, SHARE),),
        in_specs=[
            pl.BlockSpec((1, 4 * GROUP, 128), lambda i: (i, 0, 0)),
            pl.BlockSpec((1, 4 * PLANES, 128), lambda i: (i, 0, 0)),
            fine_block,
            pl.BlockSpec((256, 512), lambda i: (0, 0)),
        ],
        out_specs=fine_block,
        out_shape=jax.ShapeDtypeStruct(trajectory.shape, jnp.bfloat16),
        scratch_shapes=[pltpu.VMEM((16, GROUP, 128), f32)],
        compiler_params=params(32),
        cost_estimate=estimate(5),
    )(send_state, costate, trajectory, jnp.asarray(spreading()))


def solution(mesh):
    in_specs = (
        P(None, None, "narrow", "wide"),
        P(None, None, "narrow", "wide"),
        P(None, None, "narrow", "wide"),
        P(None, "narrow", "wide"),
    )
    out_specs = P(None, None, "narrow", "wide")
    return jax.shard_map(shards, mesh=mesh, in_specs=in_specs, out_specs=out_specs, check_vma=False)
```

time: 271 us -> 123 us (0.45)
  waiting for transfers between devices: 130 us -> 20.6 us
  Pallas kernels: 0 us -> 37.4 us
  other arithmetic: 19.4 us -> 0.25 us
  local copies, waits for them, and re-layouts: 32.9 us -> 13.9 us
  starting transfers between devices: 46.6 us -> 28.9 us
  matrix products: 15.1 us -> 0 us
  blocking collectives: 25.7 us -> 19.4 us
    ppermute x16 -> x4, waiting for transfers between devices: 105 us -> 20.5 us  [the longest x1 8.13 us: shards(): before = lax.ppermute(edge(slice(14, 16)), 'narrow', onward)]
    pallas_call x0 -> x5, Pallas kernels: none -> 37.4 us  [the longest x1 11.1 us: shards(): pl.pallas_call(adjoint, in_specs=[full] * 5, out_specs=full, out_shape=ja...]
    all_to_all x3 -> x2, waiting for transfers between devices: 24.5 us -> 0.01 us  [the longest x1 0.01 us: shards(): lax.all_to_all(send_state, 'wide', split_axis=0, concat_axis=0, tiled=True)]
    dot_general x5 -> x0, matrix products: 15.1 us -> none  [the longest x2 6.34 us: tangent_step(): jnp.einsum('flrb,rbc->flrc', updated, kernel, precision=lax.Precision.HIG...]
    ppermute x16 -> x4, starting transfers between devices: 30.3 us -> 18.2 us  [the longest x1 6.78 us: shards(): south = lax.ppermute(held_state[:, :GROUP], 'narrow', backward)]
    reshape x6 -> x0, local copies, waits for them, and re-layouts: 11.5 us -> none  [the longest x1 5.51 us: shards(): jnp.repeat(coarse_part, COARSEN, axis=3)]
    convert_element_type x1 -> x0, other arithmetic: 11.2 us -> none  [shards(): return (trajectory.astype(jnp.float32) + fine_part).astype(jnp.bfloat16)]
    broadcast_in_dim x2 -> x1, local copies, waits for them, and re-layouts: 10.8 us -> 0.01 us  [edge(): return jnp.concatenate([innov[:, rows], weight[None, rows]], axis=0)]
  transfers between devices with their start and end apart: 19 -> 6, of which waited for: 16 -> 3; matrix products, arithmetic and copies ran while one was open for 8% -> 0% of each run, Pallas kernels for 0% -> 10%
where the time goes in v1:
time: 123 us; the launch traced here: 121 us
  Pallas kernels  37.4 us (30%)
  starting transfers between devices  28.9 us (23%)
  waiting for transfers between devices  20.6 us (17%)
  blocking collectives  19.4 us (16%)
  local copies, waits for them, and re-layouts  13.9 us (11%)
    all_to_all x1, blocking collectives, shards(): lax.all_to_all(send_cost, 'wide', split_axis=0, concat_axis=0, tiled=True)  19.4 us
    unnamed x26, local copies, waits for them, and re-layouts  13.8 us
    pallas_call x1, Pallas kernels, shards(): pl.pallas_call(adjoint, in_specs=[full] * 5, out_specs=full, out_shape=ja...  11.1 us
    pallas_call x1, Pallas kernels, shards(): pl.pallas_call(prolong, grid=(pl.cdiv(LEVELS, SHARE),), in_specs=[pl.Bloc...  11 us
    pallas_call x1, Pallas kernels, shards(): pl.pallas_call(tangent, in_specs=[full] * 5, out_specs=[full] * 2, out_sh...  10.6 us
    ppermute x1, waiting for transfers between devices, shards(): before = lax.ppermute(edge(slice(14, 16)), 'narrow', onward)  8.13 us
    ppermute x1, waiting for transfers between devices, shards(): south = lax.ppermute(held_state[:, :GROUP], 'narrow', backward)  8 us
    ppermute x1, starting transfers between devices, shards(): south = lax.ppermute(held_state[:, :GROUP], 'narrow', backward)  6.78 us
  transfers between devices with their start and end apart: 6, of which 3 were waited for; matrix products, arithmetic and copies ran while one was open for 0% of the time, Pallas kernels for 10%

profile of v1, /device:TPU:64, one launch (start us, length us, event | category | flops | bytes accessed | tf_op | source)
XLA Modules:
  0.0 120.5 jit_solution(617389826118865079)
XLA Ops:
  0.0 0.0 copy-start.3
  0.0 2.7 %copy-done.3 = bf16[5,72,64,128]{3,2,1,0:T(8,128)(2,1)S(1)} copy-done((bf16[5,72,64,128]{3,2,1,0:T(8,128)(2,1)S(1)}, bf16[5,72,64,128]{3,2,1,0:T(8,128)(2,1)}, u32[]{:S(2)}) %copy-start.3) | copy-done | bytes 5898264
  2.7 0.0 copy-start.5
  2.7 1.3 %copy-done.5 = f32[5,72,16,32]{1,3,2,0:T(8,128)S(1)} copy-done((f32[5,72,16,32]{1,3,2,0:T(8,128)S(1)}, f32[5,72,16,32]{1,3,2,0:T(8,128)}, u32[]{:S(2)}) %copy-start.5) | copy-done | bytes 737304
  4.0 0.0 copy-start.7
  4.0 0.9 copy-done.7
  4.9 3.7 %shard_map.82 = f32[2048,128]{1,0:T(8,128)} custom-call(f32[5,16,32,72]{3,2,1,0:T(8,128)S(1)} %bitcast.14, bf16[5,72,64,128]{3,2,1,0:T(8,128)(2,1)S(1)} %copy-done.3, f32[512,128]{1,0:T(8,128)S(1)} %copy-done.7), custom_call_target="tpu_custom_call" | custom-call | flops 3000000000 | bytes 3000000 | tf_op jit(solution)/shard_map/pallas_call | solution.py:330
  8.6 0.0 copy-start.2
  8.6 0.0 copy-start.1
  8.6 5.8 %all-to-all-start.1 = ((f32[16,128,128]{2,1,0:T(8,128)}), f32[16,128,128]{2,1,0:T(8,128)S(1)}, u32[]{:S(2)}, u32[]{:S(2)}) async-start(f32[16,128,128]{2,1,0:T(8,128)} %bitcast.1.back_ref), calls=%async_computation.1 | async-start | bytes 2097152 | tf_op jit(solution)/shard_map/all_to_all | solution.py:345
  14.4 0.0 copy-done.2
  14.4 0.0 copy-done.1
  14.5 3.4 %collective-permute-start = (f32[6,2,32,72]{3,2,1,0:T(8,128)S(1)}, f32[6,2,32,72]{3,2,1,0:T(8,128)S(1)}, u32[]{:S(2)}, u32[]{:S(2)}) collective-permute-start(f32[6,2,32,72]{3,2,1,0:T(8,128)S(1)} %pad_maximum_fusion), channel_id=1, source_target_pairs={{0,1},{1,2},{2,3},{3,4},{4,5},{5,6},{6,7},{8,9},{9,10},{10,11},{11... | collective-permute-start | bytes 331784 | tf_op jit(solution)/shard_map/ppermute | solution.py:326
  17.9 6.1 %collective-permute-start.1 = (f32[6,2,32,72]{3,2,1,0:T(8,128)S(1)}, f32[6,2,32,72]{3,2,1,0:T(8,128)S(1)}, u32[]{:S(2)}, u32[]{:S(2)}) collective-permute-start(f32[6,2,32,72]{3,2,1,0:T(8,128)S(1)} %pad_maximum_fusion.1), channel_id=1, source_target_pairs={{1,0},{2,1},{3,2},{4,3},{5,4},{6,5},{7,6},{9,8},{10,9},{11,10},{12... | collective-permute-start | bytes 331784 | tf_op jit(solution)/shard_map/ppermute | solution.py:327
  24.0 8.1 %collective-permute-done.before_ref = f32[6,2,32,72]{3,2,1,0:T(8,128)S(1)} collective-permute-done((f32[6,2,32,72]{3,2,1,0:T(8,128)S(1)}, f32[6,2,32,72]{3,2,1,0:T(8,128)S(1)}, u32[]{:S(2)}, u32[]{:S(2)}) %collective-permute-start) | collective-permute-done | bytes 110624 | tf_op jit(solution)/shard_map/ppermute | solution.py:326
  32.1 0.0 collective-permute-done.1.after_ref
  32.1 1.0 shard_map.83
  33.1 0.0 copy-start
  33.1 1.1 copy-done
  34.2 0.0 all-to-all-done.1.recv_ref
  34.2 0.0 copy-start.12
  34.2 5.0 %all-to-all-start = ((f32[16,160,128]{2,1,0:T(8,128)}), f32[16,160,128]{2,1,0:T(8,128)S(1)}, u32[]{:S(2)}, u32[]{:S(2)}) async-start(f32[16,160,128]{2,1,0:T(8,128)} %bitcast.9), calls=%async_computation | async-start | bytes 2621440 | tf_op jit(solution)/shard_map/all_to_all | solution.py:360
  39.2 6.8 %collective-permute-start.3 = (f32[16,32,128]{2,1,0:T(8,128)S(1)}, f32[16,32,128]{2,1,0:T(8,128)S(1)}, u32[]{:S(2)}, u32[]{:S(2)}) collective-permute-start(f32[16,32,128]{2,1,0:T(8,128)S(1)} %get-tuple-element.11), channel_id=1, source_target_pairs={{1,0},{2,1},{3,2},{4,3},{5,4},{6,5},{7,6},{9,8},{10,9},{11,10},{12... | collective-permute-start | bytes 786440 | tf_op jit(solution)/shard_map/ppermute | solution.py:359
  46.0 1.9 %collective-permute-start.2 = (f32[16,32,128]{2,1,0:T(8,128)S(1)}, f32[16,32,128]{2,1,0:T(8,128)S(1)}, u32[]{:S(2)}, u32[]{:S(2)}) collective-permute-start(f32[16,32,128]{2,1,0:T(8,128)S(1)} %get-tuple-element.12), channel_id=1, source_target_pairs={{0,1},{1,2},{2,3},{3,4},{4,5},{5,6},{6,7},{8,9},{9,10},{10,11},{11... | collective-permute-start | bytes 786440 | tf_op jit(solution)/shard_map/ppermute | solution.py:358
  48.0 0.0 copy-done.12
  48.0 0.2 broadcast_select_fusion.resp_ref
  48.2 8.0 %collective-permute-done.3.after_ref = f32[16,32,128]{2,1,0:T(8,128)S(1)} collective-permute-done((f32[16,32,128]{2,1,0:T(8,128)S(1)}, f32[16,32,128]{2,1,0:T(8,128)S(1)}, u32[]{:S(2)}, u32[]{:S(2)}) %collective-permute-start.3) | collective-permute-done | bytes 262176 | tf_op jit(solution)/shard_map/ppermute | solution.py:359
  56.2 4.4 %collective-permute-done.2.before_ref = f32[16,32,128]{2,1,0:T(8,128)S(1)} collective-permute-done((f32[16,32,128]{2,1,0:T(8,128)S(1)}, f32[16,32,128]{2,1,0:T(8,128)S(1)}, u32[]{:S(2)}, u32[]{:S(2)}) %collective-permute-start.2) | collective-permute-done | bytes 262176 | tf_op jit(solution)/shard_map/ppermute | solution.py:358
  60.6 10.6 %shard_map.84 = (f32[24,32,512]{2,1,0:T(8,128)S(1)}, f32[24,32,512]{2,1,0:T(8,128)S(1)}) custom-call(f32[16,128,128]{2,1,0:T(8,128)S(1)} %all-to-all-done.1.recv_ref, f32[16,32,128]{2,1,0:T(8,128)S(1)} %collective-permute-done.2.before_ref, f32[16,32,128]{2,1,0:T(8,128)S(1)} %collective-permute-done.3.after_ref, ...), custom_call_target="tpu_custom_call" | custom-call | flops 5000000000 | bytes 5000000 | tf_op jit(solution)/shard_map/pallas_call | solution.py:364
  71.1 0.0 copy-start.8
  71.2 1.1 copy-done.8
  72.3 0.0 copy-start.10
  72.3 1.2 copy-done.10
  73.5 0.0 all-to-all-done.recv_ref
  73.5 0.0 copy-start.9
  73.5 1.4 %copy-done.9 = f32[24,32,512]{2,1,0:T(8,128)S(1)} copy-done((f32[24,32,512]{2,1,0:T(8,128)S(1)}, f32[24,32,512]{2,1,0:T(8,128)}, u32[]{:S(2)}) %copy-start.9) | copy-done | bytes 1572888
  74.9 0.0 copy-start.11
  74.9 1.4 %copy-done.11 = f32[24,32,512]{2,1,0:T(8,128)S(1)} copy-done((f32[24,32,512]{2,1,0:T(8,128)S(1)}, f32[24,32,512]{2,1,0:T(8,128)}, u32[]{:S(2)}) %copy-start.11) | copy-done | bytes 1572888
  76.3 11.1 %shard_map.85 = f32[16,100,128]{2,1,0:T(8,128)S(1)} custom-call(f32[16,160,128]{2,1,0:T(8,128)S(1)} %all-to-all-done.recv_ref, f32[24,32,512]{2,1,0:T(8,128)S(1)} %copy-done.9, f32[24,32,512]{2,1,0:T(8,128)S(1)} %copy-done.11, f32[24,1,512]{2,1,0:T(1,128)S(1)} %broadcast_select_fusion.resp_ref, bf16[4,768,256]{2,1,0:T(8,128)(2,1)} %constant.37.clone.basis_ref), custom_call_target="tpu_custom_call" | custom-call | flops 5000000000 | bytes 5000000 | tf_op jit(solution)/shard_map/pallas_call | solution.py:373
  87.4 0.0 copy-start.6
  87.4 19.4 %all_to_all.15.cost_ref = f32[16,100,128]{2,1,0:T(8,128)S(1)} all-to-all(f32[16,100,128]{2,1,0:T(8,128)S(1)} %shard_map.85), channel_id=1, replica_groups=mesh['wide'=16,'narrow'=8] {'wide'}, dimensions={0} | all-to-all | bytes 1638400 | tf_op jit(solution)/shard_map/all_to_all | solution.py:382
  106.8 0.0 copy-done.6
  106.8 0.0 copy-start.4
  106.8 2.7 %copy-done.4 = bf16[5,72,64,128]{3,2,1,0:T(8,128)(2,1)S(1)} copy-done((bf16[5,72,64,128]{3,2,1,0:T(8,128)(2,1)S(1)}, bf16[5,72,64,128]{3,2,1,0:T(8,128)(2,1)}, u32[]{:S(2)}) %copy-start.4) | copy-done | bytes 5898264
  109.5 11.0 %shard_map.86 = bf16[5,72,64,128]{3,2,1,0:T(8,128)(2,1)} custom-call(f32[16,128,128]{2,1,0:T(8,128)} %bitcast.1.back_ref, f32[16,100,128]{2,1,0:T(8,128)S(1)} %all_to_all.15.cost_ref, bf16[5,72,64,128]{3,2,1,0:T(8,128)(2,1)S(1)} %copy-done.4, bf16[256,512]{1,0:T(8,128)(2,1)S(1)} %copy-done.6), custom_call_target="tpu_custom_call" | custom-call | flops 5000000000 | bytes 5000000 | tf_op jit(solution)/shard_map/pallas_call | solution.py:385
  (7 shorter events, 0.2 us)
Async XLA Ops:
  0.0 2.7 %copy-start.3 = (bf16[5,72,64,128]{3,2,1,0:T(8,128)(2,1)S(1)}, bf16[5,72,64,128]{3,2,1,0:T(8,128)(2,1)}, u32[]{:S(2)}) copy-start(bf16[5,72,64,128]{3,2,1,0:T(8,128)(2,1)} %traj_ref.3) | copy-start | bytes 17694724
  2.7 1.3 %copy-start.5 = (f32[5,72,16,32]{1,3,2,0:T(8,128)S(1)}, f32[5,72,16,32]{1,3,2,0:T(8,128)}, u32[]{:S(2)}) copy-start(f32[5,72,16,32]{1,3,2,0:T(8,128)} %param.10) | copy-start | bytes 2211844
  4.0 0.9 copy-start.7
  8.6 5.8 %copy-start.2 = (f32[72,16,32]{0,2,1:T(8,128)S(1)}, f32[72,16,32]{0,2,1:T(8,128)}, u32[]{:S(2)}) copy-start(f32[72,16,32]{0,2,1:T(8,128)} %param.11) | copy-start | bytes 442372
  8.6 5.8 %copy-start.1 = (f32[5,72,16,32]{1,3,2,0:T(8,128)S(1)}, f32[5,72,16,32]{1,3,2,0:T(8,128)}, u32[]{:S(2)}) copy-start(f32[5,72,16,32]{1,3,2,0:T(8,128)} %param.9) | copy-start | bytes 2211844
  8.6 25.6 %all-to-all-start.1 = ((f32[16,128,128]{2,1,0:T(8,128)}), f32[16,128,128]{2,1,0:T(8,128)S(1)}, u32[]{:S(2)}, u32[]{:S(2)}) async-start(f32[16,128,128]{2,1,0:T(8,128)} %bitcast.1.back_ref), calls=%async_computation.1 | async-start | bytes 2097152 | tf_op jit(solution)/shard_map/all_to_all | solution.py:345
  14.5 17.6 %collective-permute-start = (f32[6,2,32,72]{3,2,1,0:T(8,128)S(1)}, f32[6,2,32,72]{3,2,1,0:T(8,128)S(1)}, u32[]{:S(2)}, u32[]{:S(2)}) collective-permute-start(f32[6,2,32,72]{3,2,1,0:T(8,128)S(1)} %pad_maximum_fusion), channel_id=1, source_target_pairs={{0,1},{1,2},{2,3},{3,4},{4,5},{5,6},{6,7},{8,9},{9,10},{10,11},{11... | collective-permute-start | bytes 331784 | tf_op jit(solution)/shard_map/ppermute | solution.py:326
  17.9 14.2 %collective-permute-start.1 = (f32[6,2,32,72]{3,2,1,0:T(8,128)S(1)}, f32[6,2,32,72]{3,2,1,0:T(8,128)S(1)}, u32[]{:S(2)}, u32[]{:S(2)}) collective-permute-start(f32[6,2,32,72]{3,2,1,0:T(8,128)S(1)} %pad_maximum_fusion.1), channel_id=1, source_target_pairs={{1,0},{2,1},{3,2},{4,3},{5,4},{6,5},{7,6},{9,8},{10,9},{11,10},{12... | collective-permute-start | bytes 331784 | tf_op jit(solution)/shard_map/ppermute | solution.py:327
  33.1 1.1 copy-start
  34.2 13.8 %copy-start.12 = (f32[512]{0:T(512)S(1)}, f32[512]{0:T(512)}, u32[]{:S(2)}) copy-start(f32[512]{0:T(512)} %constant.38.clone) | copy-start | bytes 6148
  34.2 39.3 %all-to-all-start = ((f32[16,160,128]{2,1,0:T(8,128)}), f32[16,160,128]{2,1,0:T(8,128)S(1)}, u32[]{:S(2)}, u32[]{:S(2)}) async-start(f32[16,160,128]{2,1,0:T(8,128)} %bitcast.9), calls=%async_computation | async-start | bytes 2621440 | tf_op jit(solution)/shard_map/all_to_all | solution.py:360
  39.2 16.9 %collective-permute-start.3 = (f32[16,32,128]{2,1,0:T(8,128)S(1)}, f32[16,32,128]{2,1,0:T(8,128)S(1)}, u32[]{:S(2)}, u32[]{:S(2)}) collective-permute-start(f32[16,32,128]{2,1,0:T(8,128)S(1)} %get-tuple-element.11), channel_id=1, source_target_pairs={{1,0},{2,1},{3,2},{4,3},{5,4},{6,5},{7,6},{9,8},{10,9},{11,10},{12... | collective-permute-start | bytes 786440 | tf_op jit(solution)/shard_map/ppermute | solution.py:359
  46.0 14.6 %collective-permute-start.2 = (f32[16,32,128]{2,1,0:T(8,128)S(1)}, f32[16,32,128]{2,1,0:T(8,128)S(1)}, u32[]{:S(2)}, u32[]{:S(2)}) collective-permute-start(f32[16,32,128]{2,1,0:T(8,128)S(1)} %get-tuple-element.12), channel_id=1, source_target_pairs={{0,1},{1,2},{2,3},{3,4},{4,5},{5,6},{6,7},{8,9},{9,10},{10,11},{11... | collective-permute-start | bytes 786440 | tf_op jit(solution)/shard_map/ppermute | solution.py:358
  71.1 1.1 copy-start.8
  72.3 1.2 copy-start.10
  73.5 1.4 %copy-start.9 = (f32[24,32,512]{2,1,0:T(8,128)S(1)}, f32[24,32,512]{2,1,0:T(8,128)}, u32[]{:S(2)}) copy-start(f32[24,32,512]{2,1,0:T(8,128)} %copy-done.8) | copy-start | bytes 4718596
  74.9 1.4 %copy-start.11 = (f32[24,32,512]{2,1,0:T(8,128)S(1)}, f32[24,32,512]{2,1,0:T(8,128)}, u32[]{:S(2)}) copy-start(f32[24,32,512]{2,1,0:T(8,128)} %copy-done.10) | copy-start | bytes 4718596
  87.4 19.4 %copy-start.6 = (bf16[256,512]{1,0:T(8,128)(2,1)S(1)}, bf16[256,512]{1,0:T(8,128)(2,1)}, u32[]{:S(2)}) copy-start(bf16[256,512]{1,0:T(8,128)(2,1)} %constant.40.clone.spread_ref) | copy-start | bytes 786436
  106.8 2.7 %copy-start.4 = (bf16[5,72,64,128]{3,2,1,0:T(8,128)(2,1)S(1)}, bf16[5,72,64,128]{3,2,1,0:T(8,128)(2,1)}, u32[]{:S(2)}) copy-start(bf16[5,72,64,128]{3,2,1,0:T(8,128)(2,1)} %traj_ref.3) | copy-start | bytes 17694724

commit v2 on v1

--- a/solution.py
+++ b/solution.py
@@ -21,6 +21,8 @@
 WIDE = 16
 HALO = 4
 BAND = ROWS + 2 * HALO
+SLOTS = 3
+KEPT = 448
 
 diffusion = 0.2
 advection_scale = 0.3
@@ -46,19 +48,11 @@
 def stacked(matrix):
     high = matrix.astype(ml_dtypes.bfloat16)
     low = (matrix - high.astype(np.float64)).astype(ml_dtypes.bfloat16)
-    return np.concatenate([high, high, low], axis=0)
+    return np.concatenate([high, low], axis=0)
 
 
 EVEN, ODD, WAVES = harmonics()
 BASIS = np.stack([stacked(EVEN), stacked(ODD), stacked(EVEN.T), stacked(ODD.T)])
-
-
-def pooling():
-    fine = np.arange(4 * COLS)
-    matrix = np.zeros((4, 4 * COLS, 4 * COLS), np.float32)
-    for part in range(4):
-        matrix[part, fine, part * COLS + fine // 4] = 1.0 / 16
-    return matrix.reshape(4 * 4 * COLS, 4 * COLS)
 
 
 def spreading():
@@ -87,11 +81,26 @@
                 send_ref[pl.ds(group * GROUP + field * SHARE + level, WIDE, stride=size), :] = value
 
 
-def pack_state(back_ref, traj_ref, pool_ref, send_ref, turned_ref, fine_ref):
+def pooling():
+    fine = lax.broadcasted_iota(jnp.int32, (16 * COLS, 4 * COLS), 0)
+    lane = lax.broadcasted_iota(jnp.int32, (16 * COLS, 4 * COLS), 1)
+    meets = (fine // (4 * COLS) == lane // COLS) & ((fine % (4 * COLS)) // 4 == lane % COLS)
+    return jnp.where(meets, 1.0 / 16, 0.0)
+
+
+def pack_state(back_in, traj_in, send_ref, turned_ref, fine_ref, back_ref, wind_ref, sems):
+    copies = [pltpu.make_async_copy(traj_in.at[0], wind_ref, sems.at[FIELDS])]
+    copies += [pltpu.make_async_copy(back_in.at[f], back_ref.at[f], sems.at[f]) for f in range(FIELDS)]
+    for copy in copies:
+        copy.start()
     spare = jnp.zeros((8, 128), jnp.float32)
-    fine_ref[...] = traj_ref[0].astype(jnp.float32).reshape(LEVELS * 64, 128)
+    pool = pooling()
+    copies[0].wait()
+    fine_ref[...] = wind_ref[...].astype(jnp.float32).reshape(LEVELS * 64, 128)
     for group in range(4):
         for field in range(FIELDS):
+            if group == 0:
+                copies[1 + field].wait()
             block = back_ref[field, 4 * group : 4 * group + 4].reshape(4 * COLS, LEVELS)
             turned_ref[field * 4 + group, 0:LEVELS, :] = block.T
             turned_ref[field * 4 + group, LEVELS:, :] = spare
@@ -104,7 +113,7 @@
             parts.append(total)
         mean = jnp.dot(
             jnp.concatenate(parts, axis=1),
-            pool_ref[...],
+            pool,
             precision=lax.Precision.HIGHEST,
             preferred_element_type=jnp.float32,
         )
@@ -161,11 +170,11 @@
 
 
 def product(ref, count, basis_ref, which):
-    rows = slice(0, count)
-    total = jnp.dot(ref[rows, :], basis_ref[which, 0:CYCLE], preferred_element_type=jnp.float32)
-    return total + jnp.dot(
-        ref[rows, 0:HALF], basis_ref[which, CYCLE:], preferred_element_type=jnp.float32
-    )
+    high, low = ref[0:count, 0:HALF], ref[0:count, HALF:CYCLE]
+    basis_high, basis_low = basis_ref[which, 0:HALF], basis_ref[which, HALF:CYCLE]
+    total = jnp.dot(high, basis_high, preferred_element_type=jnp.float32)
+    total = total + jnp.dot(low, basis_high, preferred_element_type=jnp.float32)
+    return total + jnp.dot(high, basis_low, preferred_element_type=jnp.float32)
 
 
 def filtered(even_ref, odd_ref, basis_ref, resp_ref, first, rows, out_ref):
@@ -186,7 +195,7 @@
         out_ref[0:rows, SHARE * field : SHARE * field + SHARE, :] = source_ref[0:rows, PLANES : PLANES + SHARE, :]
 
 
-def tangent(recv_ref, before_ref, after_ref, resp_ref, basis_ref, state_ref, drift_ref, row_ref, even_ref, odd_ref):
+def tangent(recv_ref, before_ref, after_ref, resp_ref, basis_ref, kept_out, row_ref, state_ref, drift_ref, even_ref, odd_ref, sems):
     for group in range(6):
         def load(source):
             if group == 0:
@@ -201,6 +210,8 @@
         unpack_rows(load, store)
     drift_ref[:, GROUP - 8 :, :] = jnp.zeros((BAND, 8, CYCLE), jnp.float32)
     expand(row_ref, BAND, drift_ref)
+    drift_copy = pltpu.make_async_copy(drift_ref, kept_out.at[BAND : 2 * BAND], sems.at[0])
+    drift_copy.start()
 
     for step in range(2):
         first, last = 1 + step, BAND - 1 - step
@@ -215,11 +226,21 @@
             fold_store(even_ref, odd_ref, index - first, moved)
             return carry
 
-        lax.fori_loop(first, last, body, 0)
+        lax.fori_loop(first, last, body, 0, unroll=4)
         filtered(even_ref, odd_ref, basis_ref, resp_ref, first, last - first, state_ref)
-
-
-def adjoint(recv_ref, state_ref, drift_ref, resp_ref, basis_ref, send_ref, row_ref, field_ref, weight_ref, even_ref, odd_ref):
+    state_copy = pltpu.make_async_copy(state_ref, kept_out.at[0:BAND], sems.at[1])
+    state_copy.start()
+    drift_copy.wait()
+    state_copy.wait()
+
+
+def adjoint(recv_ref, kept_in, traj_in, resp_ref, basis_ref, send_ref, held_ref, row_ref, field_ref, weight_ref, state_ref, drift_ref, even_ref, odd_ref, sems):
+    held_copy = pltpu.make_async_copy(traj_in, held_ref, sems.at[2])
+    state_copy = pltpu.make_async_copy(kept_in.at[0:BAND], state_ref, sems.at[0])
+    state_copy.start()
+    drift_copy = pltpu.make_async_copy(kept_in.at[BAND : 2 * BAND], drift_ref, sems.at[1])
+    drift_copy.start()
+    held_copy.start()
     for group in range(5):
         def load(source):
             return recv_ref[source, GROUP * group : GROUP * group + GROUP, :]
@@ -236,11 +257,14 @@
     for field in range(FIELDS):
         weight_ref[2:22, SHARE * field : SHARE * field + SHARE, :] = row_ref[2:22, PLANES : PLANES + SHARE, :]
 
+    state_copy.wait()
+    drift_copy.wait()
+
     def depart(index, carry):
         fold_store(even_ref, odd_ref, index - 2, weight_ref[index] * (state_ref[index] - row_ref[index]))
         return carry
 
-    lax.fori_loop(2, 22, depart, 0)
+    lax.fori_loop(2, 22, depart, 0, unroll=4)
     for step in range(2):
         first, last = 2 + step, BAND - 2 - step
         filtered(even_ref, odd_ref, basis_ref, resp_ref, first, last - first, field_ref)
@@ -258,7 +282,7 @@
                 row_ref[index] = moved
             return carry
 
-        lax.fori_loop(first + 1, last - 1, body, 0)
+        lax.fori_loop(first + 1, last - 1, body, 0, unroll=4)
     block = lane_block()
     for group in range(4):
         for quarter in range(4):
@@ -269,32 +293,63 @@
                 for row in range(1, 4):
                     value = jnp.where(block == row, turn(pieces[row], row - source), value)
                 send_ref[4 * quarter + source, PLANES * group : PLANES * group + PLANES, :] = value[:PLANES]
-
-
-def prolong(back_ref, cost_ref, traj_ref, spread_ref, out_ref, wide_ref):
-    for group in range(4):
-        change = (
-            back_ref[0, GROUP * group : GROUP * group + PLANES, :]
-            - cost_ref[0, PLANES * group : PLANES * group + PLANES, :]
+    held_copy.wait()
+
+
+def prolong(back_ref, cost_ref, traj_ref, spread_ref, out_ref, wide_ref, slot_ref, sems):
+    whole, rest = LEVELS // SHARE, LEVELS % SHARE
+
+    upper = lax.broadcasted_iota(jnp.int32, (8, 128), 0) < 4
+
+    def fill(owner, slot, levels):
+        for group in range(4):
+            change = (
+                back_ref[owner, GROUP * group : GROUP * group + PLANES, :]
+                - cost_ref[owner, PLANES * group : PLANES * group + PLANES, :]
+            )
+            high = change.astype(jnp.bfloat16)
+            low = (change - high.astype(jnp.float32)).astype(jnp.bfloat16)
+            spread = jnp.dot(
+                jnp.concatenate([high, low], axis=1), spread_ref[...], preferred_element_type=jnp.float32
+            )
+            for part in range(4):
+                wide_ref[4 * group + part, 0:PLANES, :] = spread[:, 128 * part : 128 * part + 128]
+        for field in range(FIELDS):
+            for level in range(levels):
+                plane = field * SHARE + level
+                rows = []
+                for pair in range(8):
+                    above = jnp.broadcast_to(wide_ref[2 * pair, plane : plane + 1, :], (8, 128))
+                    below = jnp.broadcast_to(wide_ref[2 * pair + 1, plane : plane + 1, :], (8, 128))
+                    rows.append(jnp.where(upper, above, below))
+                fine = jnp.concatenate(rows, axis=0)
+                first_guess = traj_ref[field, SHARE * owner + level].astype(jnp.float32)
+                slot_ref[slot, field, level] = (first_guess + fine).astype(jnp.bfloat16)
+
+    def copy(owner, slot, levels=SHARE):
+        return pltpu.make_async_copy(
+            slot_ref.at[slot, :, 0:levels], out_ref.at[:, pl.ds(SHARE * owner, levels)], sems.at[slot]
         )
-        high = change.astype(jnp.bfloat16)
-        low = (change - high.astype(jnp.float32)).astype(jnp.bfloat16)
-        spread = jnp.dot(
-            jnp.concatenate([high, low], axis=1), spread_ref[...], preferred_element_type=jnp.float32
-        )
-        for part in range(4):
-            wide_ref[4 * group + part, 0:PLANES, :] = spread[:, 128 * part : 128 * part + 128]
-    upper = lax.broadcasted_iota(jnp.int32, (8, 128), 0) < 4
-    for field in range(FIELDS):
-        for level in range(SHARE):
-            plane = field * SHARE + level
-            rows = []
-            for pair in range(8):
-                above = jnp.broadcast_to(wide_ref[2 * pair, plane : plane + 1, :], (8, 128))
-                below = jnp.broadcast_to(wide_ref[2 * pair + 1, plane : plane + 1, :], (8, 128))
-                rows.append(jnp.where(upper, above, below))
-            fine = jnp.concatenate(rows, axis=0)
-            out_ref[field, level] = (traj_ref[field, level].astype(jnp.float32) + fine).astype(jnp.bfloat16)
+
+    for owner in range(SLOTS):
+        fill(owner, owner, SHARE)
+        copy(owner, owner).start()
+
+    def body(owner, carry):
+        slot = lax.rem(owner, SLOTS)
+        copy(owner - SLOTS, slot).wait()
+        fill(owner, slot, SHARE)
+        copy(owner, slot).start()
+        return carry
+
+    lax.fori_loop(SLOTS, whole, body, 0)
+    slot = whole % SLOTS
+    copy(whole - SLOTS, slot).wait()
+    fill(whole, slot, rest)
+    copy(whole, slot, rest).start()
+    for owner in range(whole - SLOTS + 1, whole):
+        copy(owner, owner % SLOTS).wait()
+    copy(whole, slot, rest).wait()
 
 
 def response_rows(narrow_index):
@@ -327,20 +382,22 @@
     after = lax.ppermute(edge(slice(0, 2)), "narrow", backward)
 
     full = pl.BlockSpec(memory_space=pltpu.VMEM)
+    away = pl.BlockSpec(memory_space=pltpu.HBM)
     send_state = pl.pallas_call(
         pack_state,
-        grid=(1,),
-        in_specs=[
-            pl.BlockSpec((FIELDS, ROWS, COLS, LEVELS), lambda i: (0, 0, 0, 0)),
-            pl.BlockSpec((1, LEVELS, 64, 128), lambda i: (0, 0, 0, 0)),
-            pl.BlockSpec((512, 128), lambda i: (0, 0)),
+        in_specs=[away] * 2,
+        out_specs=full,
+        out_shape=jax.ShapeDtypeStruct((WIDE * 4 * GROUP, 128), f32),
+        scratch_shapes=[
+            pltpu.VMEM((24, 80, 128), f32),
+            pltpu.VMEM((LEVELS * 64, 128), f32),
+            pltpu.VMEM((FIELDS, ROWS, COLS, LEVELS), f32),
+            pltpu.VMEM((LEVELS, 64, 128), jnp.bfloat16),
+            pltpu.SemaphoreType.DMA((FIELDS + 1,)),
         ],
-        out_specs=pl.BlockSpec((WIDE * 4 * GROUP, 128), lambda i: (0, 0)),
-        out_shape=jax.ShapeDtypeStruct((WIDE * 4 * GROUP, 128), f32),
-        scratch_shapes=[pltpu.VMEM((24, 80, 128), f32), pltpu.VMEM((LEVELS * 64, 128), f32)],
-        compiler_params=params(40),
+        compiler_params=params(60),
         cost_estimate=estimate(3),
-    )(back, trajectory, jnp.asarray(pooling()))
+    )(back, trajectory)
     send_state = send_state.reshape(WIDE, 4 * GROUP, 128)
     held_state = lax.all_to_all(send_state, "wide", split_axis=0, concat_axis=0, tiled=True)
 
@@ -350,7 +407,7 @@
         out_specs=full,
         out_shape=jax.ShapeDtypeStruct((WIDE * 5 * GROUP, 128), f32),
         scratch_shapes=[pltpu.VMEM((30, 80, 128), f32)],
-        compiler_params=params(40),
+        compiler_params=params(16),
         cost_estimate=estimate(3),
     )(innov, weight, before, after)
     send_depart = send_depart.reshape(WIDE, 5 * GROUP, 128)
@@ -361,42 +418,42 @@
 
     rows_shape = (BAND, GROUP, CYCLE)
     folded = pltpu.VMEM(((BAND - 2) * GROUP, CYCLE), jnp.bfloat16)
-    state, drift = pl.pallas_call(
+    kept = pl.pallas_call(
         tangent,
         in_specs=[full] * 5,
-        out_specs=[full] * 2,
-        out_shape=[jax.ShapeDtypeStruct(rows_shape, f32)] * 2,
-        scratch_shapes=[pltpu.VMEM(rows_shape, f32), folded, folded],
-        compiler_params=params(48),
+        out_specs=away,
+        out_shape=jax.ShapeDtypeStruct((KEPT, GROUP, CYCLE), f32),
+        scratch_shapes=[pltpu.VMEM(rows_shape, f32)] * 3 + [folded, folded, pltpu.SemaphoreType.DMA((2,))],
+        compiler_params=params(40),
         cost_estimate=estimate(5),
     )(held_state, north, south, response, basis)
-    send_cost = pl.pallas_call(
+    send_cost, held = pl.pallas_call(
         adjoint,
-        in_specs=[full] * 5,
-        out_specs=full,
-        out_shape=jax.ShapeDtypeStruct((WIDE, 4 * PLANES, 128), f32),
-        scratch_shapes=[pltpu.VMEM(rows_shape, f32)] * 3 + [folded, folded],
-        compiler_params=params(48),
+        in_specs=[full, away, away, full, full],
+        out_specs=[full, full],
+        out_shape=[
+            jax.ShapeDtypeStruct((WIDE, 4 * PLANES, 128), f32),
+            jax.ShapeDtypeStruct(trajectory.shape, jnp.bfloat16),
+        ],
+        scratch_shapes=[pltpu.VMEM(rows_shape, f32)] * 5 + [folded, folded, pltpu.SemaphoreType.DMA((3,))],
+        compiler_params=params(40),
         cost_estimate=estimate(5),
-    )(held_depart, state, drift, response, basis)
+    )(held_depart, kept, trajectory, response, basis)
     costate = lax.all_to_all(send_cost, "wide", split_axis=0, concat_axis=0, tiled=True)
 
-    fine_block = pl.BlockSpec((FIELDS, SHARE, 64, 128), lambda i: (0, i, 0, 0))
     return pl.pallas_call(
         prolong,
-        grid=(pl.cdiv(LEVELS, SHARE),),
-        in_specs=[
-            pl.BlockSpec((1, 4 * GROUP, 128), lambda i: (i, 0, 0)),
-            pl.BlockSpec((1, 4 * PLANES, 128), lambda i: (i, 0, 0)),
-            fine_block,
-            pl.BlockSpec((256, 512), lambda i: (0, 0)),
+        in_specs=[full] * 4,
+        out_specs=away,
+        out_shape=jax.ShapeDtypeStruct(trajectory.shape, jnp.bfloat16),
+        scratch_shapes=[
+            pltpu.VMEM((16, GROUP, 128), f32),
+            pltpu.VMEM((SLOTS, FIELDS, SHARE, 64, 128), jnp.bfloat16),
+            pltpu.SemaphoreType.DMA((SLOTS,)),
         ],
-        out_specs=fine_block,
-        out_shape=jax.ShapeDtypeStruct(trajectory.shape, jnp.bfloat16),
-        scratch_shapes=[pltpu.VMEM((16, GROUP, 128), f32)],
-        compiler_params=params(32),
+        compiler_params=params(24),
         cost_estimate=estimate(5),
-    )(send_state, costate, trajectory, jnp.asarray(spreading()))
+    )(send_state, costate, held, jnp.asarray(spreading()))
 
 
 def solution(mesh):

time: 123 us -> 102 us (0.83)
  local copies, waits for them, and re-layouts: 13.9 us -> 1.15 us
  Pallas kernels: 37.4 us -> 29.7 us
    unnamed x26 -> x14, local copies, waits for them, and re-layouts: 13.8 us -> 1.08 us
    pallas_call x4, Pallas kernels: 36.4 us -> 28.8 us  [the longest x1 9.63 us: shards(): pl.pallas_call(adjoint, in_specs=[full, away, away, full, full], out_spec...]
  transfers between devices with their start and end apart: 6 -> 6, of which waited for: 3 -> 3; matrix products, arithmetic and copies ran while one was open for 0% -> 0% of each run, Pallas kernels for 10% -> 9%
where the time goes in v2:
time: 102 us; the launch traced here: 100 us
  Pallas kernels  29.7 us (29%)
  starting transfers between devices  29.1 us (29%)
  waiting for transfers between devices  20.4 us (20%)
  blocking collectives  19.4 us (19%)
  local copies, waits for them, and re-layouts  1.15 us (1%)
    all_to_all x1, blocking collectives, shards(): lax.all_to_all(send_cost, 'wide', split_axis=0, concat_axis=0, tiled=True)  19.4 us
    pallas_call x1, Pallas kernels, shards(): pl.pallas_call(adjoint, in_specs=[full, away, away, full, full], out_spec...  9.63 us
    ppermute x1, waiting for transfers between devices, shards(): before = lax.ppermute(edge(slice(14, 16)), 'narrow', onward)  8.13 us
    ppermute x1, waiting for transfers between devices, shards(): south = lax.ppermute(held_state[:, :GROUP], 'narrow', backward)  7.83 us
    pallas_call x1, Pallas kernels, shards(): pl.pallas_call(tangent, in_specs=[full] * 5, out_specs=away, out_shape=ja...  7.78 us
    ppermute x1, starting transfers between devices, shards(): south = lax.ppermute(held_state[:, :GROUP], 'narrow', backward)  6.78 us
    ppermute x1, starting transfers between devices, shards(): after = lax.ppermute(edge(slice(0, 2)), 'narrow', backward)  6.06 us
    pallas_call x1, Pallas kernels, shards(): pl.pallas_call(prolong, in_specs=[full] * 4, out_specs=away, out_shape=ja...  6.04 us
  transfers between devices with their start and end apart: 6, of which 3 were waited for; matrix products, arithmetic and copies ran while one was open for 0% of the time, Pallas kernels for 9%

profile of v2, /device:TPU:64, one launch (start us, length us, event | category | flops | bytes accessed | tf_op | source)
XLA Modules:
  0.0 100.4 jit_solution(8868530833734936246)
XLA Ops:
  0.0 5.3 %shard_map.73 = f32[2048,128]{1,0:T(8,128)} custom-call(f32[5,16,32,72]{3,2,1,0:T(8,128)} %bitcast.16, bf16[5,72,64,128]{3,2,1,0:T(8,128)(2,1)} %traj_in.3), custom_call_target="tpu_custom_call" | custom-call | flops 3000000000 | bytes 3000000 | tf_op jit(solution)/shard_map/pallas_call | solution.py:386
  5.3 0.0 copy-start.4
  5.3 0.0 copy-start.3
  5.4 5.8 %all-to-all-start.1 = ((f32[16,128,128]{2,1,0:T(8,128)}), f32[16,128,128]{2,1,0:T(8,128)S(1)}, u32[]{:S(2)}, u32[]{:S(2)}) async-start(f32[16,128,128]{2,1,0:T(8,128)} %bitcast.10), calls=%async_computation.1 | async-start | bytes 2097152 | tf_op jit(solution)/shard_map/all_to_all | solution.py:402
  11.1 0.0 copy-done.4
  11.2 0.0 copy-done.3
  11.2 3.4 %collective-permute-start = (f32[6,2,32,72]{3,2,1,0:T(8,128)S(1)}, f32[6,2,32,72]{3,2,1,0:T(8,128)S(1)}, u32[]{:S(2)}, u32[]{:S(2)}) collective-permute-start(f32[6,2,32,72]{3,2,1,0:T(8,128)S(1)} %pad_maximum_fusion), channel_id=1, source_target_pairs={{0,1},{1,2},{2,3},{3,4},{4,5},{5,6},{6,7},{8,9},{9,10},{10,11},{11... | collective-permute-start | bytes 331784 | tf_op jit(solution)/shard_map/ppermute | solution.py:381
  14.7 6.1 %collective-permute-start.1 = (f32[6,2,32,72]{3,2,1,0:T(8,128)S(1)}, f32[6,2,32,72]{3,2,1,0:T(8,128)S(1)}, u32[]{:S(2)}, u32[]{:S(2)}) collective-permute-start(f32[6,2,32,72]{3,2,1,0:T(8,128)S(1)} %pad_maximum_fusion.1), channel_id=1, source_target_pairs={{1,0},{2,1},{3,2},{4,3},{5,4},{6,5},{7,6},{9,8},{10,9},{11,10},{12... | collective-permute-start | bytes 331784 | tf_op jit(solution)/shard_map/ppermute | solution.py:382
  20.7 8.1 %collective-permute-done.before_ref = f32[6,2,32,72]{3,2,1,0:T(8,128)S(1)} collective-permute-done((f32[6,2,32,72]{3,2,1,0:T(8,128)S(1)}, f32[6,2,32,72]{3,2,1,0:T(8,128)S(1)}, u32[]{:S(2)}, u32[]{:S(2)}) %collective-permute-start) | collective-permute-done | bytes 110624 | tf_op jit(solution)/shard_map/ppermute | solution.py:381
  28.9 0.0 collective-permute-done.1.after_ref
  28.9 1.0 shard_map.74
  29.9 0.0 copy-start.1
  29.9 1.0 %copy-done.1 = f32[2560,128]{1,0:T(8,128)} copy-done((f32[2560,128]{1,0:T(8,128)}, f32[2560,128]{1,0:T(8,128)S(1)}, u32[]{:S(2)}) %copy-start.1) | copy-done | bytes 1310744
  30.9 0.0 all-to-all-done.1.recv_ref
  30.9 0.0 copy-start.6
  30.9 0.0 copy-start
  30.9 5.0 %all-to-all-start = ((f32[16,160,128]{2,1,0:T(8,128)}), f32[16,160,128]{2,1,0:T(8,128)S(1)}, u32[]{:S(2)}, u32[]{:S(2)}) async-start(f32[16,160,128]{2,1,0:T(8,128)} %bitcast.9), calls=%async_computation | async-start | bytes 2621440 | tf_op jit(solution)/shard_map/all_to_all | solution.py:417
  35.9 6.8 %collective-permute-start.3 = (f32[16,32,128]{2,1,0:T(8,128)S(1)}, f32[16,32,128]{2,1,0:T(8,128)S(1)}, u32[]{:S(2)}, u32[]{:S(2)}) collective-permute-start(f32[16,32,128]{2,1,0:T(8,128)S(1)} %get-tuple-element.11), channel_id=1, source_target_pairs={{1,0},{2,1},{3,2},{4,3},{5,4},{6,5},{7,6},{9,8},{10,9},{11,10},{12... | collective-permute-start | bytes 786440 | tf_op jit(solution)/shard_map/ppermute | solution.py:416
  42.7 2.1 %collective-permute-start.2 = (f32[16,32,128]{2,1,0:T(8,128)S(1)}, f32[16,32,128]{2,1,0:T(8,128)S(1)}, u32[]{:S(2)}, u32[]{:S(2)}) collective-permute-start(f32[16,32,128]{2,1,0:T(8,128)S(1)} %get-tuple-element.12), channel_id=1, source_target_pairs={{0,1},{1,2},{2,3},{3,4},{4,5},{5,6},{6,7},{8,9},{9,10},{10,11},{11... | collective-permute-start | bytes 786440 | tf_op jit(solution)/shard_map/ppermute | solution.py:415
  44.9 0.0 copy-done.6
  44.9 0.2 broadcast_select_fusion.resp_ref
  45.1 7.8 %collective-permute-done.3.after_ref = f32[16,32,128]{2,1,0:T(8,128)S(1)} collective-permute-done((f32[16,32,128]{2,1,0:T(8,128)S(1)}, f32[16,32,128]{2,1,0:T(8,128)S(1)}, u32[]{:S(2)}, u32[]{:S(2)}) %collective-permute-start.3) | collective-permute-done | bytes 262176 | tf_op jit(solution)/shard_map/ppermute | solution.py:416
  52.9 4.4 %collective-permute-done.2.before_ref = f32[16,32,128]{2,1,0:T(8,128)S(1)} collective-permute-done((f32[16,32,128]{2,1,0:T(8,128)S(1)}, f32[16,32,128]{2,1,0:T(8,128)S(1)}, u32[]{:S(2)}, u32[]{:S(2)}) %collective-permute-start.2) | collective-permute-done | bytes 262176 | tf_op jit(solution)/shard_map/ppermute | solution.py:415
  57.3 0.0 copy-done
  57.3 7.8 %shard_map.75.kept_in = f32[448,32,512]{2,1,0:T(8,128)} custom-call(f32[16,128,128]{2,1,0:T(8,128)S(1)} %all-to-all-done.1.recv_ref, f32[16,32,128]{2,1,0:T(8,128)S(1)} %collective-permute-done.2.before_ref, f32[16,32,128]{2,1,0:T(8,128)S(1)} %collective-permute-done.3.after_ref, f32[24,1,512]{2,1,0:T(1,128)S(1)} %broadcast_select_fusion.resp_ref, ...), custom_call_target="tpu_custom_call" | custom-call | flops 5000000000 | bytes 5000000 | tf_op jit(solution)/shard_map/pallas_call | solution.py:421
  65.1 0.0 all-to-all-done.recv_ref
  65.1 9.6 %shard_map.76 = (f32[16,100,128]{2,1,0:T(8,128)S(1)}, bf16[5,72,64,128]{3,2,1,0:T(8,128)(2,1)S(1)}) custom-call(f32[16,160,128]{2,1,0:T(8,128)S(1)} %all-to-all-done.recv_ref, f32[448,32,512]{2,1,0:T(8,128)} %shard_map.75.kept_in, bf16[5,72,64,128]{3,2,1,0:T(8,128)(2,1)} %traj_in.3, f32[24,1,512]{2,1,0:T(1,128)S(1)} %broadcast_select_fusion.resp_ref, ...), custom_call_target="tpu_custom_call" | custom-call | flops 5000000000 | bytes 5000000 | tf_op jit(solution)/shard_map/pallas_call | solution.py:430
  74.7 0.0 copy-start.2
  74.8 0.0 copy-start.5
  74.8 19.4 %all_to_all.15.cost_ref = f32[16,100,128]{2,1,0:T(8,128)S(1)} all-to-all(f32[16,100,128]{2,1,0:T(8,128)S(1)} %get-tuple-element.7), channel_id=1, replica_groups=mesh['wide'=16,'narrow'=8] {'wide'}, dimensions={0} | all-to-all | bytes 1638400 | tf_op jit(solution)/shard_map/all_to_all | solution.py:442
  94.2 0.0 copy-done.2
  94.2 0.0 copy-done.5
  94.2 6.0 %shard_map.77 = bf16[5,72,64,128]{3,2,1,0:T(8,128)(2,1)} custom-call(f32[16,128,128]{2,1,0:T(8,128)S(1)} %bitcast.11, f32[16,100,128]{2,1,0:T(8,128)S(1)} %all_to_all.15.cost_ref, bf16[5,72,64,128]{3,2,1,0:T(8,128)(2,1)S(1)} %get-tuple-element.8.traj_ref, bf16[256,512]{1,0:T(8,128)(2,1)S(1)} %copy-done.5), custom_call_target="tpu_custom_call" | custom-call | flops 5000000000 | bytes 5000000 | tf_op jit(solution)/shard_map/pallas_call | solution.py:444
  (7 shorter events, 0.2 us)
Async XLA Ops:
  5.3 5.8 %copy-start.4 = (f32[72,16,32]{0,2,1:T(8,128)S(1)}, f32[72,16,32]{0,2,1:T(8,128)}, u32[]{:S(2)}) copy-start(f32[72,16,32]{0,2,1:T(8,128)} %param.10) | copy-start | bytes 442372
  5.3 5.8 %copy-start.3 = (f32[5,72,16,32]{1,3,2,0:T(8,128)S(1)}, f32[5,72,16,32]{1,3,2,0:T(8,128)}, u32[]{:S(2)}) copy-start(f32[5,72,16,32]{1,3,2,0:T(8,128)} %param.8) | copy-start | bytes 2211844
  5.4 25.6 %all-to-all-start.1 = ((f32[16,128,128]{2,1,0:T(8,128)}), f32[16,128,128]{2,1,0:T(8,128)S(1)}, u32[]{:S(2)}, u32[]{:S(2)}) async-start(f32[16,128,128]{2,1,0:T(8,128)} %bitcast.10), calls=%async_computation.1 | async-start | bytes 2097152 | tf_op jit(solution)/shard_map/all_to_all | solution.py:402
  11.2 17.6 %collective-permute-start = (f32[6,2,32,72]{3,2,1,0:T(8,128)S(1)}, f32[6,2,32,72]{3,2,1,0:T(8,128)S(1)}, u32[]{:S(2)}, u32[]{:S(2)}) collective-permute-start(f32[6,2,32,72]{3,2,1,0:T(8,128)S(1)} %pad_maximum_fusion), channel_id=1, source_target_pairs={{0,1},{1,2},{2,3},{3,4},{4,5},{5,6},{6,7},{8,9},{9,10},{10,11},{11... | collective-permute-start | bytes 331784 | tf_op jit(solution)/shard_map/ppermute | solution.py:381
  14.7 14.2 %collective-permute-start.1 = (f32[6,2,32,72]{3,2,1,0:T(8,128)S(1)}, f32[6,2,32,72]{3,2,1,0:T(8,128)S(1)}, u32[]{:S(2)}, u32[]{:S(2)}) collective-permute-start(f32[6,2,32,72]{3,2,1,0:T(8,128)S(1)} %pad_maximum_fusion.1), channel_id=1, source_target_pairs={{1,0},{2,1},{3,2},{4,3},{5,4},{6,5},{7,6},{9,8},{10,9},{11,10},{12... | collective-permute-start | bytes 331784 | tf_op jit(solution)/shard_map/ppermute | solution.py:382
  29.9 1.1 %copy-start.1 = (f32[2560,128]{1,0:T(8,128)}, f32[2560,128]{1,0:T(8,128)S(1)}, u32[]{:S(2)}) copy-start(f32[2560,128]{1,0:T(8,128)S(1)} %shard_map.74) | copy-start | bytes 3932164
  30.9 14.0 %copy-start.6 = (f32[512]{0:T(512)S(1)}, f32[512]{0:T(512)}, u32[]{:S(2)}) copy-start(f32[512]{0:T(512)} %constant.36.clone) | copy-start | bytes 6148
  30.9 26.4 %copy-start = (bf16[4,512,256]{2,1,0:T(8,128)(2,1)S(1)}, bf16[4,512,256]{2,1,0:T(8,128)(2,1)}, u32[]{:S(2)}) copy-start(bf16[4,512,256]{2,1,0:T(8,128)(2,1)} %constant.35.clone.basis_ref) | copy-start | bytes 3145732
  30.9 34.2 %all-to-all-start = ((f32[16,160,128]{2,1,0:T(8,128)}), f32[16,160,128]{2,1,0:T(8,128)S(1)}, u32[]{:S(2)}, u32[]{:S(2)}) async-start(f32[16,160,128]{2,1,0:T(8,128)} %bitcast.9), calls=%async_computation | async-start | bytes 2621440 | tf_op jit(solution)/shard_map/all_to_all | solution.py:417
  35.9 17.0 %collective-permute-start.3 = (f32[16,32,128]{2,1,0:T(8,128)S(1)}, f32[16,32,128]{2,1,0:T(8,128)S(1)}, u32[]{:S(2)}, u32[]{:S(2)}) collective-permute-start(f32[16,32,128]{2,1,0:T(8,128)S(1)} %get-tuple-element.11), channel_id=1, source_target_pairs={{1,0},{2,1},{3,2},{4,3},{5,4},{6,5},{7,6},{9,8},{10,9},{11,10},{12... | collective-permute-start | bytes 786440 | tf_op jit(solution)/shard_map/ppermute | solution.py:416
  42.7 14.6 %collective-permute-start.2 = (f32[16,32,128]{2,1,0:T(8,128)S(1)}, f32[16,32,128]{2,1,0:T(8,128)S(1)}, u32[]{:S(2)}, u32[]{:S(2)}) collective-permute-start(f32[16,32,128]{2,1,0:T(8,128)S(1)} %get-tuple-element.12), channel_id=1, source_target_pairs={{0,1},{1,2},{2,3},{3,4},{4,5},{5,6},{6,7},{8,9},{9,10},{10,11},{11... | collective-permute-start | bytes 786440 | tf_op jit(solution)/shard_map/ppermute | solution.py:415
  74.7 19.4 %copy-start.2 = (f32[2048,128]{1,0:T(8,128)S(1)}, f32[2048,128]{1,0:T(8,128)}, u32[]{:S(2)}) copy-start(f32[2048,128]{1,0:T(8,128)} %shard_map.73) | copy-start | bytes 3145732
  74.8 19.4 %copy-start.5 = (bf16[256,512]{1,0:T(8,128)(2,1)S(1)}, bf16[256,512]{1,0:T(8,128)(2,1)}, u32[]{:S(2)}) copy-start(bf16[256,512]{1,0:T(8,128)(2,1)} %constant.37.clone.spread_ref) | copy-start | bytes 786436

commit v3 on v2

--- a/solution.py
+++ b/solution.py
@@ -72,13 +72,17 @@
     return pl.CostEstimate(flops=int(micros * 1e9), bytes_accessed=int(micros * 1e6), transcendentals=0)
 
 
-def scatter_levels(turned_ref, send_ref, fields, groups):
+def scatter_levels(turned_ref, send_ref, fields, groups, flip):
     size = groups * GROUP
     for field in range(fields):
         for group in range(groups):
             for level in range(SHARE):
-                value = turned_ref[field * groups + group, pl.ds(level, WIDE, stride=SHARE), :]
-                send_ref[pl.ds(group * GROUP + field * SHARE + level, WIDE, stride=size), :] = value
+                for half in range(2):
+                    first = half * SHARE * WIDE // 2 + level
+                    value = turned_ref[field * groups + group, pl.ds(first, WIDE // 2, stride=SHARE), :]
+                    owner = (WIDE // 2) * (half + flip - 2 * half * flip)
+                    at = owner * size + group * GROUP + field * SHARE + level
+                    send_ref[pl.ds(at, WIDE // 2, stride=size), :] = value
 
 
 def pooling():
@@ -88,7 +92,7 @@
     return jnp.where(meets, 1.0 / 16, 0.0)
 
 
-def pack_state(back_in, traj_in, send_ref, turned_ref, fine_ref, back_ref, wind_ref, sems):
+def pack_state(place_ref, back_in, traj_in, send_ref, turned_ref, fine_ref, back_ref, wind_ref, sems):
     copies = [pltpu.make_async_copy(traj_in.at[0], wind_ref, sems.at[FIELDS])]
     copies += [pltpu.make_async_copy(back_in.at[f], back_ref.at[f], sems.at[f]) for f in range(FIELDS)]
     for copy in copies:
@@ -119,10 +123,10 @@
         )
         turned_ref[FIELDS * 4 + group, 0:LEVELS, :] = advection_scale * jnp.tanh(mean)
         turned_ref[FIELDS * 4 + group, LEVELS:, :] = spare
-    scatter_levels(turned_ref, send_ref, FIELDS + 1, 4)
-
-
-def pack_departures(innov_ref, weight_ref, before_ref, after_ref, send_ref, turned_ref):
+    scatter_levels(turned_ref, send_ref, FIELDS + 1, 4, place_ref[0])
+
+
+def pack_departures(place_ref, innov_ref, weight_ref, near_ref, far_ref, send_ref, turned_ref):
     spare = jnp.zeros((8, 128), jnp.float32)
     for field in range(FIELDS + 1):
         source = innov_ref.at[field] if field < FIELDS else weight_ref
@@ -130,10 +134,13 @@
             if group < 4:
                 block = source[4 * group : 4 * group + 4].reshape(4 * COLS, LEVELS)
             else:
-                block = jnp.concatenate([before_ref[field], after_ref[field]], axis=0).reshape(4 * COLS, LEVELS)
+                near, far = near_ref[field], far_ref[field]
+                before = jnp.where(place_ref[3] == 1, near, far)
+                after = jnp.where(place_ref[3] == 1, far, near)
+                block = jnp.concatenate([before, after], axis=0).reshape(4 * COLS, LEVELS)
             turned_ref[field * 5 + group, 0:LEVELS, :] = block.T
             turned_ref[field * 5 + group, LEVELS:, :] = spare
-    scatter_levels(turned_ref, send_ref, FIELDS + 1, 5)
+    scatter_levels(turned_ref, send_ref, FIELDS + 1, 5, place_ref[0])
 
 
 def lane_block():
@@ -153,7 +160,7 @@
             value = turn(pieces[0], -row)
             for source in range(1, 4):
                 value = jnp.where(block == source, turn(pieces[source], source - row), value)
-            store(row, slice(128 * quarter, 128 * quarter + 128), value)
+            store(row, quarter, value)
 
 
 def split_store(ref, at, value):
@@ -195,17 +202,17 @@
         out_ref[0:rows, SHARE * field : SHARE * field + SHARE, :] = source_ref[0:rows, PLANES : PLANES + SHARE, :]
 
 
-def tangent(recv_ref, before_ref, after_ref, resp_ref, basis_ref, kept_out, row_ref, state_ref, drift_ref, even_ref, odd_ref, sems):
+def tangent(place_ref, recv_ref, near_ref, far_ref, resp_ref, basis_ref, kept_out, row_ref, state_ref, drift_ref, even_ref, odd_ref, sems):
     for group in range(6):
         def load(source):
             if group == 0:
-                return before_ref[source]
+                return jnp.where(place_ref[3] == 1, near_ref[source], far_ref[source])
             if group == 5:
-                return after_ref[source]
+                return jnp.where(place_ref[3] == 1, far_ref[source], near_ref[source])
             return recv_ref[source, GROUP * (group - 1) : GROUP * group, :]
 
-        def store(row, lanes, value):
-            row_ref[4 * group + row, :, lanes] = value
+        def store(row, quarter, value):
+            row_ref[4 * group + row, :, 128 * quarter : 128 * quarter + 128] = value
 
         unpack_rows(load, store)
     drift_ref[:, GROUP - 8 :, :] = jnp.zeros((BAND, 8, CYCLE), jnp.float32)
@@ -234,7 +241,7 @@
     state_copy.wait()
 
 
-def adjoint(recv_ref, kept_in, traj_in, resp_ref, basis_ref, send_ref, held_ref, row_ref, field_ref, weight_ref, state_ref, drift_ref, even_ref, odd_ref, sems):
+def adjoint(place_ref, recv_ref, kept_in, traj_in, resp_ref, basis_ref, send_ref, held_ref, row_ref, field_ref, weight_ref, state_ref, drift_ref, even_ref, odd_ref, sems):
     held_copy = pltpu.make_async_copy(traj_in, held_ref, sems.at[2])
     state_copy = pltpu.make_async_copy(kept_in.at[0:BAND], state_ref, sems.at[0])
     state_copy.start()
@@ -245,12 +252,14 @@
         def load(source):
             return recv_ref[source, GROUP * group : GROUP * group + GROUP, :]
 
-        def store(row, lanes, value):
+        def store(row, quarter, value):
             if group < 4:
-                at = 4 * group + row + HALO
+                row_ref[4 * group + row + HALO, :, 128 * quarter : 128 * quarter + 128] = value
             else:
                 at = 2 + row if row < 2 else 18 + row
-            row_ref[at, :, lanes] = value
+                swapped = place_ref[1] if row < 2 else place_ref[2]
+                lanes = pl.multiple_of(128 * lax.rem(quarter + 2 * swapped, 4), 128)
+                row_ref[at, :, pl.ds(lanes, 128)] = value
 
         unpack_rows(load, store)
     weight_ref[:, GROUP - 8 :, :] = jnp.zeros((BAND, 8, CYCLE), jnp.float32)
@@ -296,16 +305,17 @@
     held_copy.wait()
 
 
-def prolong(back_ref, cost_ref, traj_ref, spread_ref, out_ref, wide_ref, slot_ref, sems):
+def prolong(place_ref, back_ref, cost_ref, traj_ref, spread_ref, out_ref, wide_ref, slot_ref, sems):
     whole, rest = LEVELS // SHARE, LEVELS % SHARE
 
     upper = lax.broadcasted_iota(jnp.int32, (8, 128), 0) < 4
 
     def fill(owner, slot, levels):
+        source = lax.rem(owner + (WIDE // 2) * place_ref[0], WIDE)
         for group in range(4):
             change = (
-                back_ref[owner, GROUP * group : GROUP * group + PLANES, :]
-                - cost_ref[owner, PLANES * group : PLANES * group + PLANES, :]
+                back_ref[source, GROUP * group : GROUP * group + PLANES, :]
+                - cost_ref[source, PLANES * group : PLANES * group + PLANES, :]
             )
             high = change.astype(jnp.bfloat16)
             low = (change - high.astype(jnp.float32)).astype(jnp.bfloat16)
@@ -367,8 +377,16 @@
     f32 = jnp.float32
     narrow_count = lax.axis_size("narrow")
     narrow_index = lax.axis_index("narrow")
-    onward = [(i, i + 1) for i in range(narrow_count - 1)]
-    backward = [(i + 1, i) for i in range(narrow_count - 1)]
+    middle = narrow_count // 2
+    near, far = [], []
+    for row in range(narrow_count - 1):
+        for lane in range(WIDE):
+            other = (lane + WIDE // 2) % WIDE if row == middle - 1 else lane
+            one, two = lane * narrow_count + row, other * narrow_count + row + 1
+            swaps = near if row % 2 == 0 else far
+            swaps += [(one, two), (two, one)]
+    odd = narrow_index % 2 == 1
+    place = jnp.stack([narrow_index >= middle, narrow_index == middle, narrow_index == middle - 1, odd]).astype(jnp.int32)
     innov = innovation.transpose(0, 2, 3, 1)
     back = background.transpose(0, 2, 3, 1)
     weight = obs_weight.transpose(1, 2, 0)
@@ -378,14 +396,16 @@
     def edge(rows):
         return jnp.concatenate([innov[:, rows], weight[None, rows]], axis=0)
 
-    before = lax.ppermute(edge(slice(14, 16)), "narrow", onward)
-    after = lax.ppermute(edge(slice(0, 2)), "narrow", backward)
+    first, last = edge(slice(0, 2)), edge(slice(14, 16))
+    edge_near = lax.ppermute(jnp.where(odd, first, last), ("wide", "narrow"), near)
+    edge_far = lax.ppermute(jnp.where(odd, last, first), ("wide", "narrow"), far)
 
     full = pl.BlockSpec(memory_space=pltpu.VMEM)
     away = pl.BlockSpec(memory_space=pltpu.HBM)
+    small = pl.BlockSpec(memory_space=pltpu.SMEM)
     send_state = pl.pallas_call(
         pack_state,
-        in_specs=[away] * 2,
+        in_specs=[small, away, away],
         out_specs=full,
         out_shape=jax.ShapeDtypeStruct((WIDE * 4 * GROUP, 128), f32),
         scratch_shapes=[
@@ -397,39 +417,40 @@
         ],
         compiler_params=params(60),
         cost_estimate=estimate(3),
-    )(back, trajectory)
+    )(place, back, trajectory)
     send_state = send_state.reshape(WIDE, 4 * GROUP, 128)
     held_state = lax.all_to_all(send_state, "wide", split_axis=0, concat_axis=0, tiled=True)
 
     send_depart = pl.pallas_call(
         pack_departures,
-        in_specs=[full] * 4,
+        in_specs=[small] + [full] * 4,
         out_specs=full,
         out_shape=jax.ShapeDtypeStruct((WIDE * 5 * GROUP, 128), f32),
         scratch_shapes=[pltpu.VMEM((30, 80, 128), f32)],
         compiler_params=params(16),
         cost_estimate=estimate(3),
-    )(innov, weight, before, after)
+    )(place, innov, weight, edge_near, edge_far)
     send_depart = send_depart.reshape(WIDE, 5 * GROUP, 128)
 
-    north = lax.ppermute(held_state[:, 3 * GROUP :], "narrow", onward)
-    south = lax.ppermute(held_state[:, :GROUP], "narrow", backward)
+    first, last = held_state[:, :GROUP], held_state[:, 3 * GROUP :]
+    rows_near = lax.ppermute(jnp.where(odd, first, last), ("wide", "narrow"), near)
+    rows_far = lax.ppermute(jnp.where(odd, last, first), ("wide", "narrow"), far)
     held_depart = lax.all_to_all(send_depart, "wide", split_axis=0, concat_axis=0, tiled=True)
 
     rows_shape = (BAND, GROUP, CYCLE)
     folded = pltpu.VMEM(((BAND - 2) * GROUP, CYCLE), jnp.bfloat16)
     kept = pl.pallas_call(
         tangent,
-        in_specs=[full] * 5,
+        in_specs=[small] + [full] * 5,
         out_specs=away,
         out_shape=jax.ShapeDtypeStruct((KEPT, GROUP, CYCLE), f32),
         scratch_shapes=[pltpu.VMEM(rows_shape, f32)] * 3 + [folded, folded, pltpu.SemaphoreType.DMA((2,))],
         compiler_params=params(40),
         cost_estimate=estimate(5),
-    )(held_state, north, south, response, basis)
+    )(place, held_state, rows_near, rows_far, response, basis)
     send_cost, held = pl.pallas_call(
         adjoint,
-        in_specs=[full, away, away, full, full],
+        in_specs=[small, full, away, away, full, full],
         out_specs=[full, full],
         out_shape=[
             jax.ShapeDtypeStruct((WIDE, 4 * PLANES, 128), f32),
@@ -438,12 +459,12 @@
         scratch_shapes=[pltpu.VMEM(rows_shape, f32)] * 5 + [folded, folded, pltpu.SemaphoreType.DMA((3,))],
         compiler_params=params(40),
         cost_estimate=estimate(5),
-    )(held_depart, kept, trajectory, response, basis)
+    )(place, held_depart, kept, trajectory, response, basis)
     costate = lax.all_to_all(send_cost, "wide", split_axis=0, concat_axis=0, tiled=True)
 
     return pl.pallas_call(
         prolong,
-        in_specs=[full] * 4,
+        in_specs=[small] + [full] * 4,
         out_specs=away,
         out_shape=jax.ShapeDtypeStruct(trajectory.shape, jnp.bfloat16),
         scratch_shapes=[
@@ -453,7 +474,7 @@
         ],
         compiler_params=params(24),
         cost_estimate=estimate(5),
-    )(send_state, costate, held, jnp.asarray(spreading()))
+    )(place, send_state, costate, held, jnp.asarray(spreading()))
 
 
 def solution(mesh):

time: 102 us -> 92.4 us (0.906); the launches traced: 100 us -> 92 us
  starting transfers between devices: 29.1 us -> 19.7 us
  waiting for transfers between devices: 20.4 us -> 16.5 us
  Pallas kernels: 29.7 us -> 32.6 us
  blocking collectives: 19.4 us -> 20.7 us
    ppermute x4, starting transfers between devices: 18.3 us -> 9.43 us  [the longest x2 8.25 us: shards(): lax.ppermute(jnp.where(odd, last, first), ('wide', 'narrow'), far)]
    ppermute x4, waiting for transfers between devices: 20.4 us -> 14.2 us  [the longest x2 14.2 us: shards(): lax.ppermute(jnp.where(odd, last, first), ('wide', 'narrow'), far)]
    pallas_call x5, Pallas kernels: 29.7 us -> 32.6 us  [the longest x1 9.74 us: shards(): pl.pallas_call(adjoint, in_specs=[small, full, away, away, full, full], o...]
    all_to_all x1, waiting for transfers between devices: 0.01 us -> 2.21 us  [shards(): lax.all_to_all(send_state, 'wide', split_axis=0, concat_axis=0, tiled=True)]
    all_to_all x1, blocking collectives: 19.4 us -> 20.7 us  [shards(): lax.all_to_all(send_cost, 'wide', split_axis=0, concat_axis=0, tiled=True)]
  transfers between devices with their start and end apart: 6 -> 6, of which waited for: 3 -> 3; matrix products, arithmetic and copies ran while one was open for 0% -> 0% of each run, Pallas kernels for 9% -> 11%
where the time goes in v3:
time: 92.4 us; the launch traced here: 92 us
  Pallas kernels  32.6 us (35%)
  blocking collectives  20.7 us (22%)
  starting transfers between devices  19.7 us (21%)
  waiting for transfers between devices  16.5 us (18%)
  local copies, waits for them, and re-layouts  1.12 us (1%)
  other arithmetic  0.94 us (1%)
    all_to_all x1, blocking collectives, shards(): lax.all_to_all(send_cost, 'wide', split_axis=0, concat_axis=0, tiled=True)  20.7 us
    ppermute x2, waiting for transfers between devices, shards(): lax.ppermute(jnp.where(odd, last, first), ('wide', 'narrow'), far)  14.2 us
    pallas_call x1, Pallas kernels, shards(): pl.pallas_call(adjoint, in_specs=[small, full, away, away, full, full], o...  9.74 us
    pallas_call x1, Pallas kernels, shards(): pl.pallas_call(tangent, in_specs=[small] + [full] * 5, out_specs=away, ou...  8.33 us
    ppermute x2, starting transfers between devices, shards(): lax.ppermute(jnp.where(odd, last, first), ('wide', 'narrow'), far)  8.25 us
    pallas_call x1, Pallas kernels, shards(): pl.pallas_call(prolong, in_specs=[small] + [full] * 4, out_specs=away, ou...  6.58 us
    pallas_call x1, Pallas kernels, shards(): pl.pallas_call(pack_state, in_specs=[small, away, away], out_specs=full,...  6.16 us
    all_to_all x1, starting transfers between devices, shards(): lax.all_to_all(send_state, 'wide', split_axis=0, concat_axis=0, tiled=True)  5.78 us
  transfers between devices with their start and end apart: 6, of which 3 were waited for; matrix products, arithmetic and copies ran while one was open for 0% of the time, Pallas kernels for 11%

profile of v3, /device:TPU:64, one launch (start us, length us, event | category | flops | bytes accessed | tf_op | source)
XLA Modules:
  0.0 92.0 jit_solution(739607967359265092)
XLA Ops:
  0.0 0.7 add_convert_fusion.place_ref
  0.7 6.2 %shard_map.73 = f32[2048,128]{1,0:T(8,128)} custom-call(s32[4]{0:T(128)} %add_convert_fusion.place_ref, f32[5,16,32,72]{3,2,1,0:T(8,128)} %bitcast.20, bf16[5,72,64,128]{3,2,1,0:T(8,128)(2,1)} %traj_in.3), custom_call_target="tpu_custom_call" | custom-call | flops 3000000000 | bytes 3000000 | tf_op jit(solution)/shard_map/pallas_call | solution.py:406
  6.8 0.0 copy-start.4
  6.8 0.0 copy-start.3
  6.8 5.8 %all-to-all-start.1 = ((f32[16,128,128]{2,1,0:T(8,128)}), f32[16,128,128]{2,1,0:T(8,128)S(1)}, u32[]{:S(2)}, u32[]{:S(2)}) async-start(f32[16,128,128]{2,1,0:T(8,128)} %bitcast.14), calls=%async_computation.1 | async-start | bytes 2097152 | tf_op jit(solution)/shard_map/all_to_all | solution.py:422
  12.6 0.0 copy-start.5
  12.6 0.0 copy-done.4
  12.7 0.0 copy-done.3
  12.8 4.5 %collective-permute-start.1 = (f32[6,2,32,72]{3,2,1,0:T(8,128)S(1)}, f32[6,2,32,72]{3,2,1,0:T(8,128)S(1)}, u32[]{:S(2)}, u32[]{:S(2)}) collective-permute-start(f32[6,2,32,72]{3,2,1,0:T(8,128)S(1)} %get-tuple-element.13), channel_id=1, source_target_pairs={{1,2},{2,1},{9,10},{10,9},{17,18},{18,17},{25,26},{26,25},{33,34},... | collective-permute-start | bytes 331784 | tf_op jit(solution)/shard_map/ppermute | solution.py:401
  17.3 0.5 collective-permute-start
  17.7 6.3 %collective-permute-done.1.far_ref = f32[6,2,32,72]{3,2,1,0:T(8,128)S(1)} collective-permute-done((f32[6,2,32,72]{3,2,1,0:T(8,128)S(1)}, f32[6,2,32,72]{3,2,1,0:T(8,128)S(1)}, u32[]{:S(2)}, u32[]{:S(2)}) %collective-permute-start.1) | collective-permute-done | bytes 110624 | tf_op jit(solution)/shard_map/ppermute | solution.py:401
  24.0 0.0 collective-permute-done.near_ref
  24.0 0.0 copy-done.5
  24.0 1.8 %shard_map.74 = f32[2560,128]{1,0:T(8,128)S(1)} custom-call(s32[4]{0:T(128)S(1)} %copy-done.5, f32[5,16,32,72]{3,2,1,0:T(8,128)S(1)} %bitcast.17, f32[16,32,72]{2,1,0:T(8,128)S(1)} %bitcast.19, f32[6,2,32,72]{3,2,1,0:T(8,128)S(1)} %collective-permute-done.near_ref, f32[6,2,32,72]{3,2,1,0:T(8,128)S(1)} %collective-permute-done.1.far_ref), custom_call_target="tpu_custom_call" | custom-call | flops 3000000000 | bytes 3000000 | tf_op jit(solution)/shard_map/pallas_call | solution.py:424
  25.8 0.0 copy-start.1
  25.9 1.0 %copy-done.1 = f32[2560,128]{1,0:T(8,128)} copy-done((f32[2560,128]{1,0:T(8,128)}, f32[2560,128]{1,0:T(8,128)S(1)}, u32[]{:S(2)}) %copy-start.1) | copy-done | bytes 1310744
  26.9 2.2 %all-to-all-done.1.recv_ref = f32[16,128,128]{2,1,0:T(8,128)S(1)} async-done(((f32[16,128,128]{2,1,0:T(8,128)}), f32[16,128,128]{2,1,0:T(8,128)S(1)}, u32[]{:S(2)}, u32[]{:S(2)}) %all-to-all-start.1) | async-done | bytes 1048608 | tf_op jit(solution)/shard_map/all_to_all | solution.py:422
  29.1 0.0 copy-start.7
  29.1 0.0 copy-start
  29.1 4.5 %all-to-all-start = ((f32[16,160,128]{2,1,0:T(8,128)}), f32[16,160,128]{2,1,0:T(8,128)S(1)}, u32[]{:S(2)}, u32[]{:S(2)}) async-start(f32[16,160,128]{2,1,0:T(8,128)} %bitcast.13), calls=%async_computation | async-start | bytes 2621440 | tf_op jit(solution)/shard_map/all_to_all | solution.py:438
  33.7 3.7 %collective-permute-start.3 = (f32[16,32,128]{2,1,0:T(8,128)S(1)}, f32[16,32,128]{2,1,0:T(8,128)S(1)}, u32[]{:S(2)}, u32[]{:S(2)}) collective-permute-start(f32[16,32,128]{2,1,0:T(8,128)S(1)} %get-tuple-element.11), channel_id=1, source_target_pairs={{1,2},{2,1},{9,10},{10,9},{17,18},{18,17},{25,26},{26,25},{33,34},... | collective-permute-start | bytes 786440 | tf_op jit(solution)/shard_map/ppermute | solution.py:437
  37.5 0.7 collective-permute-start.2
  38.2 0.0 copy-done.7
  38.2 0.2 broadcast_select_fusion.resp_ref
  38.4 8.0 %collective-permute-done.3.far_ref = f32[16,32,128]{2,1,0:T(8,128)S(1)} collective-permute-done((f32[16,32,128]{2,1,0:T(8,128)S(1)}, f32[16,32,128]{2,1,0:T(8,128)S(1)}, u32[]{:S(2)}, u32[]{:S(2)}) %collective-permute-start.3) | collective-permute-done | bytes 262176 | tf_op jit(solution)/shard_map/ppermute | solution.py:437
  46.4 0.0 collective-permute-done.2.near_ref
  46.4 0.0 copy-done
  46.4 8.3 %shard_map.75.kept_in = f32[448,32,512]{2,1,0:T(8,128)} custom-call(s32[4]{0:T(128)S(1)} %copy-done.5, f32[16,128,128]{2,1,0:T(8,128)S(1)} %all-to-all-done.1.recv_ref, f32[16,32,128]{2,1,0:T(8,128)S(1)} %collective-permute-done.2.near_ref, f32[16,32,128]{2,1,0:T(8,128)S(1)} %collective-permute-done.3.far_ref, ...), custom_call_target="tpu_custom_call" | custom-call | flops 5000000000 | bytes 5000000 | tf_op jit(solution)/shard_map/pallas_call | solution.py:442
  54.7 0.0 all-to-all-done.recv_ref
  54.7 9.7 %shard_map.76 = (f32[16,100,128]{2,1,0:T(8,128)S(1)}, bf16[5,72,64,128]{3,2,1,0:T(8,128)(2,1)S(1)}) custom-call(s32[4]{0:T(128)S(1)} %copy-done.5, f32[16,160,128]{2,1,0:T(8,128)S(1)} %all-to-all-done.recv_ref, f32[448,32,512]{2,1,0:T(8,128)} %shard_map.75.kept_in, bf16[5,72,64,128]{3,2,1,0:T(8,128)(2,1)} %traj_in.3, ...), custom_call_target="tpu_custom_call" | custom-call | flops 5000000000 | bytes 5000000 | tf_op jit(solution)/shard_map/pallas_call | solution.py:451
  64.5 0.0 copy-start.2
  64.5 0.0 copy-start.6
  64.5 20.7 %all_to_all.15.cost_ref = f32[16,100,128]{2,1,0:T(8,128)S(1)} all-to-all(f32[16,100,128]{2,1,0:T(8,128)S(1)} %get-tuple-element.7), channel_id=1, replica_groups=mesh['wide'=16,'narrow'=8] {'wide'}, dimensions={0} | all-to-all | bytes 1638400 | tf_op jit(solution)/shard_map/all_to_all | solution.py:463
  85.2 0.0 copy-done.2
  85.2 0.0 copy-done.6
  85.2 6.6 %shard_map.77 = bf16[5,72,64,128]{3,2,1,0:T(8,128)(2,1)} custom-call(s32[4]{0:T(128)S(1)} %copy-done.5, f32[16,128,128]{2,1,0:T(8,128)S(1)} %bitcast.15, f32[16,100,128]{2,1,0:T(8,128)S(1)} %all_to_all.15.cost_ref, bf16[5,72,64,128]{3,2,1,0:T(8,128)(2,1)S(1)} %get-tuple-element.8.traj_ref, bf16[256,512]{1,0:T(8,128)(2,1)S(1)} %copy-done.6), custom_call_target="tpu_custom_call" | custom-call | flops 5000000000 | bytes 5000000 | tf_op jit(solution)/shard_map/pallas_call | solution.py:465
  (6 shorter events, 0.2 us)
Async XLA Ops:
  6.8 5.8 %copy-start.4 = (f32[72,16,32]{0,2,1:T(8,128)S(1)}, f32[72,16,32]{0,2,1:T(8,128)}, u32[]{:S(2)}) copy-start(f32[72,16,32]{0,2,1:T(8,128)} %param.10) | copy-start | bytes 442372
  6.8 5.8 %copy-start.3 = (f32[5,72,16,32]{1,3,2,0:T(8,128)S(1)}, f32[5,72,16,32]{1,3,2,0:T(8,128)}, u32[]{:S(2)}) copy-start(f32[5,72,16,32]{1,3,2,0:T(8,128)} %param.8) | copy-start | bytes 2211844
  6.8 22.3 %all-to-all-start.1 = ((f32[16,128,128]{2,1,0:T(8,128)}), f32[16,128,128]{2,1,0:T(8,128)S(1)}, u32[]{:S(2)}, u32[]{:S(2)}) async-start(f32[16,128,128]{2,1,0:T(8,128)} %bitcast.14), calls=%async_computation.1 | async-start | bytes 2097152 | tf_op jit(solution)/shard_map/all_to_all | solution.py:422
  12.6 11.4 %copy-start.5 = (s32[4]{0:T(128)S(1)}, s32[4]{0:T(128)}, u32[]{:S(2)}) copy-start(s32[4]{0:T(128)} %add_convert_fusion.place_ref) | copy-start | bytes 52
  12.8 11.2 %collective-permute-start.1 = (f32[6,2,32,72]{3,2,1,0:T(8,128)S(1)}, f32[6,2,32,72]{3,2,1,0:T(8,128)S(1)}, u32[]{:S(2)}, u32[]{:S(2)}) collective-permute-start(f32[6,2,32,72]{3,2,1,0:T(8,128)S(1)} %get-tuple-element.13), channel_id=1, source_target_pairs={{1,2},{2,1},{9,10},{10,9},{17,18},{18,17},{25,26},{26,25},{33,34},... | collective-permute-start | bytes 331784 | tf_op jit(solution)/shard_map/ppermute | solution.py:401
  17.3 6.8 %collective-permute-start = (f32[6,2,32,72]{3,2,1,0:T(8,128)S(1)}, f32[6,2,32,72]{3,2,1,0:T(8,128)S(1)}, u32[]{:S(2)}, u32[]{:S(2)}) collective-permute-start(f32[6,2,32,72]{3,2,1,0:T(8,128)S(1)} %get-tuple-element.14), channel_id=1, source_target_pairs={{0,1},{1,0},{8,9},{9,8},{16,17},{17,16},{24,25},{25,24},{32,33},{3... | collective-permute-start | bytes 331784 | tf_op jit(solution)/shard_map/ppermute | solution.py:400
  25.8 1.1 %copy-start.1 = (f32[2560,128]{1,0:T(8,128)}, f32[2560,128]{1,0:T(8,128)S(1)}, u32[]{:S(2)}) copy-start(f32[2560,128]{1,0:T(8,128)S(1)} %shard_map.74) | copy-start | bytes 3932164
  29.1 9.1 %copy-start.7 = (f32[512]{0:T(512)S(1)}, f32[512]{0:T(512)}, u32[]{:S(2)}) copy-start(f32[512]{0:T(512)} %constant.52.clone) | copy-start | bytes 6148
  29.1 17.3 %copy-start = (bf16[4,512,256]{2,1,0:T(8,128)(2,1)S(1)}, bf16[4,512,256]{2,1,0:T(8,128)(2,1)}, u32[]{:S(2)}) copy-start(bf16[4,512,256]{2,1,0:T(8,128)(2,1)} %constant.51.clone.basis_ref) | copy-start | bytes 3145732
  29.1 25.6 %all-to-all-start = ((f32[16,160,128]{2,1,0:T(8,128)}), f32[16,160,128]{2,1,0:T(8,128)S(1)}, u32[]{:S(2)}, u32[]{:S(2)}) async-start(f32[16,160,128]{2,1,0:T(8,128)} %bitcast.13), calls=%async_computation | async-start | bytes 2621440 | tf_op jit(solution)/shard_map/all_to_all | solution.py:438
  33.7 12.6 %collective-permute-start.3 = (f32[16,32,128]{2,1,0:T(8,128)S(1)}, f32[16,32,128]{2,1,0:T(8,128)S(1)}, u32[]{:S(2)}, u32[]{:S(2)}) collective-permute-start(f32[16,32,128]{2,1,0:T(8,128)S(1)} %get-tuple-element.11), channel_id=1, source_target_pairs={{1,2},{2,1},{9,10},{10,9},{17,18},{18,17},{25,26},{26,25},{33,34},... | collective-permute-start | bytes 786440 | tf_op jit(solution)/shard_map/ppermute | solution.py:437
  37.5 8.9 %collective-permute-start.2 = (f32[16,32,128]{2,1,0:T(8,128)S(1)}, f32[16,32,128]{2,1,0:T(8,128)S(1)}, u32[]{:S(2)}, u32[]{:S(2)}) collective-permute-start(f32[16,32,128]{2,1,0:T(8,128)S(1)} %get-tuple-element.12), channel_id=1, source_target_pairs={{0,1},{1,0},{8,9},{9,8},{16,17},{17,16},{24,25},{25,24},{32,33},{3... | collective-permute-start | bytes 786440 | tf_op jit(solution)/shard_map/ppermute | solution.py:436
  64.5 20.7 %copy-start.2 = (f32[2048,128]{1,0:T(8,128)S(1)}, f32[2048,128]{1,0:T(8,128)}, u32[]{:S(2)}) copy-start(f32[2048,128]{1,0:T(8,128)} %shard_map.73) | copy-start | bytes 3145732
  64.5 20.7 %copy-start.6 = (bf16[256,512]{1,0:T(8,128)(2,1)S(1)}, bf16[256,512]{1,0:T(8,128)(2,1)}, u32[]{:S(2)}) copy-start(bf16[256,512]{1,0:T(8,128)(2,1)} %constant.53.clone.spread_ref) | copy-start | bytes 786436

commit v4 on v3

--- a/solution.py
+++ b/solution.py
@@ -21,7 +21,7 @@
 WIDE = 16
 HALO = 4
 BAND = ROWS + 2 * HALO
-SLOTS = 3
+SLOTS = 4
 KEPT = 448
 
 diffusion = 0.2
@@ -72,17 +72,27 @@
     return pl.CostEstimate(flops=int(micros * 1e9), bytes_accessed=int(micros * 1e6), transcendentals=0)
 
 
-def scatter_levels(turned_ref, send_ref, fields, groups, flip):
+def scatter_levels(turned_ref, send_ref, fields, groups):
     size = groups * GROUP
-    for field in range(fields):
-        for group in range(groups):
-            for level in range(SHARE):
-                for half in range(2):
-                    first = half * SHARE * WIDE // 2 + level
-                    value = turned_ref[field * groups + group, pl.ds(first, WIDE // 2, stride=SHARE), :]
-                    owner = (WIDE // 2) * (half + flip - 2 * half * flip)
-                    at = owner * size + group * GROUP + field * SHARE + level
-                    send_ref[pl.ds(at, WIDE // 2, stride=size), :] = value
+    half_count = WIDE // 2
+
+    def scatter(flip):
+        for field in range(fields):
+            for group in range(groups):
+                for owner in range(pl.cdiv(LEVELS, SHARE)):
+                    value = turned_ref[field * groups + group, SHARE * owner : SHARE * owner + SHARE, :]
+                    at = (owner ^ (half_count * flip)) * size + group * GROUP + field * SHARE
+                    send_ref[at : at + SHARE, :] = value
+
+    flipped = lax.axis_index("narrow") >= lax.axis_size("narrow") // 2
+
+    @pl.when(flipped)
+    def _():
+        scatter(1)
+
+    @pl.when(jnp.logical_not(flipped))
+    def _():
+        scatter(0)
 
 
 def pooling():
@@ -92,7 +102,7 @@
     return jnp.where(meets, 1.0 / 16, 0.0)
 
 
-def pack_state(place_ref, back_in, traj_in, send_ref, turned_ref, fine_ref, back_ref, wind_ref, sems):
+def pack_state(back_in, traj_in, send_ref, turned_ref, fine_ref, back_ref, wind_ref, sems):
     copies = [pltpu.make_async_copy(traj_in.at[0], wind_ref, sems.at[FIELDS])]
     copies += [pltpu.make_async_copy(back_in.at[f], back_ref.at[f], sems.at[f]) for f in range(FIELDS)]
     for copy in copies:
@@ -123,7 +133,7 @@
         )
         turned_ref[FIELDS * 4 + group, 0:LEVELS, :] = advection_scale * jnp.tanh(mean)
         turned_ref[FIELDS * 4 + group, LEVELS:, :] = spare
-    scatter_levels(turned_ref, send_ref, FIELDS + 1, 4, place_ref[0])
+    scatter_levels(turned_ref, send_ref, FIELDS + 1, 4)
 
 
 def pack_departures(place_ref, innov_ref, weight_ref, near_ref, far_ref, send_ref, turned_ref):
@@ -140,7 +150,7 @@
                 block = jnp.concatenate([before, after], axis=0).reshape(4 * COLS, LEVELS)
             turned_ref[field * 5 + group, 0:LEVELS, :] = block.T
             turned_ref[field * 5 + group, LEVELS:, :] = spare
-    scatter_levels(turned_ref, send_ref, FIELDS + 1, 5, place_ref[0])
+    scatter_levels(turned_ref, send_ref, FIELDS + 1, 5)
 
 
 def lane_block():
@@ -258,7 +268,7 @@
             else:
                 at = 2 + row if row < 2 else 18 + row
                 swapped = place_ref[1] if row < 2 else place_ref[2]
-                lanes = pl.multiple_of(128 * lax.rem(quarter + 2 * swapped, 4), 128)
+                lanes = pl.multiple_of(128 * ((quarter + 2 * swapped) & 3), 128)
                 row_ref[at, :, pl.ds(lanes, 128)] = value
 
         unpack_rows(load, store)
@@ -281,10 +291,9 @@
         def body(index, carry):
             here = field_ref[index]
             carried = drift_ref[index] * here
-            near = field_ref[index - 1] + field_ref[index + 1]
-            near = near + pltpu.roll(here, CYCLE - 1, 1) + pltpu.roll(here, 1, 1)
-            moved = here + diffusion * (near - 4.0 * here)
-            moved = moved + pltpu.roll(carried, 1, 1) - pltpu.roll(carried, CYCLE - 1, 1)
+            spread = diffusion * here
+            moved = here + diffusion * (field_ref[index - 1] + field_ref[index + 1] - 4.0 * here)
+            moved = moved + pltpu.roll(spread + carried, 1, 1) + pltpu.roll(spread - carried, CYCLE - 1, 1)
             if step == 0:
                 fold_store(even_ref, odd_ref, index - 3, moved)
             else:
@@ -311,7 +320,7 @@
     upper = lax.broadcasted_iota(jnp.int32, (8, 128), 0) < 4
 
     def fill(owner, slot, levels):
-        source = lax.rem(owner + (WIDE // 2) * place_ref[0], WIDE)
+        source = (owner + (WIDE // 2) * place_ref[0]) & (WIDE - 1)
         for group in range(4):
             change = (
                 back_ref[source, GROUP * group : GROUP * group + PLANES, :]
@@ -346,7 +355,7 @@
         copy(owner, owner).start()
 
     def body(owner, carry):
-        slot = lax.rem(owner, SLOTS)
+        slot = owner & (SLOTS - 1)
         copy(owner - SLOTS, slot).wait()
         fill(owner, slot, SHARE)
         copy(owner, slot).start()
@@ -405,7 +414,7 @@
     small = pl.BlockSpec(memory_space=pltpu.SMEM)
     send_state = pl.pallas_call(
         pack_state,
-        in_specs=[small, away, away],
+        in_specs=[away, away],
         out_specs=full,
         out_shape=jax.ShapeDtypeStruct((WIDE * 4 * GROUP, 128), f32),
         scratch_shapes=[
@@ -417,7 +426,7 @@
         ],
         compiler_params=params(60),
         cost_estimate=estimate(3),
-    )(place, back, trajectory)
+    )(back, trajectory)
     send_state = send_state.reshape(WIDE, 4 * GROUP, 128)
     held_state = lax.all_to_all(send_state, "wide", split_axis=0, concat_axis=0, tiled=True)
 

time: 92.4 us -> 88.5 us (0.958)
  Pallas kernels: 32.6 us -> 29.5 us
    pallas_call x1, Pallas kernels: 6.16 us -> 4.94 us  [shards(): pl.pallas_call(pack_state, in_specs=[away, away], out_specs=full, out_sha...]
  transfers between devices with their start and end apart: 6 -> 6, of which waited for: 3 -> 4; matrix products, arithmetic and copies ran while one was open for 0% -> 0% of each run, Pallas kernels for 11% -> 11%
where the time goes in v4:
time: 88.5 us; the launch traced here: 88.2 us
  Pallas kernels  29.5 us (33%)
  blocking collectives  20.7 us (23%)
  starting transfers between devices  19.8 us (22%)
  waiting for transfers between devices  16.4 us (19%)
  local copies, waits for them, and re-layouts  1.11 us (1%)
    all_to_all x1, blocking collectives, shards(): lax.all_to_all(send_cost, 'wide', split_axis=0, concat_axis=0, tiled=True)  20.7 us
    ppermute x2, waiting for transfers between devices, shards(): lax.ppermute(jnp.where(odd, last, first), ('wide', 'narrow'), far)  13.5 us
    pallas_call x1, Pallas kernels, shards(): pl.pallas_call(adjoint, in_specs=[small, full, away, away, full, full], o...  8.98 us
    ppermute x2, starting transfers between devices, shards(): lax.ppermute(jnp.where(odd, last, first), ('wide', 'narrow'), far)  8.82 us
    pallas_call x1, Pallas kernels, shards(): pl.pallas_call(tangent, in_specs=[small] + [full] * 5, out_specs=away, ou...  8.33 us
    pallas_call x1, Pallas kernels, shards(): pl.pallas_call(prolong, in_specs=[small] + [full] * 4, out_specs=away, ou...  5.98 us
    all_to_all x1, starting transfers between devices, shards(): lax.all_to_all(send_state, 'wide', split_axis=0, concat_axis=0, tiled=True)  5.77 us
    pallas_call x1, Pallas kernels, shards(): pl.pallas_call(pack_state, in_specs=[away, away], out_specs=full, out_sha...  4.94 us
  transfers between devices with their start and end apart: 6, of which 4 were waited for; matrix products, arithmetic and copies ran while one was open for 0% of the time, Pallas kernels for 11%

profile of v4, /device:TPU:64, one launch (start us, length us, event | category | flops | bytes accessed | tf_op | source)
XLA Modules:
  0.0 88.2 jit_solution(8233000221645688681)
XLA Ops:
  0.0 4.9 %shard_map.73 = f32[2048,128]{1,0:T(8,128)} custom-call(f32[5,16,32,72]{3,2,1,0:T(8,128)} %bitcast.20, bf16[5,72,64,128]{3,2,1,0:T(8,128)(2,1)} %traj_in.3), custom_call_target="tpu_custom_call" | custom-call | flops 3000000000 | bytes 3000000 | tf_op jit(solution)/shard_map/pallas_call | solution.py:415
  4.9 0.0 copy-start.4
  5.0 0.0 copy-start.3
  5.0 5.8 %all-to-all-start.1 = ((f32[16,128,128]{2,1,0:T(8,128)}), f32[16,128,128]{2,1,0:T(8,128)S(1)}, u32[]{:S(2)}, u32[]{:S(2)}) async-start(f32[16,128,128]{2,1,0:T(8,128)} %bitcast.14), calls=%async_computation.1 | async-start | bytes 2097152 | tf_op jit(solution)/shard_map/all_to_all | solution.py:431
  10.8 0.0 copy-done.4
  10.8 0.0 copy-done.3
  10.9 4.5 %collective-permute-start.1 = (f32[6,2,32,72]{3,2,1,0:T(8,128)S(1)}, f32[6,2,32,72]{3,2,1,0:T(8,128)S(1)}, u32[]{:S(2)}, u32[]{:S(2)}) collective-permute-start(f32[6,2,32,72]{3,2,1,0:T(8,128)S(1)} %get-tuple-element.13), channel_id=1, source_target_pairs={{1,2},{2,1},{9,10},{10,9},{17,18},{18,17},{25,26},{26,25},{33,34},... | collective-permute-start | bytes 331784 | tf_op jit(solution)/shard_map/ppermute | solution.py:410
  15.4 0.5 collective-permute-start
  15.9 0.1 add_convert_fusion.place_ref
  16.0 6.1 %collective-permute-done.1.far_ref = f32[6,2,32,72]{3,2,1,0:T(8,128)S(1)} collective-permute-done((f32[6,2,32,72]{3,2,1,0:T(8,128)S(1)}, f32[6,2,32,72]{3,2,1,0:T(8,128)S(1)}, u32[]{:S(2)}, u32[]{:S(2)}) %collective-permute-start.1) | collective-permute-done | bytes 110624 | tf_op jit(solution)/shard_map/ppermute | solution.py:410
  22.1 0.1 collective-permute-done.near_ref
  22.2 1.3 %shard_map.74 = f32[2560,128]{1,0:T(8,128)S(1)} custom-call(s32[4]{0:T(128)S(1)} %add_convert_fusion.place_ref, f32[5,16,32,72]{3,2,1,0:T(8,128)S(1)} %bitcast.17, f32[16,32,72]{2,1,0:T(8,128)S(1)} %bitcast.19, f32[6,2,32,72]{3,2,1,0:T(8,128)S(1)} %collective-permute-done.near_ref, f32[6,2,32,72]{3,2,1,0:T(8,128)S(1)} %collective-permute-done.1.far_ref), custom_call_target="tpu_custom_call" | custom-call | flops 3000000000 | bytes 3000000 | tf_op jit(solution)/shard_map/pallas_call | solution.py:433
  23.4 0.0 copy-start.1
  23.4 1.0 %copy-done.1 = f32[2560,128]{1,0:T(8,128)} copy-done((f32[2560,128]{1,0:T(8,128)}, f32[2560,128]{1,0:T(8,128)S(1)}, u32[]{:S(2)}) %copy-start.1) | copy-done | bytes 1310744
  24.5 2.7 %all-to-all-done.1.recv_ref = f32[16,128,128]{2,1,0:T(8,128)S(1)} async-done(((f32[16,128,128]{2,1,0:T(8,128)}), f32[16,128,128]{2,1,0:T(8,128)S(1)}, u32[]{:S(2)}, u32[]{:S(2)}) %all-to-all-start.1) | async-done | bytes 1048608 | tf_op jit(solution)/shard_map/all_to_all | solution.py:431
  27.2 0.0 copy-start.6
  27.2 0.0 copy-start
  27.2 4.0 %all-to-all-start = ((f32[16,160,128]{2,1,0:T(8,128)}), f32[16,160,128]{2,1,0:T(8,128)S(1)}, u32[]{:S(2)}, u32[]{:S(2)}) async-start(f32[16,160,128]{2,1,0:T(8,128)} %bitcast.13), calls=%async_computation | async-start | bytes 2621440 | tf_op jit(solution)/shard_map/all_to_all | solution.py:447
  31.3 4.3 %collective-permute-start.3 = (f32[16,32,128]{2,1,0:T(8,128)S(1)}, f32[16,32,128]{2,1,0:T(8,128)S(1)}, u32[]{:S(2)}, u32[]{:S(2)}) collective-permute-start(f32[16,32,128]{2,1,0:T(8,128)S(1)} %get-tuple-element.11), channel_id=1, source_target_pairs={{1,2},{2,1},{9,10},{10,9},{17,18},{18,17},{25,26},{26,25},{33,34},... | collective-permute-start | bytes 786440 | tf_op jit(solution)/shard_map/ppermute | solution.py:446
  35.6 0.7 collective-permute-start.2
  36.4 0.0 copy-done.6
  36.4 0.2 broadcast_select_fusion.resp_ref
  36.5 7.4 %collective-permute-done.3.far_ref = f32[16,32,128]{2,1,0:T(8,128)S(1)} collective-permute-done((f32[16,32,128]{2,1,0:T(8,128)S(1)}, f32[16,32,128]{2,1,0:T(8,128)S(1)}, u32[]{:S(2)}, u32[]{:S(2)}) %collective-permute-start.3) | collective-permute-done | bytes 262176 | tf_op jit(solution)/shard_map/ppermute | solution.py:446
  43.9 0.0 collective-permute-done.2.near_ref
  43.9 0.0 copy-done
  44.0 8.3 %shard_map.75.kept_in = f32[448,32,512]{2,1,0:T(8,128)} custom-call(s32[4]{0:T(128)S(1)} %add_convert_fusion.place_ref, f32[16,128,128]{2,1,0:T(8,128)S(1)} %all-to-all-done.1.recv_ref, f32[16,32,128]{2,1,0:T(8,128)S(1)} %collective-permute-done.2.near_ref, f32[16,32,128]{2,1,0:T(8,128)S(1)} %collective-permute-done.3.far_ref, ...), custom_call_target="tpu_custom_call" | custom-call | flops 5000000000 | bytes 5000000 | tf_op jit(solution)/shard_map/pallas_call | solution.py:451
  52.3 0.0 all-to-all-done.recv_ref
  52.3 9.0 %shard_map.76 = (f32[16,100,128]{2,1,0:T(8,128)S(1)}, bf16[5,72,64,128]{3,2,1,0:T(8,128)(2,1)S(1)}) custom-call(s32[4]{0:T(128)S(1)} %add_convert_fusion.place_ref, f32[16,160,128]{2,1,0:T(8,128)S(1)} %all-to-all-done.recv_ref, f32[448,32,512]{2,1,0:T(8,128)} %shard_map.75.kept_in, bf16[5,72,64,128]{3,2,1,0:T(8,128)(2,1)} %traj_in.3, ...), custom_call_target="tpu_custom_call" | custom-call | flops 5000000000 | bytes 5000000 | tf_op jit(solution)/shard_map/pallas_call | solution.py:460
  61.3 0.0 copy-start.2
  61.3 0.0 copy-start.5
  61.3 20.7 %all_to_all.15.cost_ref = f32[16,100,128]{2,1,0:T(8,128)S(1)} all-to-all(f32[16,100,128]{2,1,0:T(8,128)S(1)} %get-tuple-element.7), channel_id=1, replica_groups=mesh['wide'=16,'narrow'=8] {'wide'}, dimensions={0} | all-to-all | bytes 1638400 | tf_op jit(solution)/shard_map/all_to_all | solution.py:472
  82.0 0.0 copy-done.2
  82.0 0.0 copy-done.5
  82.0 6.0 %shard_map.77 = bf16[5,72,64,128]{3,2,1,0:T(8,128)(2,1)} custom-call(s32[4]{0:T(128)S(1)} %add_convert_fusion.place_ref, f32[16,128,128]{2,1,0:T(8,128)S(1)} %bitcast.15, f32[16,100,128]{2,1,0:T(8,128)S(1)} %all_to_all.15.cost_ref, bf16[5,72,64,128]{3,2,1,0:T(8,128)(2,1)S(1)} %get-tuple-element.8.traj_ref, bf16[256,512]{1,0:T(8,128)(2,1)S(1)} %copy-done.5), custom_call_target="tpu_custom_call" | custom-call | flops 5000000000 | bytes 5000000 | tf_op jit(solution)/shard_map/pallas_call | solution.py:474
  (6 shorter events, 0.2 us)
Async XLA Ops:
  4.9 5.8 %copy-start.4 = (f32[72,16,32]{0,2,1:T(8,128)S(1)}, f32[72,16,32]{0,2,1:T(8,128)}, u32[]{:S(2)}) copy-start(f32[72,16,32]{0,2,1:T(8,128)} %param.10) | copy-start | bytes 442372
  5.0 5.8 %copy-start.3 = (f32[5,72,16,32]{1,3,2,0:T(8,128)S(1)}, f32[5,72,16,32]{1,3,2,0:T(8,128)}, u32[]{:S(2)}) copy-start(f32[5,72,16,32]{1,3,2,0:T(8,128)} %param.8) | copy-start | bytes 2211844
  5.0 22.3 %all-to-all-start.1 = ((f32[16,128,128]{2,1,0:T(8,128)}), f32[16,128,128]{2,1,0:T(8,128)S(1)}, u32[]{:S(2)}, u32[]{:S(2)}) async-start(f32[16,128,128]{2,1,0:T(8,128)} %bitcast.14), calls=%async_computation.1 | async-start | bytes 2097152 | tf_op jit(solution)/shard_map/all_to_all | solution.py:431
  10.9 11.2 %collective-permute-start.1 = (f32[6,2,32,72]{3,2,1,0:T(8,128)S(1)}, f32[6,2,32,72]{3,2,1,0:T(8,128)S(1)}, u32[]{:S(2)}, u32[]{:S(2)}) collective-permute-start(f32[6,2,32,72]{3,2,1,0:T(8,128)S(1)} %get-tuple-element.13), channel_id=1, source_target_pairs={{1,2},{2,1},{9,10},{10,9},{17,18},{18,17},{25,26},{26,25},{33,34},... | collective-permute-start | bytes 331784 | tf_op jit(solution)/shard_map/ppermute | solution.py:410
  15.4 6.8 %collective-permute-start = (f32[6,2,32,72]{3,2,1,0:T(8,128)S(1)}, f32[6,2,32,72]{3,2,1,0:T(8,128)S(1)}, u32[]{:S(2)}, u32[]{:S(2)}) collective-permute-start(f32[6,2,32,72]{3,2,1,0:T(8,128)S(1)} %get-tuple-element.14), channel_id=1, source_target_pairs={{0,1},{1,0},{8,9},{9,8},{16,17},{17,16},{24,25},{25,24},{32,33},{3... | collective-permute-start | bytes 331784 | tf_op jit(solution)/shard_map/ppermute | solution.py:409
  23.4 1.1 %copy-start.1 = (f32[2560,128]{1,0:T(8,128)}, f32[2560,128]{1,0:T(8,128)S(1)}, u32[]{:S(2)}) copy-start(f32[2560,128]{1,0:T(8,128)S(1)} %shard_map.74) | copy-start | bytes 3932164
  27.2 9.1 %copy-start.6 = (f32[512]{0:T(512)S(1)}, f32[512]{0:T(512)}, u32[]{:S(2)}) copy-start(f32[512]{0:T(512)} %constant.52.clone) | copy-start | bytes 6148
  27.2 16.7 %copy-start = (bf16[4,512,256]{2,1,0:T(8,128)(2,1)S(1)}, bf16[4,512,256]{2,1,0:T(8,128)(2,1)}, u32[]{:S(2)}) copy-start(bf16[4,512,256]{2,1,0:T(8,128)(2,1)} %constant.51.clone.basis_ref) | copy-start | bytes 3145732
  27.2 25.1 %all-to-all-start = ((f32[16,160,128]{2,1,0:T(8,128)}), f32[16,160,128]{2,1,0:T(8,128)S(1)}, u32[]{:S(2)}, u32[]{:S(2)}) async-start(f32[16,160,128]{2,1,0:T(8,128)} %bitcast.13), calls=%async_computation | async-start | bytes 2621440 | tf_op jit(solution)/shard_map/all_to_all | solution.py:447
  31.3 12.6 %collective-permute-start.3 = (f32[16,32,128]{2,1,0:T(8,128)S(1)}, f32[16,32,128]{2,1,0:T(8,128)S(1)}, u32[]{:S(2)}, u32[]{:S(2)}) collective-permute-start(f32[16,32,128]{2,1,0:T(8,128)S(1)} %get-tuple-element.11), channel_id=1, source_target_pairs={{1,2},{2,1},{9,10},{10,9},{17,18},{18,17},{25,26},{26,25},{33,34},... | collective-permute-start | bytes 786440 | tf_op jit(solution)/shard_map/ppermute | solution.py:446
  35.6 8.3 %collective-permute-start.2 = (f32[16,32,128]{2,1,0:T(8,128)S(1)}, f32[16,32,128]{2,1,0:T(8,128)S(1)}, u32[]{:S(2)}, u32[]{:S(2)}) collective-permute-start(f32[16,32,128]{2,1,0:T(8,128)S(1)} %get-tuple-element.12), channel_id=1, source_target_pairs={{0,1},{1,0},{8,9},{9,8},{16,17},{17,16},{24,25},{25,24},{32,33},{3... | collective-permute-start | bytes 786440 | tf_op jit(solution)/shard_map/ppermute | solution.py:445
  61.3 20.7 %copy-start.2 = (f32[2048,128]{1,0:T(8,128)S(1)}, f32[2048,128]{1,0:T(8,128)}, u32[]{:S(2)}) copy-start(f32[2048,128]{1,0:T(8,128)} %shard_map.73) | copy-start | bytes 3145732
  61.3 20.7 %copy-start.5 = (bf16[256,512]{1,0:T(8,128)(2,1)S(1)}, bf16[256,512]{1,0:T(8,128)(2,1)}, u32[]{:S(2)}) copy-start(bf16[256,512]{1,0:T(8,128)(2,1)} %constant.53.clone.spread_ref) | copy-start | bytes 786436

commit v5 on v4

--- a/solution.py
+++ b/solution.py
@@ -18,10 +18,13 @@
 SHARE = 5
 GROUP = 32
 PLANES = FIELDS * SHARE
+SENT = PLANES + SHARE
+STATE_ROWS, DEPART_ROWS = 4 * SENT, 5 * SENT + 2
 WIDE = 16
 HALO = 4
 BAND = ROWS + 2 * HALO
 SLOTS = 4
+PITCH = 72
 KEPT = 448
 
 diffusion = 0.2
@@ -72,8 +75,7 @@
     return pl.CostEstimate(flops=int(micros * 1e9), bytes_accessed=int(micros * 1e6), transcendentals=0)
 
 
-def scatter_levels(turned_ref, send_ref, fields, groups):
-    size = groups * GROUP
+def scatter_levels(turned_ref, send_ref, fields, groups, size):
     half_count = WIDE // 2
 
     def scatter(flip):
@@ -81,7 +83,7 @@
             for group in range(groups):
                 for owner in range(pl.cdiv(LEVELS, SHARE)):
                     value = turned_ref[field * groups + group, SHARE * owner : SHARE * owner + SHARE, :]
-                    at = (owner ^ (half_count * flip)) * size + group * GROUP + field * SHARE
+                    at = (owner ^ (half_count * flip)) * size + group * SENT + field * SHARE
                     send_ref[at : at + SHARE, :] = value
 
     flipped = lax.axis_index("narrow") >= lax.axis_size("narrow") // 2
@@ -99,7 +101,7 @@
     fine = lax.broadcasted_iota(jnp.int32, (16 * COLS, 4 * COLS), 0)
     lane = lax.broadcasted_iota(jnp.int32, (16 * COLS, 4 * COLS), 1)
     meets = (fine // (4 * COLS) == lane // COLS) & ((fine % (4 * COLS)) // 4 == lane % COLS)
-    return jnp.where(meets, 1.0 / 16, 0.0)
+    return jnp.where(meets, 1.0 / 16, 0.0).astype(jnp.bfloat16)
 
 
 def pack_state(back_in, traj_in, send_ref, turned_ref, fine_ref, back_ref, wind_ref, sems):
@@ -110,7 +112,8 @@
     spare = jnp.zeros((8, 128), jnp.float32)
     pool = pooling()
     copies[0].wait()
-    fine_ref[...] = wind_ref[...].astype(jnp.float32).reshape(LEVELS * 64, 128)
+    for level in range(LEVELS):
+        fine_ref[PITCH * level : PITCH * level + 64, :] = wind_ref[level].astype(jnp.float32)
     for group in range(4):
         for field in range(FIELDS):
             if group == 0:
@@ -121,19 +124,18 @@
         parts = []
         for part in range(4):
             first = 16 * group + 4 * part
-            total = fine_ref[pl.ds(first, LEVELS, stride=64), :]
+            total = fine_ref[pl.ds(first, LEVELS, stride=PITCH), :]
             for extra in range(1, 4):
-                total = total + fine_ref[pl.ds(first + extra, LEVELS, stride=64), :]
+                total = total + fine_ref[pl.ds(first + extra, LEVELS, stride=PITCH), :]
             parts.append(total)
-        mean = jnp.dot(
-            jnp.concatenate(parts, axis=1),
-            pool,
-            precision=lax.Precision.HIGHEST,
-            preferred_element_type=jnp.float32,
-        )
+        total = jnp.concatenate(parts, axis=1)
+        high = total.astype(jnp.bfloat16)
+        low = (total - high.astype(jnp.float32)).astype(jnp.bfloat16)
+        mean = jnp.dot(high, pool, preferred_element_type=jnp.float32)
+        mean = mean + jnp.dot(low, pool, preferred_element_type=jnp.float32)
         turned_ref[FIELDS * 4 + group, 0:LEVELS, :] = advection_scale * jnp.tanh(mean)
         turned_ref[FIELDS * 4 + group, LEVELS:, :] = spare
-    scatter_levels(turned_ref, send_ref, FIELDS + 1, 4)
+    scatter_levels(turned_ref, send_ref, FIELDS + 1, 4, STATE_ROWS)
 
 
 def pack_departures(place_ref, innov_ref, weight_ref, near_ref, far_ref, send_ref, turned_ref):
@@ -150,7 +152,7 @@
                 block = jnp.concatenate([before, after], axis=0).reshape(4 * COLS, LEVELS)
             turned_ref[field * 5 + group, 0:LEVELS, :] = block.T
             turned_ref[field * 5 + group, LEVELS:, :] = spare
-    scatter_levels(turned_ref, send_ref, FIELDS + 1, 5)
+    scatter_levels(turned_ref, send_ref, FIELDS + 1, 5, DEPART_ROWS)
 
 
 def lane_block():
@@ -219,10 +221,15 @@
                 return jnp.where(place_ref[3] == 1, near_ref[source], far_ref[source])
             if group == 5:
                 return jnp.where(place_ref[3] == 1, far_ref[source], near_ref[source])
-            return recv_ref[source, GROUP * (group - 1) : GROUP * group, :]
+            first = SENT * (group - 1) if group < 4 else STATE_ROWS - GROUP
+            return recv_ref[source, first : first + GROUP, :]
 
         def store(row, quarter, value):
-            row_ref[4 * group + row, :, 128 * quarter : 128 * quarter + 128] = value
+            lanes = slice(128 * quarter, 128 * quarter + 128)
+            if group in (0, 4):
+                row_ref[4 * group + row, 0:SENT, lanes] = value[GROUP - SENT :]
+            else:
+                row_ref[4 * group + row, :, lanes] = value
 
         unpack_rows(load, store)
     drift_ref[:, GROUP - 8 :, :] = jnp.zeros((BAND, 8, CYCLE), jnp.float32)
@@ -260,7 +267,7 @@
     held_copy.start()
     for group in range(5):
         def load(source):
-            return recv_ref[source, GROUP * group : GROUP * group + GROUP, :]
+            return recv_ref[source, SENT * group : SENT * group + GROUP, :]
 
         def store(row, quarter, value):
             if group < 4:
@@ -323,7 +330,7 @@
         source = (owner + (WIDE // 2) * place_ref[0]) & (WIDE - 1)
         for group in range(4):
             change = (
-                back_ref[source, GROUP * group : GROUP * group + PLANES, :]
+                back_ref[source, SENT * group : SENT * group + PLANES, :]
                 - cost_ref[source, PLANES * group : PLANES * group + PLANES, :]
             )
             high = change.astype(jnp.bfloat16)
@@ -416,10 +423,10 @@
         pack_state,
         in_specs=[away, away],
         out_specs=full,
-        out_shape=jax.ShapeDtypeStruct((WIDE * 4 * GROUP, 128), f32),
+        out_shape=jax.ShapeDtypeStruct((WIDE * STATE_ROWS, 128), f32),
         scratch_shapes=[
             pltpu.VMEM((24, 80, 128), f32),
-            pltpu.VMEM((LEVELS * 64, 128), f32),
+            pltpu.VMEM((LEVELS * PITCH, 128), f32),
             pltpu.VMEM((FIELDS, ROWS, COLS, LEVELS), f32),
             pltpu.VMEM((LEVELS, 64, 128), jnp.bfloat16),
             pltpu.SemaphoreType.DMA((FIELDS + 1,)),
@@ -427,21 +434,21 @@
         compiler_params=params(60),
         cost_estimate=estimate(3),
     )(back, trajectory)
-    send_state = send_state.reshape(WIDE, 4 * GROUP, 128)
+    send_state = send_state.reshape(WIDE, STATE_ROWS, 128)
     held_state = lax.all_to_all(send_state, "wide", split_axis=0, concat_axis=0, tiled=True)
 
     send_depart = pl.pallas_call(
         pack_departures,
         in_specs=[small] + [full] * 4,
         out_specs=full,
-        out_shape=jax.ShapeDtypeStruct((WIDE * 5 * GROUP, 128), f32),
+        out_shape=jax.ShapeDtypeStruct((WIDE * DEPART_ROWS, 128), f32),
         scratch_shapes=[pltpu.VMEM((30, 80, 128), f32)],
         compiler_params=params(16),
         cost_estimate=estimate(3),
     )(place, innov, weight, edge_near, edge_far)
-    send_depart = send_depart.reshape(WIDE, 5 * GROUP, 128)
-
-    first, last = held_state[:, :GROUP], held_state[:, 3 * GROUP :]
+    send_depart = send_depart.reshape(WIDE, DEPART_ROWS, 128)
+
+    first, last = held_state[:, :GROUP], held_state[:, STATE_ROWS - GROUP :]
     rows_near = lax.ppermute(jnp.where(odd, first, last), ("wide", "narrow"), near)
     rows_far = lax.ppermute(jnp.where(odd, last, first), ("wide", "narrow"), far)
     held_depart = lax.all_to_all(send_depart, "wide", split_axis=0, concat_axis=0, tiled=True)

time: 88.5 us -> 87 us (0.983)
  Pallas kernels: 29.5 us -> 28.1 us
    pallas_call x1, Pallas kernels: 4.94 us -> 3.6 us  [shards(): pl.pallas_call(pack_state, in_specs=[away, away], out_specs=full, out_sha...]
where the time goes in v5:
time: 87 us; the launch traced here: 86.6 us
  Pallas kernels  28.1 us (32%)
  blocking collectives  20.7 us (24%)
  starting transfers between devices  19.6 us (23%)
  waiting for transfers between devices  16.5 us (19%)
  local copies, waits for them, and re-layouts  1.09 us (1%)
    all_to_all x1, blocking collectives, shards(): lax.all_to_all(send_cost, 'wide', split_axis=0, concat_axis=0, tiled=True)  20.7 us
    ppermute x2, waiting for transfers between devices, shards(): lax.ppermute(jnp.where(odd, last, first), ('wide', 'narrow'), far)  14.3 us
    pallas_call x1, Pallas kernels, shards(): pl.pallas_call(adjoint, in_specs=[small, full, away, away, full, full], o...  8.98 us
    pallas_call x1, Pallas kernels, shards(): pl.pallas_call(tangent, in_specs=[small] + [full] * 5, out_specs=away, ou...  8.34 us
    ppermute x2, starting transfers between devices, shards(): lax.ppermute(jnp.where(odd, last, first), ('wide', 'narrow'), far)  8.22 us
    pallas_call x1, Pallas kernels, shards(): pl.pallas_call(prolong, in_specs=[small] + [full] * 4, out_specs=away, ou...  5.99 us
    all_to_all x1, starting transfers between devices, shards(): lax.all_to_all(send_state, 'wide', split_axis=0, concat_axis=0, tiled=True)  5.78 us
    all_to_all x1, starting transfers between devices, shards(): lax.all_to_all(send_depart, 'wide', split_axis=0, concat_axis=0, tiled=True)  4.59 us
  transfers between devices with their start and end apart: 6, of which 4 were waited for; matrix products, arithmetic and copies ran while one was open for 0% of the time, Pallas kernels for 11%

profile of v5, /device:TPU:64, one launch (start us, length us, event | category | flops | bytes accessed | tf_op | source)
XLA Modules:
  0.0 86.6 jit_solution(11399261109799631958)
XLA Ops:
  0.0 3.6 %shard_map.73 = f32[1920,128]{1,0:T(8,128)} custom-call(f32[5,16,32,72]{3,2,1,0:T(8,128)} %bitcast.20, bf16[5,72,64,128]{3,2,1,0:T(8,128)(2,1)} %traj_in.3), custom_call_target="tpu_custom_call" | custom-call | flops 3000000000 | bytes 3000000 | tf_op jit(solution)/shard_map/pallas_call | solution.py:422
  3.6 0.0 copy-start.4
  3.6 0.0 copy-start.3
  3.6 5.8 %all-to-all-start.1 = ((f32[16,120,128]{2,1,0:T(8,128)}), f32[16,120,128]{2,1,0:T(8,128)S(1)}, u32[]{:S(2)}, u32[]{:S(2)}) async-start(f32[16,120,128]{2,1,0:T(8,128)} %bitcast.14), calls=%async_computation.1 | async-start | bytes 1966080 | tf_op jit(solution)/shard_map/all_to_all | solution.py:438
  9.4 0.0 copy-done.4
  9.5 0.0 copy-done.3
  9.5 4.5 %collective-permute-start.1 = (f32[6,2,32,72]{3,2,1,0:T(8,128)S(1)}, f32[6,2,32,72]{3,2,1,0:T(8,128)S(1)}, u32[]{:S(2)}, u32[]{:S(2)}) collective-permute-start(f32[6,2,32,72]{3,2,1,0:T(8,128)S(1)} %get-tuple-element.13), channel_id=1, source_target_pairs={{1,2},{2,1},{9,10},{10,9},{17,18},{18,17},{25,26},{26,25},{33,34},... | collective-permute-start | bytes 331784 | tf_op jit(solution)/shard_map/ppermute | solution.py:417
  14.1 0.5 collective-permute-start
  14.6 0.1 add_convert_fusion.place_ref
  14.6 6.1 %collective-permute-done.1.far_ref = f32[6,2,32,72]{3,2,1,0:T(8,128)S(1)} collective-permute-done((f32[6,2,32,72]{3,2,1,0:T(8,128)S(1)}, f32[6,2,32,72]{3,2,1,0:T(8,128)S(1)}, u32[]{:S(2)}, u32[]{:S(2)}) %collective-permute-start.1) | collective-permute-done | bytes 110624 | tf_op jit(solution)/shard_map/ppermute | solution.py:417
  20.7 0.1 collective-permute-done.near_ref
  20.8 1.2 %shard_map.74 = f32[2432,128]{1,0:T(8,128)S(1)} custom-call(s32[4]{0:T(128)S(1)} %add_convert_fusion.place_ref, f32[5,16,32,72]{3,2,1,0:T(8,128)S(1)} %bitcast.17, f32[16,32,72]{2,1,0:T(8,128)S(1)} %bitcast.19, f32[6,2,32,72]{3,2,1,0:T(8,128)S(1)} %collective-permute-done.near_ref, f32[6,2,32,72]{3,2,1,0:T(8,128)S(1)} %collective-permute-done.1.far_ref), custom_call_target="tpu_custom_call" | custom-call | flops 3000000000 | bytes 3000000 | tf_op jit(solution)/shard_map/pallas_call | solution.py:440
  22.0 0.0 copy-start.1
  22.0 1.0 %copy-done.1 = f32[2432,128]{1,0:T(8,128)} copy-done((f32[2432,128]{1,0:T(8,128)}, f32[2432,128]{1,0:T(8,128)S(1)}, u32[]{:S(2)}) %copy-start.1) | copy-done | bytes 1245208
  23.1 2.1 %all-to-all-done.1.recv_ref = f32[16,120,128]{2,1,0:T(8,128)S(1)} async-done(((f32[16,120,128]{2,1,0:T(8,128)}), f32[16,120,128]{2,1,0:T(8,128)S(1)}, u32[]{:S(2)}, u32[]{:S(2)}) %all-to-all-start.1) | async-done | bytes 983072 | tf_op jit(solution)/shard_map/all_to_all | solution.py:438
  25.2 0.0 copy-start.6
  25.2 0.0 copy-start
  25.2 4.6 %all-to-all-start = ((f32[16,152,128]{2,1,0:T(8,128)}), f32[16,152,128]{2,1,0:T(8,128)S(1)}, u32[]{:S(2)}, u32[]{:S(2)}) async-start(f32[16,152,128]{2,1,0:T(8,128)} %bitcast.13), calls=%async_computation | async-start | bytes 2490368 | tf_op jit(solution)/shard_map/all_to_all | solution.py:454
  29.8 0.1 slice_select_fusion
  29.9 3.7 %collective-permute-start.3 = (f32[16,32,128]{2,1,0:T(8,128)S(1)}, f32[16,32,128]{2,1,0:T(8,128)S(1)}, u32[]{:S(2)}, u32[]{:S(2)}) collective-permute-start(f32[16,32,128]{2,1,0:T(8,128)S(1)} %get-tuple-element.11), channel_id=1, source_target_pairs={{1,2},{2,1},{9,10},{10,9},{17,18},{18,17},{25,26},{26,25},{33,34},... | collective-permute-start | bytes 786440 | tf_op jit(solution)/shard_map/ppermute | solution.py:453
  33.6 0.5 collective-permute-start.2
  34.2 0.0 copy-done.6
  34.2 0.2 broadcast_select_fusion.resp_ref
  34.3 8.2 %collective-permute-done.3.far_ref = f32[16,32,128]{2,1,0:T(8,128)S(1)} collective-permute-done((f32[16,32,128]{2,1,0:T(8,128)S(1)}, f32[16,32,128]{2,1,0:T(8,128)S(1)}, u32[]{:S(2)}, u32[]{:S(2)}) %collective-permute-start.3) | collective-permute-done | bytes 262176 | tf_op jit(solution)/shard_map/ppermute | solution.py:453
  42.5 0.0 collective-permute-done.2.near_ref
  42.5 0.0 copy-done
  42.5 8.3 %shard_map.75.kept_in = f32[448,32,512]{2,1,0:T(8,128)} custom-call(s32[4]{0:T(128)S(1)} %add_convert_fusion.place_ref, f32[16,120,128]{2,1,0:T(8,128)S(1)} %all-to-all-done.1.recv_ref, f32[16,32,128]{2,1,0:T(8,128)S(1)} %collective-permute-done.2.near_ref, f32[16,32,128]{2,1,0:T(8,128)S(1)} %collective-permute-done.3.far_ref, ...), custom_call_target="tpu_custom_call" | custom-call | flops 5000000000 | bytes 5000000 | tf_op jit(solution)/shard_map/pallas_call | solution.py:458
  50.9 0.0 all-to-all-done.recv_ref
  50.9 9.0 %shard_map.76 = (f32[16,100,128]{2,1,0:T(8,128)S(1)}, bf16[5,72,64,128]{3,2,1,0:T(8,128)(2,1)S(1)}) custom-call(s32[4]{0:T(128)S(1)} %add_convert_fusion.place_ref, f32[16,152,128]{2,1,0:T(8,128)S(1)} %all-to-all-done.recv_ref, f32[448,32,512]{2,1,0:T(8,128)} %shard_map.75.kept_in, bf16[5,72,64,128]{3,2,1,0:T(8,128)(2,1)} %traj_in.3, ...), custom_call_target="tpu_custom_call" | custom-call | flops 5000000000 | bytes 5000000 | tf_op jit(solution)/shard_map/pallas_call | solution.py:467
  59.9 0.0 copy-start.2
  59.9 0.0 copy-start.5
  59.9 20.7 %all_to_all.15.cost_ref = f32[16,100,128]{2,1,0:T(8,128)S(1)} all-to-all(f32[16,100,128]{2,1,0:T(8,128)S(1)} %get-tuple-element.7), channel_id=1, replica_groups=mesh['wide'=16,'narrow'=8] {'wide'}, dimensions={0} | all-to-all | bytes 1638400 | tf_op jit(solution)/shard_map/all_to_all | solution.py:479
  80.6 0.0 copy-done.2
  80.6 0.0 copy-done.5
  80.6 6.0 %shard_map.77 = bf16[5,72,64,128]{3,2,1,0:T(8,128)(2,1)} custom-call(s32[4]{0:T(128)S(1)} %add_convert_fusion.place_ref, f32[16,120,128]{2,1,0:T(8,128)S(1)} %bitcast.15, f32[16,100,128]{2,1,0:T(8,128)S(1)} %all_to_all.15.cost_ref, bf16[5,72,64,128]{3,2,1,0:T(8,128)(2,1)S(1)} %get-tuple-element.8.traj_ref, bf16[256,512]{1,0:T(8,128)(2,1)S(1)} %copy-done.5), custom_call_target="tpu_custom_call" | custom-call | flops 5000000000 | bytes 5000000 | tf_op jit(solution)/shard_map/pallas_call | solution.py:481
  (5 shorter events, 0.1 us)
Async XLA Ops:
  3.6 5.8 %copy-start.4 = (f32[72,16,32]{0,2,1:T(8,128)S(1)}, f32[72,16,32]{0,2,1:T(8,128)}, u32[]{:S(2)}) copy-start(f32[72,16,32]{0,2,1:T(8,128)} %param.10) | copy-start | bytes 442372
  3.6 5.8 %copy-start.3 = (f32[5,72,16,32]{1,3,2,0:T(8,128)S(1)}, f32[5,72,16,32]{1,3,2,0:T(8,128)}, u32[]{:S(2)}) copy-start(f32[5,72,16,32]{1,3,2,0:T(8,128)} %param.8) | copy-start | bytes 2211844
  3.6 21.6 %all-to-all-start.1 = ((f32[16,120,128]{2,1,0:T(8,128)}), f32[16,120,128]{2,1,0:T(8,128)S(1)}, u32[]{:S(2)}, u32[]{:S(2)}) async-start(f32[16,120,128]{2,1,0:T(8,128)} %bitcast.14), calls=%async_computation.1 | async-start | bytes 1966080 | tf_op jit(solution)/shard_map/all_to_all | solution.py:438
  9.5 11.2 %collective-permute-start.1 = (f32[6,2,32,72]{3,2,1,0:T(8,128)S(1)}, f32[6,2,32,72]{3,2,1,0:T(8,128)S(1)}, u32[]{:S(2)}, u32[]{:S(2)}) collective-permute-start(f32[6,2,32,72]{3,2,1,0:T(8,128)S(1)} %get-tuple-element.13), channel_id=1, source_target_pairs={{1,2},{2,1},{9,10},{10,9},{17,18},{18,17},{25,26},{26,25},{33,34},... | collective-permute-start | bytes 331784 | tf_op jit(solution)/shard_map/ppermute | solution.py:417
  14.1 6.8 %collective-permute-start = (f32[6,2,32,72]{3,2,1,0:T(8,128)S(1)}, f32[6,2,32,72]{3,2,1,0:T(8,128)S(1)}, u32[]{:S(2)}, u32[]{:S(2)}) collective-permute-start(f32[6,2,32,72]{3,2,1,0:T(8,128)S(1)} %get-tuple-element.14), channel_id=1, source_target_pairs={{0,1},{1,0},{8,9},{9,8},{16,17},{17,16},{24,25},{25,24},{32,33},{3... | collective-permute-start | bytes 331784 | tf_op jit(solution)/shard_map/ppermute | solution.py:416
  22.0 1.0 %copy-start.1 = (f32[2432,128]{1,0:T(8,128)}, f32[2432,128]{1,0:T(8,128)S(1)}, u32[]{:S(2)}) copy-start(f32[2432,128]{1,0:T(8,128)S(1)} %shard_map.74) | copy-start | bytes 3735556
  25.2 9.0 %copy-start.6 = (f32[512]{0:T(512)S(1)}, f32[512]{0:T(512)}, u32[]{:S(2)}) copy-start(f32[512]{0:T(512)} %constant.52.clone) | copy-start | bytes 6148
  25.2 17.3 %copy-start = (bf16[4,512,256]{2,1,0:T(8,128)(2,1)S(1)}, bf16[4,512,256]{2,1,0:T(8,128)(2,1)}, u32[]{:S(2)}) copy-start(bf16[4,512,256]{2,1,0:T(8,128)(2,1)} %constant.51.clone.basis_ref) | copy-start | bytes 3145732
  25.2 25.7 %all-to-all-start = ((f32[16,152,128]{2,1,0:T(8,128)}), f32[16,152,128]{2,1,0:T(8,128)S(1)}, u32[]{:S(2)}, u32[]{:S(2)}) async-start(f32[16,152,128]{2,1,0:T(8,128)} %bitcast.13), calls=%async_computation | async-start | bytes 2490368 | tf_op jit(solution)/shard_map/all_to_all | solution.py:454
  29.9 12.6 %collective-permute-start.3 = (f32[16,32,128]{2,1,0:T(8,128)S(1)}, f32[16,32,128]{2,1,0:T(8,128)S(1)}, u32[]{:S(2)}, u32[]{:S(2)}) collective-permute-start(f32[16,32,128]{2,1,0:T(8,128)S(1)} %get-tuple-element.11), channel_id=1, source_target_pairs={{1,2},{2,1},{9,10},{10,9},{17,18},{18,17},{25,26},{26,25},{33,34},... | collective-permute-start | bytes 786440 | tf_op jit(solution)/shard_map/ppermute | solution.py:453
  33.6 8.9 %collective-permute-start.2 = (f32[16,32,128]{2,1,0:T(8,128)S(1)}, f32[16,32,128]{2,1,0:T(8,128)S(1)}, u32[]{:S(2)}, u32[]{:S(2)}) collective-permute-start(f32[16,32,128]{2,1,0:T(8,128)S(1)} %get-tuple-element.12), channel_id=1, source_target_pairs={{0,1},{1,0},{8,9},{9,8},{16,17},{17,16},{24,25},{25,24},{32,33},{3... | collective-permute-start | bytes 786440 | tf_op jit(solution)/shard_map/ppermute | solution.py:452
  59.9 20.7 %copy-start.2 = (f32[1920,128]{1,0:T(8,128)S(1)}, f32[1920,128]{1,0:T(8,128)}, u32[]{:S(2)}) copy-start(f32[1920,128]{1,0:T(8,128)} %shard_map.73) | copy-start | bytes 2949124
  59.9 20.7 %copy-start.5 = (bf16[256,512]{1,0:T(8,128)(2,1)S(1)}, bf16[256,512]{1,0:T(8,128)(2,1)}, u32[]{:S(2)}) copy-start(bf16[256,512]{1,0:T(8,128)(2,1)} %constant.53.clone.spread_ref) | copy-start | bytes 786436

commit v6 on v5

--- a/solution.py
+++ b/solution.py
@@ -104,10 +104,22 @@
     return jnp.where(meets, 1.0 / 16, 0.0).astype(jnp.bfloat16)
 
 
-def pack_state(back_in, traj_in, send_ref, turned_ref, fine_ref, back_ref, wind_ref, sems):
+def pack_state(
+    back_in, traj_in, innov_in, weight_in, send_ref, near_out, far_out, turned_ref, fine_ref, back_ref, wind_ref, edge_ref, sems
+):
     copies = [pltpu.make_async_copy(traj_in.at[0], wind_ref, sems.at[FIELDS])]
     copies += [pltpu.make_async_copy(back_in.at[f], back_ref.at[f], sems.at[f]) for f in range(FIELDS)]
     for copy in copies:
+        copy.start()
+    odd = lax.axis_index("narrow") % 2
+    edges, leaving = [], []
+    for side, (out_ref, row) in enumerate(((near_out, 14 - 14 * odd), (far_out, 14 * odd))):
+        at = FIELDS + 1 + 3 * side
+        held = edge_ref.at[side]
+        edges.append(pltpu.make_async_copy(innov_in.at[:, pl.ds(row, 2)], held.at[0:FIELDS], sems.at[at]))
+        edges.append(pltpu.make_async_copy(weight_in.at[pl.ds(row, 2)], held.at[FIELDS], sems.at[at + 1]))
+        leaving.append(pltpu.make_async_copy(held, out_ref, sems.at[at + 2]))
+    for copy in edges:
         copy.start()
     spare = jnp.zeros((8, 128), jnp.float32)
     pool = pooling()
@@ -135,7 +147,13 @@
         mean = mean + jnp.dot(low, pool, preferred_element_type=jnp.float32)
         turned_ref[FIELDS * 4 + group, 0:LEVELS, :] = advection_scale * jnp.tanh(mean)
         turned_ref[FIELDS * 4 + group, LEVELS:, :] = spare
+    for copy in edges:
+        copy.wait()
+    for copy in leaving:
+        copy.start()
     scatter_levels(turned_ref, send_ref, FIELDS + 1, 4, STATE_ROWS)
+    for copy in leaving:
+        copy.wait()
 
 
 def pack_departures(place_ref, innov_ref, weight_ref, near_ref, far_ref, send_ref, turned_ref):
@@ -196,66 +214,127 @@
     return total + jnp.dot(high, basis_low, preferred_element_type=jnp.float32)
 
 
-def filtered(even_ref, odd_ref, basis_ref, resp_ref, first, rows, out_ref):
+def filtered(even_ref, odd_ref, basis_ref, resp_ref, bands, out_ref):
+    rows = sum(last - first for first, last in bands)
     count = rows * GROUP
-    band = slice(first, first + rows)
     for ref, which, lanes in ((even_ref, 0, slice(0, HALF)), (odd_ref, 1, slice(HALF, CYCLE))):
+        scale = [resp_ref[first:last, :, lanes] for first, last in bands]
+        scale = scale[0] if len(scale) == 1 else jnp.concatenate(scale, axis=0)
         coefs = product(ref, count, basis_ref, which).reshape(rows, GROUP, HALF)
-        coefs = (coefs * resp_ref[band, :, lanes]).reshape(count, HALF)
-        split_store(ref, slice(0, count), coefs)
+        split_store(ref, slice(0, count), (coefs * scale).reshape(count, HALF))
     even = product(even_ref, count, basis_ref, 2)
     odd = product(odd_ref, count, basis_ref, 3)
-    out_ref[band, :, 0:HALF] = (even + odd).reshape(rows, GROUP, HALF)
-    out_ref[band, :, HALF:CYCLE] = (even - odd).reshape(rows, GROUP, HALF)
-
-
-def expand(source_ref, rows, out_ref):
+    plus, minus = (even + odd).reshape(rows, GROUP, HALF), (even - odd).reshape(rows, GROUP, HALF)
+    start = 0
+    for first, last in bands:
+        size = last - first
+        out_ref[first:last, :, 0:HALF] = plus[start : start + size]
+        out_ref[first:last, :, HALF:CYCLE] = minus[start : start + size]
+        start += size
+
+
+def expand(source_ref, first, last, out_ref):
+    out_ref[first:last, GROUP - 8 :, :] = jnp.zeros((last - first, 8, CYCLE), jnp.float32)
     for field in range(FIELDS):
-        out_ref[0:rows, SHARE * field : SHARE * field + SHARE, :] = source_ref[0:rows, PLANES : PLANES + SHARE, :]
-
-
-def tangent(place_ref, recv_ref, near_ref, far_ref, resp_ref, basis_ref, kept_out, row_ref, state_ref, drift_ref, even_ref, odd_ref, sems):
-    for group in range(6):
-        def load(source):
-            if group == 0:
-                return jnp.where(place_ref[3] == 1, near_ref[source], far_ref[source])
-            if group == 5:
-                return jnp.where(place_ref[3] == 1, far_ref[source], near_ref[source])
-            first = SENT * (group - 1) if group < 4 else STATE_ROWS - GROUP
-            return recv_ref[source, first : first + GROUP, :]
-
-        def store(row, quarter, value):
-            lanes = slice(128 * quarter, 128 * quarter + 128)
-            if group in (0, 4):
-                row_ref[4 * group + row, 0:SENT, lanes] = value[GROUP - SENT :]
-            else:
-                row_ref[4 * group + row, :, lanes] = value
-
-        unpack_rows(load, store)
-    drift_ref[:, GROUP - 8 :, :] = jnp.zeros((BAND, 8, CYCLE), jnp.float32)
-    expand(row_ref, BAND, drift_ref)
-    drift_copy = pltpu.make_async_copy(drift_ref, kept_out.at[BAND : 2 * BAND], sems.at[0])
-    drift_copy.start()
-
-    for step in range(2):
-        first, last = 1 + step, BAND - 1 - step
-        source_ref = row_ref if step == 0 else state_ref
-
-        def body(index, carry):
-            here = source_ref[index]
-            east = pltpu.roll(here, CYCLE - 1, 1)
-            west = pltpu.roll(here, 1, 1)
-            near = source_ref[index - 1] + source_ref[index + 1] + east + west
-            moved = here + diffusion * (near - 4.0 * here) + drift_ref[index] * (east - west)
-            fold_store(even_ref, odd_ref, index - first, moved)
-            return carry
-
-        lax.fori_loop(first, last, body, 0, unroll=4)
-        filtered(even_ref, odd_ref, basis_ref, resp_ref, first, last - first, state_ref)
-    state_copy = pltpu.make_async_copy(state_ref, kept_out.at[0:BAND], sems.at[1])
-    state_copy.start()
-    drift_copy.wait()
-    state_copy.wait()
+        part = slice(SHARE * field, SHARE * field + SHARE)
+        out_ref[first:last, part, :] = source_ref[first:last, PLANES : PLANES + SHARE, :]
+
+
+def moved_rows(source_ref, drift_ref, even_ref, odd_ref, first, last, offset):
+    def body(index, carry):
+        here = source_ref[index]
+        east = pltpu.roll(here, CYCLE - 1, 1)
+        west = pltpu.roll(here, 1, 1)
+        near = source_ref[index - 1] + source_ref[index + 1] + east + west
+        moved = here + diffusion * (near - 4.0 * here) + drift_ref[index] * (east - west)
+        fold_store(even_ref, odd_ref, index - first + offset, moved)
+        return carry
+
+    lax.fori_loop(first, last, body, 0, unroll=4)
+
+
+def unpack_state(load, row_ref, group):
+    def store(row, quarter, value):
+        lanes = slice(128 * quarter, 128 * quarter + 128)
+        if group in (0, 4):
+            row_ref[4 * group + row, 0:SENT, lanes] = value[GROUP - SENT :]
+        else:
+            row_ref[4 * group + row, :, lanes] = value
+
+    unpack_rows(load, store)
+
+
+STATE, DRIFT, RAW, STEPPED = 0, BAND, 2 * BAND, 3 * BAND
+
+
+def tangent(recv_ref, resp_ref, basis_ref, kept_out, row_ref, mid_ref, state_ref, drift_ref, even_ref, odd_ref, sems):
+    copies = []
+
+    def keep(ref, first, last, place):
+        copy = pltpu.make_async_copy(
+            ref.at[first:last], kept_out.at[place + first : place + last], sems.at[len(copies)]
+        )
+        copy.start()
+        copies.append(copy)
+
+    for group in range(1, 5):
+        first = SENT * (group - 1) if group < 4 else STATE_ROWS - GROUP
+        unpack_state(lambda source: recv_ref[source, first : first + GROUP, :], row_ref, group)
+    expand(row_ref, 4, 20, drift_ref)
+    keep(row_ref, 4, 6, RAW)
+    keep(row_ref, 18, 20, RAW)
+    keep(drift_ref, 4, 20, DRIFT)
+    moved_rows(row_ref, drift_ref, even_ref, odd_ref, 5, 19, 0)
+    filtered(even_ref, odd_ref, basis_ref, resp_ref, [(5, 19)], mid_ref)
+    keep(mid_ref, 5, 7, STEPPED)
+    keep(mid_ref, 17, 19, STEPPED)
+    moved_rows(mid_ref, drift_ref, even_ref, odd_ref, 6, 18, 0)
+    filtered(even_ref, odd_ref, basis_ref, resp_ref, [(6, 18)], state_ref)
+    keep(state_ref, 6, 18, STATE)
+    for copy in copies:
+        copy.wait()
+
+
+def tangent_edges(
+    place_ref, near_ref, far_ref, resp_ref, basis_ref, kept_in, kept_out,
+    row_ref, mid_ref, state_ref, drift_ref, even_ref, odd_ref, sems,
+):
+    fetches = []
+    for ref, first, place in ((row_ref, 4, RAW), (row_ref, 18, RAW), (mid_ref, 5, STEPPED), (mid_ref, 17, STEPPED)):
+        fetches.append(
+            pltpu.make_async_copy(
+                kept_in.at[place + first : place + first + 2], ref.at[first : first + 2], sems.at[len(fetches)]
+            )
+        )
+        fetches[-1].start()
+    odd = place_ref[3] == 1
+    unpack_state(lambda source: jnp.where(odd, near_ref[source], far_ref[source]), row_ref, 0)
+    unpack_state(lambda source: jnp.where(odd, far_ref[source], near_ref[source]), row_ref, 5)
+    for copy in fetches:
+        copy.wait()
+    expand(row_ref, 1, 6, drift_ref)
+    expand(row_ref, 18, 23, drift_ref)
+    copies = []
+
+    def keep(ref, first, last, place):
+        copy = pltpu.make_async_copy(
+            ref.at[first:last], kept_out.at[place + first : place + last], sems.at[4 + len(copies)]
+        )
+        copy.start()
+        copies.append(copy)
+
+    keep(drift_ref, 3, 4, DRIFT)
+    keep(drift_ref, 20, 21, DRIFT)
+    moved_rows(row_ref, drift_ref, even_ref, odd_ref, 1, 5, 0)
+    moved_rows(row_ref, drift_ref, even_ref, odd_ref, 19, 23, 4)
+    filtered(even_ref, odd_ref, basis_ref, resp_ref, [(1, 5), (19, 23)], mid_ref)
+    moved_rows(mid_ref, drift_ref, even_ref, odd_ref, 2, 6, 0)
+    moved_rows(mid_ref, drift_ref, even_ref, odd_ref, 18, 22, 4)
+    filtered(even_ref, odd_ref, basis_ref, resp_ref, [(2, 6), (18, 22)], state_ref)
+    keep(state_ref, 2, 6, STATE)
+    keep(state_ref, 18, 22, STATE)
+    for copy in copies:
+        copy.wait()
 
 
 def adjoint(place_ref, recv_ref, kept_in, traj_in, resp_ref, basis_ref, send_ref, held_ref, row_ref, field_ref, weight_ref, state_ref, drift_ref, even_ref, odd_ref, sems):
@@ -293,7 +372,7 @@
     lax.fori_loop(2, 22, depart, 0, unroll=4)
     for step in range(2):
         first, last = 2 + step, BAND - 2 - step
-        filtered(even_ref, odd_ref, basis_ref, resp_ref, first, last - first, field_ref)
+        filtered(even_ref, odd_ref, basis_ref, resp_ref, [(first, last)], field_ref)
 
         def body(index, carry):
             here = field_ref[index]
@@ -409,31 +488,28 @@
     basis = jnp.asarray(BASIS)
     response = response_rows(narrow_index)
 
-    def edge(rows):
-        return jnp.concatenate([innov[:, rows], weight[None, rows]], axis=0)
-
-    first, last = edge(slice(0, 2)), edge(slice(14, 16))
-    edge_near = lax.ppermute(jnp.where(odd, first, last), ("wide", "narrow"), near)
-    edge_far = lax.ppermute(jnp.where(odd, last, first), ("wide", "narrow"), far)
-
     full = pl.BlockSpec(memory_space=pltpu.VMEM)
     away = pl.BlockSpec(memory_space=pltpu.HBM)
     small = pl.BlockSpec(memory_space=pltpu.SMEM)
-    send_state = pl.pallas_call(
+    edge_shape = jax.ShapeDtypeStruct((FIELDS + 1, 2, COLS, LEVELS), f32)
+    send_state, edge_near, edge_far = pl.pallas_call(
         pack_state,
-        in_specs=[away, away],
-        out_specs=full,
-        out_shape=jax.ShapeDtypeStruct((WIDE * STATE_ROWS, 128), f32),
+        in_specs=[away] * 4,
+        out_specs=[full, away, away],
+        out_shape=[jax.ShapeDtypeStruct((WIDE * STATE_ROWS, 128), f32), edge_shape, edge_shape],
         scratch_shapes=[
             pltpu.VMEM((24, 80, 128), f32),
             pltpu.VMEM((LEVELS * PITCH, 128), f32),
             pltpu.VMEM((FIELDS, ROWS, COLS, LEVELS), f32),
             pltpu.VMEM((LEVELS, 64, 128), jnp.bfloat16),
-            pltpu.SemaphoreType.DMA((FIELDS + 1,)),
+            pltpu.VMEM((2, FIELDS + 1, 2, COLS, LEVELS), f32),
+            pltpu.SemaphoreType.DMA((FIELDS + 7,)),
         ],
         compiler_params=params(60),
         cost_estimate=estimate(3),
-    )(back, trajectory)
+    )(back, trajectory, innov, weight)
+    edge_near = lax.ppermute(edge_near, ("wide", "narrow"), near)
+    edge_far = lax.ppermute(edge_far, ("wide", "narrow"), far)
     send_state = send_state.reshape(WIDE, STATE_ROWS, 128)
     held_state = lax.all_to_all(send_state, "wide", split_axis=0, concat_axis=0, tiled=True)
 
@@ -455,15 +531,26 @@
 
     rows_shape = (BAND, GROUP, CYCLE)
     folded = pltpu.VMEM(((BAND - 2) * GROUP, CYCLE), jnp.bfloat16)
+    kept_shape = jax.ShapeDtypeStruct((KEPT, GROUP, CYCLE), f32)
     kept = pl.pallas_call(
         tangent,
-        in_specs=[small] + [full] * 5,
+        in_specs=[full] * 3,
         out_specs=away,
-        out_shape=jax.ShapeDtypeStruct((KEPT, GROUP, CYCLE), f32),
-        scratch_shapes=[pltpu.VMEM(rows_shape, f32)] * 3 + [folded, folded, pltpu.SemaphoreType.DMA((2,))],
+        out_shape=kept_shape,
+        scratch_shapes=[pltpu.VMEM(rows_shape, f32)] * 4 + [folded, folded, pltpu.SemaphoreType.DMA((6,))],
         compiler_params=params(40),
         cost_estimate=estimate(5),
-    )(place, held_state, rows_near, rows_far, response, basis)
+    )(held_state, response, basis)
+    kept = pl.pallas_call(
+        tangent_edges,
+        in_specs=[small] + [full] * 4 + [away],
+        out_specs=away,
+        out_shape=kept_shape,
+        input_output_aliases={5: 0},
+        scratch_shapes=[pltpu.VMEM(rows_shape, f32)] * 4 + [folded, folded, pltpu.SemaphoreType.DMA((8,))],
+        compiler_params=params(40),
+        cost_estimate=estimate(3),
+    )(place, rows_near, rows_far, response, basis, kept)
     send_cost, held = pl.pallas_call(
         adjoint,
         in_specs=[small, full, away, away, full, full],

time: 87 us -> 86.4 us (level)
  waiting for transfers between devices: 16.5 us -> 12.4 us
  Pallas kernels: 28.1 us -> 30.4 us
  local copies, waits for them, and re-layouts: 1.09 us -> 2.37 us
  blocking collectives: 20.7 us -> 19.5 us
  starting transfers between devices: 19.6 us -> 20.7 us
    ppermute x2 -> x1, waiting for transfers between devices: 14.3 us -> 4.02 us  [shards(): lax.ppermute(jnp.where(odd, last, first), ('wide', 'narrow'), far)]
    ppermute x0 -> x2, waiting for transfers between devices: none -> 7.11 us  [the longest x1 5.2 us: shards(): edge_far = lax.ppermute(edge_far, ('wide', 'narrow'), far)]
    ppermute x0 -> x2, starting transfers between devices: none -> 5.33 us  [the longest x1 3.76 us: shards(): edge_far = lax.ppermute(edge_far, ('wide', 'narrow'), far)]
    ppermute x2 -> x1, starting transfers between devices: 8.22 us -> 3.01 us  [shards(): lax.ppermute(jnp.where(odd, last, first), ('wide', 'narrow'), far)]
    pallas_call x2 -> x3, Pallas kernels: 11.9 us -> 14.3 us  [the longest x1 5.4 us: shards(): pl.pallas_call(tangent, in_specs=[full] * 3, out_specs=away, out_shape=ke...]
    all_to_all x1, waiting for transfers between devices: 2.14 us -> 0.01 us  [shards(): lax.all_to_all(send_state, 'wide', split_axis=0, concat_axis=0, tiled=True)]
    all_to_all x1, starting transfers between devices: 4.59 us -> 6.67 us  [shards(): lax.all_to_all(send_depart, 'wide', split_axis=0, concat_axis=0, tiled=True)]
    unnamed x14, local copies, waits for them, and re-layouts: 1.06 us -> 2.37 us
  transfers between devices with their start and end apart: 6 -> 6, of which waited for: 4 -> 5; matrix products, arithmetic and copies ran while one was open for 0% -> 0% of each run, Pallas kernels for 11% -> 13%
where the time goes in v6:
time: 86.4 us; the launch traced here: 86 us
  Pallas kernels  30.4 us (35%)
  starting transfers between devices  20.7 us (24%)
  blocking collectives  19.5 us (23%)
  waiting for transfers between devices  12.4 us (14%)
  local copies, waits for them, and re-layouts  2.37 us (3%)
    all_to_all x1, blocking collectives, shards(): lax.all_to_all(send_cost, 'wide', split_axis=0, concat_axis=0, tiled=True)  19.5 us
    pallas_call x1, Pallas kernels, shards(): pl.pallas_call(adjoint, in_specs=[small, full, away, away, full, full], o...  8.97 us
    all_to_all x1, starting transfers between devices, shards(): lax.all_to_all(send_depart, 'wide', split_axis=0, concat_axis=0, tiled=True)  6.67 us
    pallas_call x1, Pallas kernels, shards(): pl.pallas_call(prolong, in_specs=[small] + [full] * 4, out_specs=away, ou...  5.99 us
    all_to_all x1, starting transfers between devices, shards(): lax.all_to_all(send_state, 'wide', split_axis=0, concat_axis=0, tiled=True)  5.65 us
    pallas_call x1, Pallas kernels, shards(): pl.pallas_call(tangent, in_specs=[full] * 3, out_specs=away, out_shape=ke...  5.4 us
    ppermute x1, waiting for transfers between devices, shards(): edge_far = lax.ppermute(edge_far, ('wide', 'narrow'), far)  5.2 us
    pallas_call x1, Pallas kernels, shards(): pl.pallas_call(tangent_edges, in_specs=[small] + [full] * 4 + [away], out...  4.54 us
  transfers between devices with their start and end apart: 6, of which 5 were waited for; matrix products, arithmetic and copies ran while one was open for 0% of the time, Pallas kernels for 13%

profile of v6, /device:TPU:64, one launch (start us, length us, event | category | flops | bytes accessed | tf_op | source)
XLA Modules:
  0.0 86.0 jit_solution(7235278494061410579)
XLA Ops:
  0.0 0.0 copy-start.4
  0.0 4.3 %shard_map.73 = (f32[1920,128]{1,0:T(8,128)}, f32[6,2,32,72]{3,2,1,0:T(8,128)}, f32[6,2,32,72]{3,2,1,0:T(8,128)}) custom-call(f32[5,16,32,72]{3,2,1,0:T(8,128)} %bitcast.16, bf16[5,72,64,128]{3,2,1,0:T(8,128)(2,1)} %traj_in.3, f32[5,16,32,72]{3,2,1,0:T(8,128)} %bitcast.12, f32[16,32,72]{2,1,0:T(8,128)} %bitcast.14), custom_call_target="tpu_custom_call" | custom-call | flops 3000000000 | bytes 3000000 | tf_op jit(solution)/shard_map/pallas_call | solution.py:495
  4.3 5.6 %all-to-all-start.1 = ((f32[16,120,128]{2,1,0:T(8,128)}), f32[16,120,128]{2,1,0:T(8,128)S(1)}, u32[]{:S(2)}, u32[]{:S(2)}) async-start(f32[16,120,128]{2,1,0:T(8,128)} %bitcast.10), calls=%async_computation.1 | async-start | bytes 1966080 | tf_op jit(solution)/shard_map/all_to_all | solution.py:514
  10.0 1.6 %collective-permute-start = (f32[6,2,32,72]{3,2,1,0:T(8,128)}, f32[6,2,32,72]{3,2,1,0:T(8,128)S(1)}, u32[]{:S(2)}, u32[]{:S(2)}) collective-permute-start(f32[6,2,32,72]{3,2,1,0:T(8,128)} %get-tuple-element.11), channel_id=1, source_target_pairs={{0,1},{1,0},{8,9},{9,8},{16,17},{17,16},{24,25},{25,24},{32,33},{3... | collective-permute-start | bytes 331784 | tf_op jit(solution)/shard_map/ppermute | solution.py:511
  11.6 3.8 %collective-permute-start.1 = (f32[6,2,32,72]{3,2,1,0:T(8,128)}, f32[6,2,32,72]{3,2,1,0:T(8,128)S(1)}, u32[]{:S(2)}, u32[]{:S(2)}) collective-permute-start(f32[6,2,32,72]{3,2,1,0:T(8,128)} %get-tuple-element.12), channel_id=1, source_target_pairs={{1,2},{2,1},{9,10},{10,9},{17,18},{18,17},{25,26},{26,25},{33,34},... | collective-permute-start | bytes 331784 | tf_op jit(solution)/shard_map/ppermute | solution.py:512
  15.4 0.0 copy-start.6
  15.4 0.1 add_convert_fusion.place_ref
  15.5 0.0 copy-start
  15.5 1.9 %collective-permute-done.near_ref = f32[6,2,32,72]{3,2,1,0:T(8,128)S(1)} collective-permute-done((f32[6,2,32,72]{3,2,1,0:T(8,128)}, f32[6,2,32,72]{3,2,1,0:T(8,128)S(1)}, u32[]{:S(2)}, u32[]{:S(2)}) %collective-permute-start) | collective-permute-done | bytes 110624 | tf_op jit(solution)/shard_map/ppermute | solution.py:511
  17.4 5.2 %collective-permute-done.1.far_ref = f32[6,2,32,72]{3,2,1,0:T(8,128)S(1)} collective-permute-done((f32[6,2,32,72]{3,2,1,0:T(8,128)}, f32[6,2,32,72]{3,2,1,0:T(8,128)S(1)}, u32[]{:S(2)}, u32[]{:S(2)}) %collective-permute-start.1) | collective-permute-done | bytes 110624 | tf_op jit(solution)/shard_map/ppermute | solution.py:512
  22.6 0.0 copy-done.4
  22.6 0.0 copy-start.3
  22.6 1.3 %copy-done.3 = f32[5,72,16,32]{1,3,2,0:T(8,128)S(1)} copy-done((f32[5,72,16,32]{1,3,2,0:T(8,128)S(1)}, f32[5,72,16,32]{1,3,2,0:T(8,128)}, u32[]{:S(2)}) %copy-start.3) | copy-done | bytes 737304
  24.0 1.2 %shard_map.74 = f32[2432,128]{1,0:T(8,128)S(1)} custom-call(s32[4]{0:T(128)S(1)} %add_convert_fusion.place_ref, f32[5,16,32,72]{3,2,1,0:T(8,128)S(1)} %bitcast.13, f32[16,32,72]{2,1,0:T(8,128)S(1)} %bitcast.15, f32[6,2,32,72]{3,2,1,0:T(8,128)S(1)} %collective-permute-done.near_ref, f32[6,2,32,72]{3,2,1,0:T(8,128)S(1)} %collective-permute-done.1.far_ref), custom_call_target="tpu_custom_call" | custom-call | flops 3000000000 | bytes 3000000 | tf_op jit(solution)/shard_map/pallas_call | solution.py:516
  25.2 0.0 copy-start.1
  25.2 1.0 %copy-done.1 = f32[2432,128]{1,0:T(8,128)} copy-done((f32[2432,128]{1,0:T(8,128)}, f32[2432,128]{1,0:T(8,128)S(1)}, u32[]{:S(2)}) %copy-start.1) | copy-done | bytes 1245208
  26.2 0.0 all-to-all-done.1.recv_ref
  26.2 6.7 %all-to-all-start = ((f32[16,152,128]{2,1,0:T(8,128)}), f32[16,152,128]{2,1,0:T(8,128)S(1)}, u32[]{:S(2)}, u32[]{:S(2)}) async-start(f32[16,152,128]{2,1,0:T(8,128)} %bitcast.9), calls=%async_computation | async-start | bytes 2490368 | tf_op jit(solution)/shard_map/all_to_all | solution.py:530
  32.9 0.0 copy-done.6
  32.9 0.2 broadcast_select_fusion.resp_ref
  33.0 0.1 slice_select_fusion
  33.1 0.1 collective-permute-start.2
  33.2 3.0 %collective-permute-start.3 = (f32[16,32,128]{2,1,0:T(8,128)S(1)}, f32[16,32,128]{2,1,0:T(8,128)S(1)}, u32[]{:S(2)}, u32[]{:S(2)}) collective-permute-start(f32[16,32,128]{2,1,0:T(8,128)S(1)} %get-tuple-element.15), channel_id=1, source_target_pairs={{1,2},{2,1},{9,10},{10,9},{17,18},{18,17},{25,26},{26,25},{33,34},... | collective-permute-start | bytes 786440 | tf_op jit(solution)/shard_map/ppermute | solution.py:529
  36.2 0.0 copy-done
  36.2 5.4 %shard_map.75.kept_in = f32[448,32,512]{2,1,0:T(8,128)} custom-call(f32[16,120,128]{2,1,0:T(8,128)S(1)} %all-to-all-done.1.recv_ref, f32[24,1,512]{2,1,0:T(1,128)S(1)} %broadcast_select_fusion.resp_ref, bf16[4,512,256]{2,1,0:T(8,128)(2,1)S(1)} %copy-done), custom_call_target="tpu_custom_call" | custom-call | flops 5000000000 | bytes 5000000 | tf_op jit(solution)/shard_map/pallas_call | solution.py:535
  41.6 0.2 collective-permute-done.2.near_ref
  41.8 4.0 %collective-permute-done.3.far_ref = f32[16,32,128]{2,1,0:T(8,128)S(1)} collective-permute-done((f32[16,32,128]{2,1,0:T(8,128)S(1)}, f32[16,32,128]{2,1,0:T(8,128)S(1)}, u32[]{:S(2)}, u32[]{:S(2)}) %collective-permute-start.3) | collective-permute-done | bytes 262176 | tf_op jit(solution)/shard_map/ppermute | solution.py:529
  45.8 4.5 %shard_map.76.kept_in = f32[448,32,512]{2,1,0:T(8,128)} custom-call(s32[4]{0:T(128)S(1)} %add_convert_fusion.place_ref, f32[16,32,128]{2,1,0:T(8,128)S(1)} %collective-permute-done.2.near_ref, f32[16,32,128]{2,1,0:T(8,128)S(1)} %collective-permute-done.3.far_ref, f32[24,1,512]{2,1,0:T(1,128)S(1)} %broadcast_select_fusion.resp_ref, ...), custom_call_target="tpu_custom_call", output_to_operand_aliasing={{}: (5, {})} | custom-call | flops 3000000000 | bytes 3000000 | tf_op jit(solution)/shard_map/pallas_call | solution.py:544
  50.4 1.1 %all-to-all-done.recv_ref = f32[16,152,128]{2,1,0:T(8,128)S(1)} async-done(((f32[16,152,128]{2,1,0:T(8,128)}), f32[16,152,128]{2,1,0:T(8,128)S(1)}, u32[]{:S(2)}, u32[]{:S(2)}) %all-to-all-start) | async-done | bytes 1245216 | tf_op jit(solution)/shard_map/all_to_all | solution.py:530
  51.5 0.0 copy-start.2
  51.5 0.0 copy-start.5
  51.5 9.0 %shard_map.77 = (f32[16,100,128]{2,1,0:T(8,128)S(1)}, bf16[5,72,64,128]{3,2,1,0:T(8,128)(2,1)S(1)}) custom-call(s32[4]{0:T(128)S(1)} %add_convert_fusion.place_ref, f32[16,152,128]{2,1,0:T(8,128)S(1)} %all-to-all-done.recv_ref, f32[448,32,512]{2,1,0:T(8,128)} %shard_map.76.kept_in, bf16[5,72,64,128]{3,2,1,0:T(8,128)(2,1)} %traj_in.3, ...), custom_call_target="tpu_custom_call" | custom-call | flops 5000000000 | bytes 5000000 | tf_op jit(solution)/shard_map/pallas_call | solution.py:554
  60.4 19.5 %all_to_all.15.cost_ref = f32[16,100,128]{2,1,0:T(8,128)S(1)} all-to-all(f32[16,100,128]{2,1,0:T(8,128)S(1)} %get-tuple-element.13), channel_id=1, replica_groups=mesh['wide'=16,'narrow'=8] {'wide'}, dimensions={0} | all-to-all | bytes 1638400 | tf_op jit(solution)/shard_map/all_to_all | solution.py:566
  80.0 0.0 copy-done.2
  80.0 0.0 copy-done.5
  80.0 6.0 %shard_map.78 = bf16[5,72,64,128]{3,2,1,0:T(8,128)(2,1)} custom-call(s32[4]{0:T(128)S(1)} %add_convert_fusion.place_ref, f32[16,120,128]{2,1,0:T(8,128)S(1)} %bitcast.11, f32[16,100,128]{2,1,0:T(8,128)S(1)} %all_to_all.15.cost_ref, bf16[5,72,64,128]{3,2,1,0:T(8,128)(2,1)S(1)} %get-tuple-element.14.traj_ref, bf16[256,512]{1,0:T(8,128)(2,1)S(1)} %copy-done.5), custom_call_target="tpu_custom_call" | custom-call | flops 5000000000 | bytes 5000000 | tf_op jit(solution)/shard_map/pallas_call | solution.py:568
  (2 shorter events, 0.1 us)
Async XLA Ops:
  0.0 22.6 %copy-start.4 = (f32[72,16,32]{0,2,1:T(8,128)S(1)}, f32[72,16,32]{0,2,1:T(8,128)}, u32[]{:S(2)}) copy-start(f32[72,16,32]{0,2,1:T(8,128)} %param.10) | copy-start | bytes 442372
  4.3 21.8 %all-to-all-start.1 = ((f32[16,120,128]{2,1,0:T(8,128)}), f32[16,120,128]{2,1,0:T(8,128)S(1)}, u32[]{:S(2)}, u32[]{:S(2)}) async-start(f32[16,120,128]{2,1,0:T(8,128)} %bitcast.10), calls=%async_computation.1 | async-start | bytes 1966080 | tf_op jit(solution)/shard_map/all_to_all | solution.py:514
  10.0 7.4 %collective-permute-start = (f32[6,2,32,72]{3,2,1,0:T(8,128)}, f32[6,2,32,72]{3,2,1,0:T(8,128)S(1)}, u32[]{:S(2)}, u32[]{:S(2)}) collective-permute-start(f32[6,2,32,72]{3,2,1,0:T(8,128)} %get-tuple-element.11), channel_id=1, source_target_pairs={{0,1},{1,0},{8,9},{9,8},{16,17},{17,16},{24,25},{25,24},{32,33},{3... | collective-permute-start | bytes 331784 | tf_op jit(solution)/shard_map/ppermute | solution.py:511
  11.6 11.1 %collective-permute-start.1 = (f32[6,2,32,72]{3,2,1,0:T(8,128)}, f32[6,2,32,72]{3,2,1,0:T(8,128)S(1)}, u32[]{:S(2)}, u32[]{:S(2)}) collective-permute-start(f32[6,2,32,72]{3,2,1,0:T(8,128)} %get-tuple-element.12), channel_id=1, source_target_pairs={{1,2},{2,1},{9,10},{10,9},{17,18},{18,17},{25,26},{26,25},{33,34},... | collective-permute-start | bytes 331784 | tf_op jit(solution)/shard_map/ppermute | solution.py:512
  15.4 17.4 %copy-start.6 = (f32[512]{0:T(512)S(1)}, f32[512]{0:T(512)}, u32[]{:S(2)}) copy-start(f32[512]{0:T(512)} %constant.52.clone) | copy-start | bytes 6148
  15.5 20.7 %copy-start = (bf16[4,512,256]{2,1,0:T(8,128)(2,1)S(1)}, bf16[4,512,256]{2,1,0:T(8,128)(2,1)}, u32[]{:S(2)}) copy-start(bf16[4,512,256]{2,1,0:T(8,128)(2,1)} %constant.51.clone.basis_ref) | copy-start | bytes 3145732
  22.6 1.3 %copy-start.3 = (f32[5,72,16,32]{1,3,2,0:T(8,128)S(1)}, f32[5,72,16,32]{1,3,2,0:T(8,128)}, u32[]{:S(2)}) copy-start(f32[5,72,16,32]{1,3,2,0:T(8,128)} %param.8) | copy-start | bytes 2211844
  25.2 1.0 %copy-start.1 = (f32[2432,128]{1,0:T(8,128)}, f32[2432,128]{1,0:T(8,128)S(1)}, u32[]{:S(2)}) copy-start(f32[2432,128]{1,0:T(8,128)S(1)} %shard_map.74) | copy-start | bytes 3735556
  26.2 25.3 %all-to-all-start = ((f32[16,152,128]{2,1,0:T(8,128)}), f32[16,152,128]{2,1,0:T(8,128)S(1)}, u32[]{:S(2)}, u32[]{:S(2)}) async-start(f32[16,152,128]{2,1,0:T(8,128)} %bitcast.9), calls=%async_computation | async-start | bytes 2490368 | tf_op jit(solution)/shard_map/all_to_all | solution.py:530
  33.1 8.7 %collective-permute-start.2 = (f32[16,32,128]{2,1,0:T(8,128)S(1)}, f32[16,32,128]{2,1,0:T(8,128)S(1)}, u32[]{:S(2)}, u32[]{:S(2)}) collective-permute-start(f32[16,32,128]{2,1,0:T(8,128)S(1)} %get-tuple-element.16), channel_id=1, source_target_pairs={{0,1},{1,0},{8,9},{9,8},{16,17},{17,16},{24,25},{25,24},{32,33},{3... | collective-permute-start | bytes 786440 | tf_op jit(solution)/shard_map/ppermute | solution.py:528
  33.2 12.6 %collective-permute-start.3 = (f32[16,32,128]{2,1,0:T(8,128)S(1)}, f32[16,32,128]{2,1,0:T(8,128)S(1)}, u32[]{:S(2)}, u32[]{:S(2)}) collective-permute-start(f32[16,32,128]{2,1,0:T(8,128)S(1)} %get-tuple-element.15), channel_id=1, source_target_pairs={{1,2},{2,1},{9,10},{10,9},{17,18},{18,17},{25,26},{26,25},{33,34},... | collective-permute-start | bytes 786440 | tf_op jit(solution)/shard_map/ppermute | solution.py:529
  51.5 28.5 %copy-start.2 = (f32[1920,128]{1,0:T(8,128)S(1)}, f32[1920,128]{1,0:T(8,128)}, u32[]{:S(2)}) copy-start(f32[1920,128]{1,0:T(8,128)} %get-tuple-element.10) | copy-start | bytes 2949124
  51.5 28.5 %copy-start.5 = (bf16[256,512]{1,0:T(8,128)(2,1)S(1)}, bf16[256,512]{1,0:T(8,128)(2,1)}, u32[]{:S(2)}) copy-start(bf16[256,512]{1,0:T(8,128)(2,1)} %constant.53.clone.spread_ref) | copy-start | bytes 786436
